TPU v7x, 32 devices: a whole 2x2x4 slice. The times are simulated.
32 devices in a mesh: seq: 8 (over z, x), ctx: 4 (over y, core).
Axes of the slice: x: 2, y: 2, z: 4, core: 2. Of those that a mesh axis runs over, the one named last changes fastest.
Arguments:
- tokens: bfloat16 [8, 2048, 1088], P('seq', 'ctx'), may hold values from -6 to 6
- segments: int32 [8, 2048], P('seq', 'ctx'), may hold values from 0 to 4, as said below
- cotangent: bfloat16 [8, 2048, 1088], P('seq', 'ctx'), may hold values from -6 to 6
- gain_one: float32 [1088], replicated, may hold values from 0.5 to 1.5
- shift_one: float32 [1088], replicated, may hold values from -3 to 3
- w_qkv: bfloat16 [1088, 3264], P('seq', 'ctx'), may hold values from -0.25 to 0.25
- bias_q: float32 [1088], replicated, may hold values from -3 to 3
- bias_v: float32 [1088], replicated, may hold values from -3 to 3
- w_out: bfloat16 [1088, 1088], P('seq', 'ctx'), may hold values from -1.5 to 1.5
- bias_out: float32 [1088], replicated, may hold values from -3 to 3
- gain_two: float32 [1088], replicated, may hold values from 0.5 to 1.5
- shift_two: float32 [1088], replicated, may hold values from -3 to 3
- w_up: bfloat16 [1088, 4352], P('seq', 'ctx'), may hold values from -0.1875 to 0.1875
- bias_up: float32 [4352], replicated, may hold values from -3 to 3
- w_down: bfloat16 [4352, 1088], P('seq', 'ctx'), may hold values from -0.09375 to 0.09375
- bias_down: float32 [1088], replicated, may hold values from -3 to 3
Outputs:
- output: bfloat16 [8, 2048, 1088], P('seq', 'ctx')
- grad_tokens: float32 [8, 2048, 1088], P('seq', 'ctx')
- grad_gain_one: float32 [1088], replicated
- grad_shift_one: float32 [1088], replicated
- grad_w_qkv: float32 [1088, 3264], P('seq', 'ctx')
- grad_bias_q: float32 [1088], replicated
- grad_bias_v: float32 [1088], replicated
- grad_w_out: float32 [1088, 1088], P('seq', 'ctx')
- grad_bias_out: float32 [1088], replicated
- grad_gain_two: float32 [1088], replicated
- grad_shift_two: float32 [1088], replicated
- grad_w_up: float32 [1088, 4352], P('seq', 'ctx')
- grad_bias_up: float32 [4352], replicated
- grad_w_down: float32 [4352, 1088], P('seq', 'ctx')
- grad_bias_down: float32 [1088], replicated
Inputs may be any that keep to these rules, and one draw needn't show every extreme that they name: `segments`: in each sequence the numbers start at 0, never fall and rise by at most one from a position to the next; each sequence holds exactly five documents. Its third document begins among the first 512 positions and ends among the last 512; the short documents before and after it are pieces that packing cut at the sequence's edges.
All inputs are finite; a program needn't handle non-finite values.
Results may differ from a plain program's by a relative error of at most 0.018.
Values may be sent and summed in bfloat16 or wider, within the bound.
No kernel may reach another device: no remote copies, remote signals or barrier semaphores. Data moves between devices by JAX's collectives and lax.ppermute only.
A program may use at most 192 MiB of HBM per device.

v0:
```python
from functools import partial

import jax
import jax.numpy as jnp
from jax import lax
from jax.sharding import PartitionSpec as P

HEADS = 17
HEAD_DIM = 64


eps = 1e-05
neg_big = -1e30


def layer_norm(values, norm_gain, norm_shift):
    average = jnp.mean(values, axis=-1, keepdims=True)
    centred = values - average
    variance = jnp.mean(centred * centred, axis=-1, keepdims=True)
    return centred * lax.rsqrt(variance + eps) * norm_gain + norm_shift


def gelu_exact(values):
    return jax.nn.gelu(values, approximate=False)


def attention_weights(w_qkv, w_out):
    pieces = (
        lax.all_gather(w_qkv, "ctx", axis=1, tiled=True),
        lax.all_gather(w_out, "ctx", axis=1, tiled=True),
    )
    return (
        lax.all_gather(pieces[0], "seq", axis=0, tiled=True),
        lax.all_gather(pieces[1], "seq", axis=0, tiled=True),
    )


def feedforward_weights(w_up, w_down):
    pieces = (
        lax.all_gather(w_up, "ctx", axis=1, tiled=True),
        lax.all_gather(w_down, "ctx", axis=1, tiled=True),
    )
    return (
        lax.all_gather(pieces[0], "seq", axis=0, tiled=True),
        lax.all_gather(pieces[1], "seq", axis=0, tiled=True),
    )


def gather_keys(key_value_local, segment_local):
    return (
        lax.all_gather(key_value_local, "ctx", axis=0, tiled=True),
        lax.all_gather(segment_local, "ctx", axis=0, tiled=True),
    )


def split_heads(matrix):
    count = matrix.shape[0]
    return matrix.reshape(count, HEADS, HEAD_DIM).transpose(1, 0, 2)


def join_heads(stack):
    return stack.transpose(1, 0, 2).reshape(stack.shape[1], HEADS * HEAD_DIM)


def mask_rows(segment_local, key_segment, row_count):
    query_pos = lax.axis_index("ctx") * row_count + jnp.arange(row_count, dtype=jnp.int32)
    key_pos = jnp.arange(key_segment.shape[0], dtype=jnp.int32)
    return (key_pos[None, :] <= query_pos[:, None]) & (
        key_segment[None, :] == segment_local[:, None]
    )


def head_forward(allowed, members):
    query_head, key_head, value_head = members
    scores = jnp.einsum(
        "qd,kd->qk", query_head, key_head, preferred_element_type=jnp.float32
    ) * HEAD_DIM ** (-0.5)
    scores = jnp.where(allowed, scores, neg_big)
    soft_low = jax.nn.softmax(scores, axis=-1).astype(jnp.bfloat16)
    log_total = jax.nn.logsumexp(scores, axis=-1)
    return (
        jnp.einsum("qk,kd->qd", soft_low, value_head, preferred_element_type=jnp.float32),
        log_total,
    )


def head_backward(allowed, members):
    query_head, key_head, value_head, grad_head = members
    scale = HEAD_DIM ** (-0.5)
    scores = (
        jnp.einsum("qd,kd->qk", query_head, key_head, preferred_element_type=jnp.float32) * scale
    )
    scores = jnp.where(allowed, scores, neg_big)
    soft = jax.nn.softmax(scores, axis=-1)
    soft_low = soft.astype(jnp.bfloat16)
    grad_soft = jnp.einsum("qd,kd->qk", grad_head, value_head, preferred_element_type=jnp.float32)
    row_dot = jnp.sum(soft * grad_soft, axis=-1, keepdims=True)
    grad_scores = (soft * (grad_soft - row_dot)).astype(jnp.bfloat16)
    grad_query = (
        jnp.einsum("qk,kd->qd", grad_scores, key_head, preferred_element_type=jnp.float32) * scale
    )
    grad_key = (
        jnp.einsum("qk,qd->kd", grad_scores, query_head, preferred_element_type=jnp.float32) * scale
    )
    grad_value = jnp.einsum("qk,qd->kd", soft_low, grad_head, preferred_element_type=jnp.float32)
    return (grad_query, grad_key, grad_value)


def body(
    tokens,
    segments,
    cotangent,
    gain_one,
    shift_one,
    w_qkv,
    bias_q,
    bias_v,
    w_out,
    bias_out,
    gain_two,
    shift_two,
    w_up,
    bias_up,
    w_down,
    bias_down,
):
    row_count = tokens.shape[1]
    model_width = tokens.shape[2]
    inputs = tokens[0].astype(jnp.float32)
    segment_local = segments[0]
    upstream = cotangent[0].astype(jnp.float32)
    normed_one, norm_back_one = jax.vjp(layer_norm, inputs, gain_one, shift_one)
    normed_low = normed_one.astype(jnp.bfloat16)
    full_qkv, full_out = attention_weights(w_qkv, w_out)
    projected = jnp.dot(normed_low, full_qkv, preferred_element_type=jnp.float32)
    queries = (projected[:, :model_width] + bias_q).astype(jnp.bfloat16)
    keys_low = projected[:, model_width : 2 * model_width].astype(jnp.bfloat16)
    values_low = (projected[:, 2 * model_width :] + bias_v).astype(jnp.bfloat16)
    key_value_local = jnp.concatenate([keys_low, values_low], axis=1)
    key_value, key_segment = gather_keys(key_value_local, segment_local)
    allowed = mask_rows(segment_local, key_segment, row_count)
    query_heads = split_heads(queries)
    attended_heads, log_totals = lax.map(
        partial(head_forward, allowed),
        (
            query_heads,
            split_heads(key_value[:, :model_width]),
            split_heads(key_value[:, model_width:]),
        ),
    )
    attended = join_heads(attended_heads).astype(jnp.bfloat16)
    middle = inputs + jnp.dot(attended, full_out, preferred_element_type=jnp.float32) + bias_out
    normed_two, norm_back_two = jax.vjp(layer_norm, middle, gain_two, shift_two)
    normed_two_low = normed_two.astype(jnp.bfloat16)
    full_up, full_down = feedforward_weights(w_up, w_down)
    hidden_pre = jnp.dot(normed_two_low, full_up, preferred_element_type=jnp.float32) + bias_up
    activated, gelu_back = jax.vjp(gelu_exact, hidden_pre)
    activated_low = activated.astype(jnp.bfloat16)
    output = (
        middle + jnp.dot(activated_low, full_down, preferred_element_type=jnp.float32) + bias_down
    )
    full_up, full_down = feedforward_weights(w_up, w_down)
    grad_mlp = upstream.astype(jnp.bfloat16)
    grad_bias_down = jnp.sum(grad_mlp.astype(jnp.float32), axis=0)
    part_w_down = jnp.einsum(
        "tf,td->fd", activated_low, grad_mlp, preferred_element_type=jnp.float32
    )
    grad_act = jnp.einsum("td,fd->tf", grad_mlp, full_down, preferred_element_type=jnp.float32)
    grad_pre = gelu_back(grad_act)[0].astype(jnp.bfloat16)
    grad_bias_up = jnp.sum(grad_pre.astype(jnp.float32), axis=0)
    part_w_up = jnp.einsum(
        "tm,tf->mf", normed_two_low, grad_pre, preferred_element_type=jnp.float32
    )
    grad_norm_two = jnp.einsum("tf,mf->tm", grad_pre, full_up, preferred_element_type=jnp.float32)
    grad_middle_part, grad_gain_two, grad_shift_two = norm_back_two(grad_norm_two)
    grad_middle = upstream + grad_middle_part
    rows_mlp = (
        lax.psum_scatter(
            part_w_up.astype(jnp.bfloat16), "seq", scatter_dimension=0, tiled=True
        ).astype(jnp.float32),
        lax.psum_scatter(
            part_w_down.astype(jnp.bfloat16), "seq", scatter_dimension=0, tiled=True
        ).astype(jnp.float32),
    )
    grad_w_up, grad_w_down = (
        lax.psum_scatter(
            rows_mlp[0].astype(jnp.bfloat16), "ctx", scatter_dimension=1, tiled=True
        ).astype(jnp.float32),
        lax.psum_scatter(
            rows_mlp[1].astype(jnp.bfloat16), "ctx", scatter_dimension=1, tiled=True
        ).astype(jnp.float32),
    )
    full_qkv, full_out = attention_weights(w_qkv, w_out)
    key_value, key_segment = gather_keys(key_value_local, segment_local)
    allowed = mask_rows(segment_local, key_segment, row_count)
    grad_branch = grad_middle.astype(jnp.bfloat16)
    grad_bias_out = jnp.sum(grad_branch.astype(jnp.float32), axis=0)
    part_w_out = jnp.einsum("tm,tn->mn", attended, grad_branch, preferred_element_type=jnp.float32)
    grad_attended = jnp.einsum(
        "tn,mn->tm", grad_branch, full_out, preferred_element_type=jnp.float32
    ).astype(jnp.bfloat16)
    grad_query_heads, grad_key_heads, grad_value_heads = lax.map(
        partial(head_backward, allowed),
        (
            query_heads,
            split_heads(key_value[:, :model_width]),
            split_heads(key_value[:, model_width:]),
            split_heads(grad_attended),
        ),
    )
    grad_pairs_part = jnp.concatenate(
        [join_heads(grad_key_heads), join_heads(grad_value_heads)], axis=1
    )
    grad_pairs = lax.psum_scatter(
        grad_pairs_part.astype(jnp.bfloat16), "ctx", scatter_dimension=0, tiled=True
    )
    grad_queries = join_heads(grad_query_heads).astype(jnp.bfloat16)
    grad_proj = jnp.concatenate([grad_queries, grad_pairs], axis=1)
    grad_bias_q = jnp.sum(grad_queries.astype(jnp.float32), axis=0)
    grad_bias_v = jnp.sum(grad_pairs[:, model_width:].astype(jnp.float32), axis=0)
    part_w_qkv = jnp.einsum("tm,tn->mn", normed_low, grad_proj, preferred_element_type=jnp.float32)
    grad_norm_one = jnp.einsum("tn,mn->tm", grad_proj, full_qkv, preferred_element_type=jnp.float32)
    grad_input_part, grad_gain_one, grad_shift_one = norm_back_one(grad_norm_one)
    grad_tokens = grad_middle + grad_input_part
    rows_attention = (
        lax.psum_scatter(
            part_w_qkv.astype(jnp.bfloat16), "seq", scatter_dimension=0, tiled=True
        ).astype(jnp.float32),
        lax.psum_scatter(
            part_w_out.astype(jnp.bfloat16), "seq", scatter_dimension=0, tiled=True
        ).astype(jnp.float32),
    )
    grad_w_qkv, grad_w_out = (
        lax.psum_scatter(
            rows_attention[0].astype(jnp.bfloat16), "ctx", scatter_dimension=1, tiled=True
        ).astype(jnp.float32),
        lax.psum_scatter(
            rows_attention[1].astype(jnp.bfloat16), "ctx", scatter_dimension=1, tiled=True
        ).astype(jnp.float32),
    )
    summed = lax.psum(
        (
            grad_gain_one,
            grad_shift_one,
            grad_bias_q,
            grad_bias_v,
            grad_bias_out,
            grad_gain_two,
            grad_shift_two,
            grad_bias_up,
            grad_bias_down,
        ),
        ("seq", "ctx"),
    )
    return (
        output[None].astype(jnp.bfloat16),
        grad_tokens[None],
        summed[0],
        summed[1],
        grad_w_qkv,
        summed[2],
        summed[3],
        grad_w_out,
        summed[4],
        summed[5],
        summed[6],
        grad_w_up,
        summed[7],
        grad_w_down,
        summed[8],
    )


def solution(mesh):
    return jax.shard_map(
        body,
        mesh=mesh,
        in_specs=(
            P("seq", "ctx", None),
            P("seq", "ctx"),
            P("seq", "ctx", None),
            P(),
            P(),
            P("seq", "ctx"),
            P(),
            P(),
            P("seq", "ctx"),
            P(),
            P(),
            P(),
            P("seq", "ctx"),
            P(),
            P("seq", "ctx"),
            P(),
        ),
        out_specs=(
            P("seq", "ctx", None),
            P("seq", "ctx", None),
            P(),
            P(),
            P("seq", "ctx"),
            P(),
            P(),
            P("seq", "ctx"),
            P(),
            P(),
            P(),
            P("seq", "ctx"),
            P(),
            P("seq", "ctx"),
            P(),
        ),
        check_vma=False,
    )
```

profile of v0, /device:TPU:0, one launch (start us, length us, event | category | flops | bytes accessed | tf_op | source)
XLA Modules:
  0.0 1532.4 jit_solution(12011125924952220269)
XLA Ops:
  7.3 11.4 all-gather.1
  22.9 109.6 %all-gather.12.cloned.1.call-done = bf16[1088,3264]{1,0:T(8,128)(2,1)} async-done(((bf16[136,3264]{1,0:T(8,128)(2,1)}), bf16[1088,3264]{1,0:T(8,128)(2,1)}) %all-gather.12.cloned.1.call-update) | async-done | bytes 7102480 | tf_op jit(solution)/shard_map/all_gather | solution.py:33
  132.5 7.2 fusion.84
  142.0 9.3 all-gather.2
  156.4 5.2 all-gather
  161.6 11.1 all-gather.20.cloned.1.call-done
  178.0 57.3 %all-gather.14.cloned.1.call-done = bf16[2048,2176]{0,1:T(8,128)(2,1)} async-done(((bf16[512,2176]{0,1:T(8,128)(2,1)}), bf16[2048,2176]{0,1:T(8,128)(2,1)}) %all-gather.14.cloned.1.call-update) | async-done | bytes 8912912 | tf_op jit(solution)/shard_map/all_gather | solution.py:51
  235.4 8.9 fusion.93
  244.2 9.1 copy.55
  253.4 9.1 copy.56
  262.6 89.0 %while.26 = (s32[]{:T(128)}, bf16[17,512,64]{1,2,0:T(8,128)(2,1)S(1)}, bf16[17,512,64]{2,1,0:T(8,128)(2,1)}, bf16[17,2048,64]{2,1,0:T(8,128)(2,1)}, bf16[17,2048...) while((s32[]{:T(128)}, ...), condition=%wide.region_5.6_spmd.clone, body=%wide.region_2.5_spmd.clone.sunk | while | flops 279968768 | bytes 13918301 | solution.py:143
  352.7 3.8 fusion.94
  356.8 73.8 %all-gather.18.cloned.1.call-done = bf16[1088,4352]{1,0:T(8,128)(2,1)} async-done(((bf16[136,4352]{1,0:T(8,128)(2,1)}), bf16[1088,4352]{1,0:T(8,128)(2,1)}) %all-gather.18.cloned.1.call-update) | async-done | bytes 9469968 | tf_op jit(solution)/shard_map/all_gather | solution.py:44
  430.7 32.4 %multiply_convert_fusion.1 = (bf16[512,4352]{1,0:T(8,128)(2,1)}, f32[512,4352]{1,0:T(8,128)}, f32[512,4352]{1,0:T(8,128)}) fusion(f32[4352]{0:T(1024)S(1)} %copy-done.32, bf16[1088,4352]{1,0:T(8,128)(2,1)} %all-gather.18.cloned.1.call-done, f32[512,1088]{0,1:T(8,128)S(1)} %get-tuple-element.281, f32[1088]{0:T(1024)S(1)} %copy-done.34, ...), kind=kOutput, calls=%fused_computation.64 | convolution fusion | flops 4998463488 | bytes 34010624 | tf_op jit(solution)/shard_map/dot_general | solution.py:156
  463.1 113.2 %all-gather.22.cloned.1.call-done = bf16[4352,1088]{1,0:T(8,128)(2,1)} async-done(((bf16[544,1088]{1,0:T(8,128)(2,1)}), bf16[4352,1088]{1,0:T(8,128)(2,1)}) %all-gather.22.cloned.1.call-update) | async-done | bytes 9469968 | tf_op jit(solution)/shard_map/all_gather | solution.py:45
  576.3 14.6 convert_reduce_fusion
  590.9 11.4 multiply_reduce_fusion.1
  616.1 226.0 %while.27 = (s32[]{:T(128)}, bf16[17,512,64]{1,2,0:T(8,128)(2,1)S(1)}, bf16[17,2048,64]{1,2,0:T(8,128)(2,1)}, bf16[17,2048,64]{1,2,0:T(8,128)(2,1)}, bf16[17,512...) while((s32[]{:T(128)}, ...), condition=%wide.region_14.15_spmd.clone, body=%wide.region_10.14_spmd.clone.sunk | while | flops 692222464 | bytes 38968436 | solution.py:202
  842.2 9.3 pad_maximum_fusion
  851.6 10.8 convolution_convert_fusion.1
  863.9 12.1 convolution_convert_fusion
  878.2 46.7 %reduce-scatter.20.cloned.1.call-done = bf16[512,2176]{0,1:T(8,128)(2,1)} async-done(((bf16[2048,2176]{0,1:T(8,128)(2,1)}), bf16[512,2176]{0,1:T(8,128)(2,1)}) %reduce-scatter.20.cloned.1.call-update) | async-done | bytes 2228240 | tf_op jit(solution)/shard_map/reduce_scatter | solution.py:214
  925.0 8.4 convolution_convert_fusion.2
  933.5 159.2 %reduce-scatter.24.cloned.1.call-done = bf16[136,4352]{1,0:T(8,128)(2,1)} async-done(((bf16[1088,4352]{1,0:T(8,128)(2,1)}), bf16[136,4352]{1,0:T(8,128)(2,1)}) %reduce-scatter.24.cloned.1.call-update) | async-done | bytes 1183760 | tf_op jit(solution)/shard_map/reduce_scatter | solution.py:178
  1096.3 171.7 %reduce-scatter.26.cloned.1.call-done = bf16[544,1088]{1,0:T(8,128)(2,1)} async-done(((bf16[4352,1088]{1,0:T(8,128)(2,1)}), bf16[544,1088]{1,0:T(8,128)(2,1)}) %reduce-scatter.26.cloned.1.call-update) | async-done | bytes 1183760 | tf_op jit(solution)/shard_map/reduce_scatter | solution.py:181
  1272.2 13.4 fusion.61
  1285.6 6.6 reduce-scatter.30.cloned.1.call-done
  1293.9 133.9 %reduce-scatter.22.cloned.1.call-done = bf16[136,3264]{1,0:T(8,128)(2,1)} async-done(((bf16[1088,3264]{1,0:T(8,128)(2,1)}), bf16[136,3264]{1,0:T(8,128)(2,1)}) %reduce-scatter.22.cloned.1.call-update) | async-done | bytes 887824 | tf_op jit(solution)/shard_map/reduce_scatter | solution.py:226
  1430.4 8.1 fusion.87
  1443.0 42.3 %all-reduce.1 = (f32[1088]{0:T(1024)}, f32[1088]{0:T(1024)}, f32[1088]{0:T(1024)}, f32[1088]{0:T(1024)}, f32[1088]{0:T(1024)}, /*index=5*/f32[1088]{0:T(1024)}, f32[1088]{0:T(1024)}, f32[4352]{0:T(1024)}, f32[1088]{0:T(1024)}) all-reduce(f32[1088]{0:T(1024)S(1)} %get-tuple-element.210, ...), channel_id=1, replica_groups=mesh['seq'=8,'ctx'=4] {'seq','ctx'}, use_global_device_ids=true, to_apply=%region_19.20 | all-reduce | flops 13056 | bytes 104448 | tf_op jit(solution)/shard_map/psum | solution.py:241
  1487.5 4.4 reduce-scatter.34.cloned.1.call-done
  1494.1 29.3 %reduce-scatter.28.cloned.1.call-done = bf16[816,136]{1,0:T(8,128)(2,1)} async-done(((bf16[3264,136]{1,0:T(8,128)(2,1)}), bf16[816,136]{1,0:T(8,128)(2,1)}) %reduce-scatter.28.cloned.1.call-update) | async-done | bytes 221968
  (333 shorter events, 373.0 us)
Async XLA Ops:
  7.2 125.3 %all-gather.12.cloned.1.call-start = ((), (), s32[]{:S(2)}) async-start(), calls=%async_computation.9 | async-start | bytes 8146944 | tf_op jit(solution)/shard_map/all_gather | solution.py:33
  7.2 125.3 %copy-start.15 = (f32[1088]{0:T(1024)S(1)}, f32[1088]{0:T(1024)}, u32[]{:S(2)}) copy-start(f32[1088]{0:T(1024)} %param.23) | copy-start | bytes 13060
  7.2 125.3 %copy-start.35 = (f32[1088]{0:T(1024)S(1)}, f32[1088]{0:T(1024)}, u32[]{:S(2)}) copy-start(f32[1088]{0:T(1024)} %param.24) | copy-start | bytes 13060
  20.7 131.8 %all-gather.24.cloned.1.call-start = ((), (), s32[]{:S(2)}) async-start(), calls=%async_computation.19 | async-start | bytes 1566720 | tf_op jit(solution)/shard_map/all_gather | solution.py:40
  21.5 151.2 %all-gather.20.cloned.1.call-start = ((), (), s32[]{:S(2)}) async-start(), calls=%async_computation.13 | async-start | bytes 1740800 | tf_op jit(solution)/shard_map/all_gather | solution.py:41
  22.2 213.2 %all-gather.14.cloned.1.call-start = ((), (), s32[]{:S(2)}) async-start(), calls=%async_computation.10 | async-start | bytes 11141120 | tf_op jit(solution)/shard_map/all_gather | solution.py:51
  22.5 117.3 %copy-start.17 = (f32[512]{0:T(512)}, f32[512]{0:T(512)S(1)}, u32[]{:S(2)}) copy-start(f32[512]{0:T(512)S(1)} %broadcast_multiply_fusion.1) | copy-start | bytes 6148
  22.8 116.9 %copy-start.20 = (f32[512]{0:T(512)}, f32[512]{0:T(512)S(1)}, u32[]{:S(2)}) copy-start(f32[512]{0:T(512)S(1)} %fusion.67) | copy-start | bytes 6148
  22.9 116.9 %copy-start.22 = (f32[512]{0:T(512)}, f32[512]{0:T(512)S(1)}, u32[]{:S(2)}) copy-start(f32[512]{0:T(512)S(1)} %fusion.79) | copy-start | bytes 6148
  22.9 117.1 %copy-start.26 = (f32[1088]{0:T(1024)S(1)}, f32[1088]{0:T(1024)}, u32[]{:S(2)}) copy-start(f32[1088]{0:T(1024)} %param.27) | copy-start | bytes 13060
  22.9 117.1 %copy-start.27 = (f32[1088]{0:T(1024)S(1)}, f32[1088]{0:T(1024)}, u32[]{:S(2)}) copy-start(f32[1088]{0:T(1024)} %param.26) | copy-start | bytes 13060
  141.9 209.8 %all-gather.16.cloned.1.call-start = ((), (), s32[]{:S(2)}) async-start(), calls=%async_computation.11 | async-start | bytes 2820096 | tf_op jit(solution)/shard_map/all_gather | solution.py:34
  152.5 278.2 %all-gather.18.cloned.1.call-start = ((), (), s32[]{:S(2)}) async-start(), calls=%async_computation.12 | async-start | bytes 10653696 | tf_op jit(solution)/shard_map/all_gather | solution.py:44
  156.3 420.0 %all-gather.22.cloned.1.call-start = ((), (), s32[]{:S(2)}) async-start(), calls=%async_computation.14 | async-start | bytes 11280384 | tf_op jit(solution)/shard_map/all_gather | solution.py:45
  175.2 700.8 %reduce-scatter.36.cloned.1.call-start = ((), (), s32[]{:S(2)}) async-start(), calls=%async_computation.24 | async-start | bytes 2820096
  262.6 90.1 %copy-start.33 = (f32[1088]{0:T(1024)S(1)}, f32[1088]{0:T(1024)}, u32[]{:S(2)}) copy-start(f32[1088]{0:T(1024)} %param.29) | copy-start | bytes 13060
  352.7 78.0 %copy-start.28 = (f32[1088]{0:T(1024)S(1)}, f32[1088]{0:T(1024)}, u32[]{:S(2)}) copy-start(f32[1088]{0:T(1024)} %param.30) | copy-start | bytes 13060
  352.7 78.0 %copy-start.32 = (f32[4352]{0:T(1024)S(1)}, f32[4352]{0:T(1024)}, u32[]{:S(2)}) copy-start(f32[4352]{0:T(1024)} %param.33) | copy-start | bytes 52228
  352.7 78.0 %copy-start.34 = (f32[1088]{0:T(1024)S(1)}, f32[1088]{0:T(1024)}, u32[]{:S(2)}) copy-start(f32[1088]{0:T(1024)} %param.31) | copy-start | bytes 13060
  356.8 219.5 %copy-start.6 = (bf16[1,512,1088]{1,2,0:T(8,128)(2,1)S(1)}, bf16[1,512,1088]{1,2,0:T(8,128)(2,1)}, u32[]{:S(2)}) copy-start(bf16[1,512,1088]{1,2,0:T(8,128)(2,1)} %param.22) | copy-start | bytes 3342340
  609.6 315.4 %reduce-scatter.20.cloned.1.call-start = ((), (), s32[]{:S(2)}) async-start(), calls=%async_computation.15 | async-start | bytes 11141120 | tf_op jit(solution)/shard_map/reduce_scatter | solution.py:214
  851.5 241.1 %reduce-scatter.24.cloned.1.call-start = ((), (), s32[]{:S(2)}) async-start(), calls=%async_computation.17 | async-start | bytes 10653696 | tf_op jit(solution)/shard_map/reduce_scatter | solution.py:178
  862.4 405.7 %reduce-scatter.26.cloned.1.call-start = ((), (), s32[]{:S(2)}) async-start(), calls=%async_computation.18 | async-start | bytes 11280384 | tf_op jit(solution)/shard_map/reduce_scatter | solution.py:181
  875.9 49.0 %copy-start.18 = (f32[512]{0:T(512)S(1)}, f32[512]{0:T(512)}, u32[]{:S(2)}) copy-start(f32[512]{0:T(512)} %copy-done.17) | copy-start | bytes 6148
  875.9 49.0 %copy-start.23 = (f32[512]{0:T(512)S(1)}, f32[512]{0:T(512)}, u32[]{:S(2)}) copy-start(f32[512]{0:T(512)} %copy-done.22) | copy-start | bytes 6148
  876.0 416.2 %reduce-scatter.30.cloned.1.call-start = ((), (), s32[]{:S(2)}) async-start(), calls=%async_computation.21 | async-start | bytes 696320
  878.2 549.6 %reduce-scatter.22.cloned.1.call-start = ((), (), s32[]{:S(2)}) async-start(), calls=%async_computation.16 | async-start | bytes 8146944 | tf_op jit(solution)/shard_map/reduce_scatter | solution.py:226
  933.4 551.9 %reduce-scatter.32.cloned.1.call-start = ((), (), s32[]{:S(2)}) async-start(), calls=%async_computation.22 | async-start | bytes 2785280
  1096.3 176.0 %copy-start.37 = (f32[1088]{0:T(1024)S(1)}, f32[1088]{0:T(1024)}, u32[]{:S(2)}) copy-start(f32[1088]{0:T(1024)} %param.35) | copy-start | bytes 13060
  1096.3 395.6 %reduce-scatter.34.cloned.1.call-start = ((), (), s32[]{:S(2)}) async-start(), calls=%async_computation.23 | async-start | bytes 1740800
  1270.6 252.8 %reduce-scatter.28.cloned.1.call-start = ((), (), s32[]{:S(2)}) async-start(), calls=%async_computation.20 | async-start | bytes 2088960
  1285.6 144.8 %copy-start.5 = (bf16[17,512,64]{1,2,0:T(8,128)(2,1)S(1)}, bf16[17,512,64]{1,2,0:T(8,128)(2,1)}, u32[]{:S(2)}) copy-start(bf16[17,512,64]{1,2,0:T(8,128)(2,1)} %copy-done.4) | copy-start | bytes 3342340
  (23 other events, 242.5 us)
Sparse Core Ops, SparseCore 0:
  20.8 111.6 all-gather.11
  134.1 18.2 all-gather.23
  154.0 18.6 all-gather.19
  174.1 61.2 all-gather.13
  238.0 53.5 all-gather.15
  293.6 137.0 all-gather.17
  432.8 143.4 all-gather.21
  609.7 68.1 reduce-scatter.35
  851.7 73.2 reduce-scatter.19
  928.3 164.3 reduce-scatter.23
  1096.7 171.2 reduce-scatter.25
  1271.1 20.9 reduce-scatter.29
  1296.2 131.5 reduce-scatter.21
  1430.4 32.0 reduce-scatter.31
  1464.9 26.9 reduce-scatter.33
  1494.5 28.8 reduce-scatter.27
where the time goes:
time: 1540 us; the launch traced here: 1530 us
  waiting for transfers between devices  919 us (60%)
  matrix products  396 us (26%)
  other arithmetic  68.7 us (4%)
  blocking collectives  68.2 us (4%)
  local copies, waits for them, and re-layouts  64.5 us (4%)
    reduce_scatter x1, waiting for transfers between devices, body(): lax.psum_scatter(part_w_down.astype(jnp.bfloat16), 'seq', scatter_dimensi...  172 us
    reduce_scatter x1, waiting for transfers between devices, body(): lax.psum_scatter(part_w_up.astype(jnp.bfloat16), 'seq', scatter_dimension...  159 us
    reduce_scatter x1, waiting for transfers between devices, body(): lax.psum_scatter(part_w_qkv.astype(jnp.bfloat16), 'seq', scatter_dimensio...  134 us
    all_gather x1, waiting for transfers between devices, feedforward_weights(): lax.all_gather(pieces[1], 'seq', axis=0, tiled=True)  113 us
    all_gather x1, waiting for transfers between devices, attention_weights(): lax.all_gather(pieces[0], 'seq', axis=0, tiled=True)  110 us
    all_gather x1, waiting for transfers between devices, feedforward_weights(): lax.all_gather(pieces[0], 'seq', axis=0, tiled=True)  73.8 us
    all_gather x1, waiting for transfers between devices, gather_keys(): lax.all_gather(key_value_local, 'ctx', axis=0, tiled=True)  57.3 us
    reduce_scatter x1, waiting for transfers between devices, body(): lax.psum_scatter(grad_pairs_part.astype(jnp.bfloat16), 'ctx', scatter_dim...  46.7 us
  transfers between devices with their start and end apart: 16, of which 12 were waited for; matrix products, arithmetic and copies ran while one was open for 32% of the time, Pallas kernels for 0%

commit v1 on v0

v1 whole, which is shorter than its diff:
```python
import functools

import jax
import jax.numpy as jnp
from jax import lax
from jax.experimental import pallas as pl
from jax.experimental.pallas import tpu as pltpu
from jax.sharding import PartitionSpec as P

HEADS = 17
HEAD_DIM = 64

eps = 1e-05
neg_big = -1e30
f32 = jnp.float32
bf16 = jnp.bfloat16

NN = (((1,), (0,)), ((), ()))
NT = (((1,), (1,)), ((), ()))
TN = (((0,), (0,)), ((), ()))


def mm(left, right, dims=NN):
    return lax.dot_general(left, right, dims, preferred_element_type=f32)


def layer_norm(values, norm_gain, norm_shift):
    average = jnp.mean(values, axis=-1, keepdims=True)
    centred = values - average
    variance = jnp.mean(centred * centred, axis=-1, keepdims=True)
    return centred * lax.rsqrt(variance + eps) * norm_gain + norm_shift


def after(value, *earlier):
    return lax.optimization_barrier((value, *earlier))[0]


def allowed_tile(start, i, j, block):
    key_pos = j * block + lax.broadcasted_iota(jnp.int32, (block, block), 0)
    allowed = key_pos >= start
    if i == j:
        query_pos = i * block + lax.broadcasted_iota(jnp.int32, (block, block), 1)
        allowed = allowed & (key_pos <= query_pos)
    return allowed


def attend_kernel(block, blocks, own_ref, start_ref, qkv_ref, out_ref, log_ref):
    slots = [own_ref[0] ^ i for i in range(blocks)]
    cols = [pl.ds(pl.multiple_of(slot * block, block), block) for slot in slots]
    scale = jnp.asarray(HEAD_DIM ** (-0.5), bf16)
    for i in range(blocks):
        query = qkv_ref[0, :, cols[i]] * scale
        start = start_ref[:, cols[i]]
        scores = []
        for j in range(i + 1):
            score = mm(qkv_ref[1, :, cols[j]], query, TN)
            scores.append(jnp.where(allowed_tile(start, i, j, block), score, neg_big))
        top = functools.reduce(
            jnp.maximum, [jnp.max(score, axis=0, keepdims=True) for score in scores]
        )
        total, sums = jnp.zeros_like(top), None
        for j in range(i + 1):
            power = jnp.exp(scores[j] - top)
            total = total + jnp.sum(power, axis=0, keepdims=True)
            part = mm(qkv_ref[2, :, cols[j]], power.astype(bf16))
            sums = part if sums is None else sums + part
        out_ref[slots[i]] = (sums / total).astype(bf16)
        log_ref[0, :, cols[i]] = top + jnp.log(total)


def attend_back_kernel(
    block, blocks, own_ref, start_ref, qkv_ref, out_ref, grad_ref, log_ref, *rest
):
    back_ref, query_sum = rest[-2:]
    slots = [own_ref[0] ^ i for i in range(blocks)]
    cols = [pl.ds(pl.multiple_of(slot * block, block), block) for slot in slots]
    scale = jnp.asarray(HEAD_DIM ** (-0.5), bf16)
    dots = [
        jnp.sum(out_ref[slot].astype(f32) * grad_ref[slot].astype(f32), axis=0, keepdims=True)
        for slot in slots
    ]
    for j in range(blocks):
        key = qkv_ref[1, :, cols[j]]
        value = qkv_ref[2, :, cols[j]]
        key_sum = value_sum = None
        for i in range(j, blocks):
            query = qkv_ref[0, :, cols[i]] * scale
            grad = grad_ref[slots[i]]
            score = mm(key, query, TN)
            allowed = allowed_tile(start_ref[:, cols[i]], i, j, block)
            soft = jnp.where(allowed, jnp.exp(score - log_ref[0, :, cols[i]]), 0.0)
            back = (soft * (mm(value, grad, TN) - dots[i])).astype(bf16)
            value_part = mm(grad, soft.astype(bf16), NT)
            key_part = mm(query, back, NT)
            value_sum = value_part if value_sum is None else value_sum + value_part
            key_sum = key_part if key_sum is None else key_sum + key_part
            if j == 0:
                query_sum[i] = mm(key, back)
            else:
                query_sum[i] += mm(key, back)
        back_ref[1, :, cols[j]] = key_sum.astype(bf16)
        back_ref[2, :, cols[j]] = value_sum.astype(bf16)
    for i in range(blocks):
        back_ref[0, :, cols[i]] = (query_sum[i] * HEAD_DIM ** (-0.5)).astype(bf16)


def attend(own, start, qkv, block, first, count):
    _, width, length = qkv.shape
    blocks = length // block
    pairs = count * block * block * blocks * (blocks + 1) // 2
    return pl.pallas_call(
        functools.partial(attend_kernel, block, blocks),
        grid_spec=pltpu.PrefetchScalarGridSpec(
            num_scalar_prefetch=1,
            grid=(count,),
            in_specs=[
                pl.BlockSpec((1, length), lambda h, own: (0, 0)),
                pl.BlockSpec((3, HEAD_DIM, length), lambda h, own: (0, first + h, 0)),
            ],
            out_specs=[
                pl.BlockSpec((blocks, HEAD_DIM, block), lambda h, own: (0, h, 0)),
                pl.BlockSpec((1, 1, length), lambda h, own: (h, 0, 0)),
            ],
        ),
        out_shape=[
            jax.ShapeDtypeStruct((blocks, count * HEAD_DIM, block), bf16),
            jax.ShapeDtypeStruct((count, 1, length), f32),
        ],
        compiler_params=pltpu.CompilerParams(vmem_limit_bytes=40 * 2**20),
        cost_estimate=pl.CostEstimate(
            flops=pairs * 4 * 256 * 2,
            bytes_accessed=count * HEAD_DIM * length * 8,
            transcendentals=pairs,
        ),
        name="attend",
    )(own, start, qkv)


def attend_back(own, start, qkv, out, grad, log, block, first, count, held):
    _, width, length = qkv.shape
    blocks = length // block
    pairs = count * block * block * blocks * (blocks + 1) // 2
    tile = pl.BlockSpec((3, HEAD_DIM, length), lambda h, own: (0, first + h, 0))
    side = pl.BlockSpec((blocks, HEAD_DIM, block), lambda h, own: (0, h, 0))
    in_specs = [
        pl.BlockSpec((1, length), lambda h, own: (0, 0)),
        tile,
        side,
        side,
        pl.BlockSpec((1, 1, length), lambda h, own: (h, 0, 0)),
    ]
    operands = (own, start, qkv, out, grad, log)
    aliases = {}
    if held is not None:
        in_specs.append(pl.BlockSpec(memory_space=pl.ANY))
        operands = (*operands, held)
        aliases = {len(operands) - 1: 0}
    return pl.pallas_call(
        functools.partial(attend_back_kernel, block, blocks),
        grid_spec=pltpu.PrefetchScalarGridSpec(
            num_scalar_prefetch=1,
            grid=(count,),
            in_specs=in_specs,
            out_specs=tile,
            scratch_shapes=[pltpu.VMEM((blocks, HEAD_DIM, block), f32)],
        ),
        out_shape=jax.ShapeDtypeStruct(qkv.shape, bf16),
        input_output_aliases=aliases,
        compiler_params=pltpu.CompilerParams(vmem_limit_bytes=40 * 2**20),
        cost_estimate=pl.CostEstimate(
            flops=pairs * 8 * 256 * 2,
            bytes_accessed=count * HEAD_DIM * length * 18,
            transcendentals=pairs,
        ),
        name="attend_back",
    )(*operands)


def solution(mesh):
    n_seq, n_ctx = mesh.shape["seq"], mesh.shape["ctx"]
    per_device = -(-HEADS // n_ctx)
    share = per_device * HEAD_DIM
    padded = share * n_ctx
    cycle = list(range(0, n_seq, 2)) + list(range(1, n_seq, 2))[::-1]
    place = [cycle.index(s) for s in range(n_seq)]
    ring_right = [(cycle[p], cycle[(p + 1) % n_seq]) for p in range(n_seq)]
    ring_left = [(cycle[p], cycle[(p - 1) % n_seq]) for p in range(n_seq)]
    steps_right, steps_left = n_seq // 2, (n_seq - 1) // 2
    groups = [(g, min(2, per_device - g)) for g in range(0, per_device, 2)]

    def swap(value, distance):
        return lax.ppermute(value, "ctx", [(c, c ^ distance) for c in range(n_ctx)])

    def ctx_gather(value):
        blocks = [value]
        for r in range(1, n_ctx):
            blocks.append(swap(blocks[r - 1], 1) if r % 2 else swap(value, r))
        return blocks

    def ctx_exchange(blocks):
        return [blocks[0]] + [swap(blocks[r], r) for r in range(1, n_ctx)]

    def ctx_reduce(parts):
        sums = [
            parts[r].astype(f32) + swap(parts[r + 1], 1).astype(f32) for r in range(0, n_ctx, 2)
        ]
        total = sums[0]
        for r in range(2, n_ctx, 2):
            total = total + swap(sums[r // 2].astype(bf16), r).astype(f32)
        return total

    def in_order(blocks, own, axis):
        size = blocks[0].shape[axis]
        shape = list(blocks[0].shape)
        shape[axis] = size * n_ctx
        whole = jnp.zeros(shape, blocks[0].dtype)
        for r, piece in enumerate(blocks):
            whole = lax.dynamic_update_slice_in_dim(whole, piece, (own ^ r) * size, axis)
        return whole

    def body(
        tokens,
        segments,
        cotangent,
        gain_one,
        shift_one,
        w_qkv,
        bias_q,
        bias_v,
        w_out,
        bias_out,
        gain_two,
        shift_two,
        w_up,
        bias_up,
        w_down,
        bias_down,
    ):
        rows, width = tokens.shape[1:]
        hidden = w_up.shape[1] * n_ctx
        own = lax.axis_index("ctx")
        spot = jnp.asarray(place, jnp.int32)[lax.axis_index("seq")]
        at = jnp.asarray(cycle * 3, jnp.int32)

        def seq_gather(value):
            size = value.shape[0]
            whole = jnp.zeros((size * n_seq, *value.shape[1:]), value.dtype)

            def put(whole, piece, step):
                row = at[spot + n_seq + step] * size
                return lax.dynamic_update_slice_in_dim(whole, piece, row, 0)

            whole = put(whole, value, 0)
            right = left = value
            for step in range(1, steps_right + 1):
                right = lax.ppermute(right, "seq", ring_right)
                whole = put(whole, right, -step)
                if step <= steps_left:
                    left = lax.ppermute(left, "seq", ring_left)
                    whole = put(whole, left, step)
            return whole, right

        def seq_reduce(part):
            size = part.shape[0] // n_seq

            def take(step):
                row = at[spot + n_seq + step] * size
                return lax.dynamic_slice_in_dim(part, row, size, 0)

            right, left = take(steps_right), take(-steps_left)
            for step in range(steps_right - 1, -1, -1):
                right = lax.ppermute(right, "seq", ring_right).astype(f32)
                if step:
                    right = (right + take(step).astype(f32)).astype(bf16)
            for step in range(steps_left - 1, -1, -1):
                left = lax.ppermute(left, "seq", ring_left).astype(f32)
                if step:
                    left = (left + take(-step).astype(f32)).astype(bf16)
            return right + left + take(0).astype(f32)

        def all_sum(value):
            for r in [1 << b for b in range(n_ctx.bit_length() - 1)]:
                value = value + swap(value, r)
            for r in [1 << b for b in range(n_seq.bit_length() - 1)]:
                value = value + lax.ppermute(value, "seq", [(s, s ^ r) for s in range(n_seq)])
            return value

        own_array = jnp.reshape(own, (1,)).astype(jnp.int32)
        inputs = tokens[0].astype(f32)
        upstream_low = cotangent[0]
        upstream = upstream_low.astype(f32)

        w_qkv_rows = in_order(ctx_gather(w_qkv), own, 1).reshape(-1, 3, width)
        w_qkv_rows = jnp.pad(w_qkv_rows, ((0, 0), (0, 0), (0, padded - width)))
        w_qkv_rows = lax.dynamic_slice_in_dim(w_qkv_rows, own * share, share, 2)
        w_qkv_own, last = seq_gather(w_qkv_rows.reshape(-1, 3 * share))

        normed_one, norm_back_one = jax.vjp(layer_norm, inputs, gain_one, shift_one)
        normed_one_blocks = ctx_gather(normed_one.astype(bf16))
        normed_one_all = jnp.concatenate(normed_one_blocks)
        segment_all = jnp.concatenate(ctx_gather(segments[0]))
        start = jnp.zeros_like(segment_all)
        for number in range(1, 5):
            count = jnp.sum((segment_all < number).astype(jnp.int32))
            start = jnp.where(segment_all == number, count, start)
        start = start[None]

        w_out_rows = after(in_order(ctx_gather(w_out), own, 1), last)
        w_out_all, last = seq_gather(w_out_rows)
        w_up_own, last = seq_gather(after(w_up, last))
        piece = w_down.shape[0] // n_ctx
        w_down_pieces = w_down.reshape(n_ctx, piece, -1)
        w_down_rows = in_order(
            ctx_exchange(
                [lax.dynamic_index_in_dim(w_down_pieces, own ^ r, 0, False) for r in range(n_ctx)]
            ),
            own,
            1,
        )
        spread = [(b, (b % n_seq) * n_ctx + b // n_seq) for b in range(n_seq * n_ctx)]
        w_down_rows = lax.ppermute(w_down_rows, ("seq", "ctx"), spread)
        w_down_own, last = seq_gather(after(w_down_rows, last))
        upstream_all = jnp.concatenate(ctx_gather(after(upstream_low, normed_one_blocks[-1])))

        bias_qkv = jnp.concatenate(
            [
                lax.dynamic_slice_in_dim(jnp.pad(bias, (0, padded - width)), own * share, share)
                for bias in (bias_q, jnp.zeros_like(bias_q), bias_v)
            ]
        )
        qkv = (mm(w_qkv_own, normed_one_all, (((0,), (1,)), ((), ()))) + bias_qkv[:, None]).astype(
            bf16
        )
        qkv = qkv.reshape(3, share, -1)
        outs, logs, arrived = [], [], []
        for first, count in groups:
            out, log = attend(own_array, start, qkv, rows, first, count)
            outs.append(out)
            logs.append(log)
            arrived.append(ctx_exchange([out[r] for r in range(n_ctx)]))
        attended = in_order(
            [jnp.concatenate([part[r] for part in arrived]) for r in range(n_ctx)], own, 0
        )[:width]
        middle = inputs + mm(attended, w_out_all, TN) + bias_out

        normed_two, norm_back_two = jax.vjp(layer_norm, middle, gain_two, shift_two)
        normed_two_all = jnp.concatenate(ctx_gather(normed_two.astype(bf16)))
        bias_up_own = lax.dynamic_slice_in_dim(bias_up, own * w_up.shape[1], w_up.shape[1])
        hidden_pre = mm(normed_two_all, w_up_own) + bias_up_own
        cumulative = 0.5 * (1.0 + lax.erf(hidden_pre * 0.5**0.5))
        activated = (hidden_pre * cumulative).astype(bf16)
        slope = cumulative + hidden_pre * jnp.exp(-0.5 * hidden_pre * hidden_pre) * (
            0.5 / jnp.pi
        ) ** 0.5
        slope = slope.astype(bf16)

        grad_pre = (mm(upstream_all, w_down_own, NT) * slope.astype(f32)).astype(bf16)
        grad_norm_two = ctx_reduce(
            jnp.split(mm(grad_pre, w_up_own, NT).astype(bf16), n_ctx)
        )
        grad_middle_part, grad_gain_two, grad_shift_two = norm_back_two(grad_norm_two)
        grad_middle = upstream + grad_middle_part
        part_w_down = mm(activated, upstream_all, TN).astype(bf16)
        part_w_up = mm(normed_two_all, grad_pre, TN).astype(bf16)
        grad_w_down_rows = seq_reduce(part_w_down)
        grad_w_up = seq_reduce(part_w_up)

        grad_branch = grad_middle.astype(bf16)
        grad_attended = mm(w_out_all, grad_branch, NT).astype(bf16)
        grad_attended = jnp.pad(grad_attended, ((0, padded - width), (0, 0)))
        grad_attended = grad_attended.reshape(n_ctx, share, -1)
        grad_attended = [
            lax.dynamic_index_in_dim(grad_attended, own ^ r, 0, False) for r in range(n_ctx)
        ]
        back = None
        for (first, count), out, log in zip(groups, outs, logs):
            span = slice(first * HEAD_DIM, (first + count) * HEAD_DIM)
            grad_own = jnp.stack(ctx_exchange([part[span] for part in grad_attended]))
            back = attend_back(
                own_array, start, qkv, out, grad_own, log, rows, first, count, back
            )
        part_w_out = mm(attended, grad_branch).astype(bf16)
        grad_w_out_rows = seq_reduce(part_w_out)

        mlp_out = ctx_reduce(jnp.split(mm(activated, w_down_own).astype(bf16), n_ctx))
        output = middle + mlp_out + bias_down

        grad_proj = back.reshape(3 * share, -1)
        grad_norm_one = ctx_reduce(
            jnp.split(mm(grad_proj, w_qkv_own, (((0,), (1,)), ((), ()))).astype(bf16), n_ctx)
        )
        grad_input_part, grad_gain_one, grad_shift_one = norm_back_one(grad_norm_one)
        grad_tokens = grad_middle + grad_input_part
        part_w_qkv = mm(normed_one_all, grad_proj, (((0,), (1,)), ((), ()))).astype(bf16)
        grad_w_qkv_rows = seq_reduce(part_w_qkv).astype(bf16)
        grad_w_qkv = in_order(
            ctx_gather(grad_w_qkv_rows.reshape(-1, 3, share)), own, 2
        )[:, :, :width].reshape(-1, 3 * width)
        grad_w_qkv = lax.dynamic_slice_in_dim(
            grad_w_qkv, own * w_qkv.shape[1], w_qkv.shape[1], 1
        ).astype(f32)

        column = w_out.shape[1]
        grad_w_out_blocks = [
            lax.dynamic_slice_in_dim(grad_w_out_rows.astype(bf16), (own ^ r) * column, column, 1)
            for r in range(n_ctx)
        ]
        grad_w_out = ctx_reduce(grad_w_out_blocks)
        gathered = [(b, a) for a, b in spread]
        grad_w_down_rows = lax.ppermute(grad_w_down_rows.astype(bf16), ("seq", "ctx"), gathered)
        column = w_down.shape[1]
        grad_w_down = in_order(
            ctx_exchange(
                [
                    lax.dynamic_slice_in_dim(grad_w_down_rows, (own ^ r) * column, column, 1)
                    for r in range(n_ctx)
                ]
            ),
            own,
            0,
        ).astype(f32)

        grad_bias_up_own = jnp.sum(grad_pre.astype(f32), axis=0)
        early = all_sum(
            jnp.concatenate(
                [
                    jnp.sum(upstream, axis=0),
                    grad_gain_two,
                    grad_shift_two,
                    jnp.sum(grad_branch.astype(f32), axis=0),
                    lax.dynamic_update_slice_in_dim(
                        jnp.zeros((hidden,), f32), grad_bias_up_own, own * w_up.shape[1], 0
                    ),
                ]
            )
        )
        grad_bias_down, grad_gain_two, grad_shift_two, grad_bias_out = (
            early[g * width : (g + 1) * width] for g in range(4)
        )
        grad_bias_up = early[4 * width :]
        grad_bias_qkv = jnp.sum(back.astype(f32), axis=2)
        late = all_sum(
            jnp.concatenate(
                [grad_gain_one, grad_shift_one]
                + [
                    lax.dynamic_update_slice_in_dim(
                        jnp.zeros((padded,), f32), grad_bias_qkv[g], own * share, 0
                    )[:width]
                    for g in (0, 2)
                ]
            )
        )
        grad_gain_one, grad_shift_one, grad_bias_q, grad_bias_v = (
            late[g * width : (g + 1) * width] for g in range(4)
        )
        return (
            output[None].astype(bf16),
            grad_tokens[None],
            grad_gain_one,
            grad_shift_one,
            grad_w_qkv,
            grad_bias_q,
            grad_bias_v,
            grad_w_out,
            grad_bias_out,
            grad_gain_two,
            grad_shift_two,
            grad_w_up,
            grad_bias_up,
            grad_w_down,
            grad_bias_down,
        )

    block = P("seq", "ctx", None)
    split = P("seq", "ctx")
    return jax.shard_map(
        body,
        mesh=mesh,
        in_specs=(
            block,
            split,
            block,
            P(),
            P(),
            split,
            P(),
            P(),
            split,
            P(),
            P(),
            P(),
            split,
            P(),
            split,
            P(),
        ),
        out_specs=(
            block,
            block,
            P(),
            P(),
            split,
            P(),
            P(),
            split,
            P(),
            P(),
            P(),
            split,
            P(),
            split,
            P(),
        ),
        check_vma=False,
    )
```

time: 1540 us -> 760 us (0.49)
  waiting for transfers between devices: 919 us -> 246 us
  matrix products: 396 us -> 82 us
  starting transfers between devices: 0.87 us -> 136 us
  local copies, waits for them, and re-layouts: 64.5 us -> 146 us
  blocking collectives: 68.2 us -> 0 us
  Pallas kernels: 0 us -> 60 us
    reduce_scatter x4 -> x0, waiting for transfers between devices: 512 us -> none  [the longest x1 172 us: body(): lax.psum_scatter(part_w_down.astype(jnp.bfloat16), 'seq', scatter_dimensi...]
    all_gather x7 -> x0, waiting for transfers between devices: 365 us -> none  [the longest x1 113 us: feedforward_weights(): lax.all_gather(pieces[1], 'seq', axis=0, tiled=True)]
    dot_general x131 -> x12, matrix products: 396 us -> 82 us  [mm(): return lax.dot_general(left, right, dims, preferred_element_type=f32)]
    ppermute x0 -> x125, waiting for transfers between devices: none -> 246 us  [the longest x61 85.5 us: swap(): return lax.ppermute(value, 'ctx', [(c, c ^ distance) for c in range(n_ctx)])]
    ppermute x0 -> x125, starting transfers between devices: none -> 136 us  [the longest x61 59.2 us: swap(): return lax.ppermute(value, 'ctx', [(c, c ^ distance) for c in range(n_ctx)])]
    dynamic_update_slice x0 -> x55, local copies, waits for them, and re-layouts: none -> 110 us  [the longest x20 108 us: in_order(): lax.dynamic_update_slice_in_dim(whole, piece, (own ^ r) * size, axis)]
    pallas_call x0 -> x6, Pallas kernels: none -> 60 us  [the longest x3 37.9 us: attend_back(): pl.pallas_call(functools.partial(attend_back_kernel, block, blocks), grid...]
    psum x1 -> x0, blocking collectives: 42.3 us -> none  [body(): lax.psum((grad_gain_one, grad_shift_one, grad_bias_q, grad_bias_v, grad_b...]
  transfers between devices with their start and end apart: 16 -> 125, of which waited for: 12 -> 45; matrix products, arithmetic and copies ran while one was open for 32% -> 35% of each run, Pallas kernels for 0% -> 5%
where the time goes in v1:
time: 760 us; the launch traced here: 748 us
  waiting for transfers between devices  246 us (32%)
  local copies, waits for them, and re-layouts  146 us (19%)
  starting transfers between devices  136 us (18%)
  matrix products  82 us (11%)
  Pallas kernels  60 us (8%)
  other arithmetic  57.7 us (8%)
  between operations  20.4 us (3%)
    dynamic_update_slice x20, local copies, waits for them, and re-layouts, in_order(): lax.dynamic_update_slice_in_dim(whole, piece, (own ^ r) * size, axis)  108 us
    ppermute x61, waiting for transfers between devices, swap(): return lax.ppermute(value, 'ctx', [(c, c ^ distance) for c in range(n_ctx)])  85.5 us
    dot_general x12, matrix products, mm(): return lax.dot_general(left, right, dims, preferred_element_type=f32)  82 us
    ppermute x16, waiting for transfers between devices, seq_reduce(): right = lax.ppermute(right, 'seq', ring_right).astype(f32)  68.6 us
    ppermute x61, starting transfers between devices, swap(): return lax.ppermute(value, 'ctx', [(c, c ^ distance) for c in range(n_ctx)])  59.2 us
    ppermute x16, waiting for transfers between devices, seq_gather(): right = lax.ppermute(right, 'seq', ring_right)  47.3 us
    pallas_call x3, Pallas kernels, attend_back(): pl.pallas_call(functools.partial(attend_back_kernel, block, blocks), grid...  37.9 us
    ppermute x12, waiting for transfers between devices, seq_gather(): left = lax.ppermute(left, 'seq', ring_left)  28.7 us
  transfers between devices with their start and end apart: 125, of which 45 were waited for; matrix products, arithmetic and copies ran while one was open for 35% of the time, Pallas kernels for 5%

profile of v1, /device:TPU:0, one launch (start us, length us, event | category | flops | bytes accessed | tf_op | source)
XLA Modules:
  0.0 747.8 jit_solution(3857453861727123251)
XLA Ops:
  82.2 6.9 collective-permute-done.9
  115.2 7.7 %add_convert_fusion = bf16[960,2048]{1,0:T(8,128)(2,1)S(1)} fusion(f32[960]{0:T(1024)S(1)} %pad_maximum_fusion.9, bf16[1088,960]{1,0:T(8,128)(2,1)S(1)} %constant_dynamic-update-slice_fusion.24, bf16[512,1088]{0,1:T(8,128)(2,1)S(1)} %collective-permute-done.15, bf16[512,1088]{0,1:T(8,128)(2,1)} %collective-permute-done.14, ...), kind=kOutput, calls=%fused_computation.12 | convolution fusion | flops 4299948032 | bytes 10481408 | tf_op jit(solution)/shard_map/dot_general | solution.py:24
  123.0 8.8 %attend.4 = (bf16[4,128,512]{2,1,0:T(8,128)(2,1)S(1)}, f32[2,1,2048]{2,1,0:T(1,128)S(1)}) custom-call(s32[1]{0:T(128)} %bitcast.1.own_ref, s32[1,2048]{1,0:T(1,128)S(1)} %compare_select_fusion.3.start_ref, bf16[3,320,2048]{2,1,0:T(8,128)(2,1)S(1)} %bitcast.161), custom_call_target="tpu_custom_call" | custom-call | flops 10737418240 | bytes 2097152 | tf_op jit(solution)/shard_map/attend/pallas_call | solution.py:111
  131.8 9.0 %attend.3 = (bf16[4,128,512]{2,1,0:T(8,128)(2,1)S(1)}, f32[2,1,2048]{2,1,0:T(1,128)S(1)}) custom-call(s32[1]{0:T(128)} %bitcast.1.own_ref, s32[1,2048]{1,0:T(1,128)S(1)} %compare_select_fusion.3.start_ref, bf16[3,320,2048]{2,1,0:T(8,128)(2,1)S(1)} %bitcast.162), custom_call_target="tpu_custom_call" | custom-call | flops 10737418240 | bytes 2097152 | tf_op jit(solution)/shard_map/attend/pallas_call | solution.py:111
  148.4 7.6 %collective-permute-done.21 = bf16[64,512]{1,0:T(8,128)(2,1)S(1)} collective-permute-done((bf16[64,512]{1,0:T(8,128)(2,1)S(1)}, bf16[64,512]{1,0:T(8,128)(2,1)S(1)}, u32[]{:S(2)}, u32[]{:S(2)}) %collective-permute-start.21) | collective-permute-done | bytes 65568 | tf_op jit(solution)/shard_map/ppermute | solution.py:192
  175.5 14.6 %collective-permute-done.33 = bf16[136,1088]{1,0:T(8,128)(2,1)S(1)} collective-permute-done((bf16[136,1088]{1,0:T(8,128)(2,1)S(1)}, bf16[136,1088]{1,0:T(8,128)(2,1)S(1)}, u32[]{:S(2)}, u32[]{:S(2)}) %collective-permute-start.33) | collective-permute-done | bytes 295968 | tf_op jit(solution)/shard_map/ppermute | solution.py:259
  208.3 7.4 collective-permute-done.42
  216.2 12.6 %collective-permute-done.36 = bf16[512,1088]{0,1:T(8,128)(2,1)S(1)} collective-permute-done((bf16[512,1088]{0,1:T(8,128)(2,1)S(1)}, bf16[512,1088]{0,1:T(8,128)(2,1)S(1)}, u32[]{:S(2)}, u32[]{:S(2)}) %collective-permute-start.36) | collective-permute-done | bytes 1114144 | tf_op jit(solution)/shard_map/ppermute | solution.py:192
  231.2 7.5 collective-permute-done.49
  257.6 12.1 %multiply_convert_fusion = (bf16[2048,1088]{0,1:T(8,128)(2,1)}, f32[2048,1088]{0,1:T(8,128)}) fusion(f32[1088]{0:T(1024)S(1)} %dynamic_slice.262, bf16[1088,1088]{1,0:T(8,128)(2,1)S(1)} %constant_dynamic-update-slice_fusion.8, bf16[512,1088]{0,1:T(8,128)(2,1)} %collective-permute-done.37, bf16[512,1088]{0,1:T(8,128)(2,1)S(1)} %collective-permute-done.36, ...), kind=kOutput, calls=%fused_computation.9 | convolution fusion | flops 4879810560 | bytes 20197632 | tf_op jit(solution)/shard_map/dot_general | solution.py:24
  269.8 8.0 %convolution_convert_fusion.2 = bf16[1088,1088]{1,0:T(8,128)(2,1)S(1)} fusion(bf16[2048,1088]{0,1:T(8,128)(2,1)} %get-tuple-element.138, bf16[2048,1088]{0,1:T(8,128)(2,1)S(1)} %constant_dynamic-update-slice_fusion.32), kind=kOutput, calls=%fused_computation.16 | convolution fusion | flops 4849799168 | bytes 11280384 | tf_op jit(solution)/shard_map/dot_general | solution.py:24
  280.7 8.5 %convolution_convert_fusion.5 = bf16[2048,1088]{0,1:T(8,128)(2,1)S(1)} fusion(bf16[2048,1088]{0,1:T(8,128)(2,1)} %get-tuple-element.138, bf16[1088,1088]{1,0:T(8,128)(2,1)S(1)} %constant_dynamic-update-slice_fusion), kind=kOutput, calls=%fused_computation.19 | convolution fusion | flops 4850843648 | bytes 11280384 | tf_op jit(solution)/shard_map/dot_general | solution.py:24
  289.3 10.4 %convert_reduce_fusion = (f32[1088]{0:T(1024)S(1)}, bf16[2048,1088]{0,1:T(8,128)(2,1)}) fusion(f32[2048,1088]{0,1:T(8,128)S(1)} %bitcast.192, bf16[1088,1088]{1,0:T(8,128)(2,1)S(1)} %constant_dynamic-update-slice_fusion, bf16[2048,1088]{0,1:T(8,128)(2,1)S(1)} %constant_dynamic-update-slice_fusion.32), kind=kOutput, calls=%fused_computation.8 | convolution fusion | flops 4879809536 | bytes 20197632 | tf_op jit(solution)/shard_map/dot_general | solution.py:24
  299.7 8.7 %convolution_convert_fusion.1 = bf16[2048,1088]{0,1:T(8,128)(2,1)S(1)} fusion(bf16[1088,1088]{1,0:T(8,128)(2,1)S(1)} %constant_dynamic-update-slice_fusion.8, bf16[2048,1088]{0,1:T(8,128)(2,1)} %get-tuple-element.141), kind=kOutput, calls=%fused_computation.15 | convolution fusion | flops 4850843648 | bytes 11280384 | tf_op jit(solution)/shard_map/dot_general | solution.py:24
  308.4 7.7 %convolution_convert_fusion.3 = bf16[1088,1088]{1,0:T(8,128)(2,1)S(1)} fusion(bf16[2048,1088]{0,1:T(8,128)(2,1)S(1)} %copy-done.61, bf16[512,1088]{0,1:T(8,128)(2,1)} %collective-permute-done.37, bf16[512,1088]{0,1:T(8,128)(2,1)S(1)} %collective-permute-done.36, bf16[512,1088]{0,1:T(8,128)(2,1)S(1)} %copy-done.58, bf16[512,1088]{0,1:T(8,128)(2,1)S(1)} %add_convert_fusion.5), kind=kOutput, calls=%fused_computation.17 | convolution fusion | flops 4867624960 | bytes 11280384 | tf_op jit(solution)/shard_map/dot_general | solution.py:24
  375.6 9.4 %collective-permute-start.64 = (bf16[512,1088]{0,1:T(8,128)(2,1)}, bf16[512,1088]{0,1:T(8,128)(2,1)}, u32[]{:S(2)}, u32[]{:S(2)}) collective-permute-start(bf16[512,1088]{0,1:T(8,128)(2,1)} %add_convert_fusion.2), channel_id=1, source_target_pairs={{0,2},{1,3},{2,0},{3,1},{4,6},{5,7},{6,4},{7,5},{8,10},{9,11},{10,... | collective-permute-start | bytes 3342344 | tf_op jit(solution)/shard_map/ppermute | solution.py:192
  394.1 15.8 %collective-permute-done.123 = bf16[136,272]{1,0:T(8,128)(2,1)S(1)} collective-permute-done((bf16[136,272]{1,0:T(8,128)(2,1)S(1)}, bf16[136,272]{1,0:T(8,128)(2,1)S(1)}, u32[]{:S(2)}, u32[]{:S(2)}) %collective-permute-start.123) | collective-permute-done | bytes 74016 | tf_op jit(solution)/shard_map/ppermute | solution.py:192
  409.9 7.7 %collective-permute-start.124 = (bf16[136,272]{1,0:T(8,128)(2,1)}, bf16[136,272]{1,0:T(8,128)(2,1)}, u32[]{:S(2)}, u32[]{:S(2)}) collective-permute-start(bf16[136,272]{1,0:T(8,128)(2,1)} %get-tuple-element.107), channel_id=1, source_target_pairs={{0,3},{1,2},{2,1},{3,0},{4,7},{5,6},{6,5},{7,4},{8,11},{9,10},{10,... | collective-permute-start | bytes 221960 | tf_op jit(solution)/shard_map/ppermute | solution.py:192
  467.6 6.9 collective-permute-done.66
  487.2 15.0 %attend_back.3.rest_0_ = bf16[3,320,2048]{2,1,0:T(8,128)(2,1)S(1)} custom-call(s32[1]{0:T(128)} %bitcast.1.own_ref, s32[1,2048]{1,0:T(1,128)S(1)} %compare_select_fusion.3.start_ref, bf16[3,320,2048]{2,1,0:T(8,128)(2,1)S(1)} %bitcast.164, bf16[4,128,512]{2,1,0:T(8,128)(2,1)S(1)} %get-tuple-element.25.out_ref, ...), custom_call_target="tpu_custom_call" | custom-call | flops 21474836480 | bytes 4718592 | tf_op jit(solution)/shard_map/attend_back/pallas_call | solution.py:158
  504.3 15.5 %attend_back.4.rest_0_ = bf16[3,320,2048]{2,1,0:T(8,128)(2,1)S(1)} custom-call(s32[1]{0:T(128)} %bitcast.1.own_ref, s32[1,2048]{1,0:T(1,128)S(1)} %compare_select_fusion.3.start_ref, bf16[3,320,2048]{2,1,0:T(8,128)(2,1)S(1)} %bitcast.165, bf16[4,128,512]{2,1,0:T(8,128)(2,1)S(1)} %get-tuple-element.26.out_ref, ...), custom_call_target="tpu_custom_call", output_to_operand_aliasing={{}: (6, {})} | custom-call | flops 21474836480 | bytes 4718592 | tf_op jit(solution)/shard_map/attend_back/pallas_call | solution.py:158
  519.8 7.5 attend_back.5
  527.3 7.3 convolution_convert_fusion.6
  543.8 10.6 %collective-permute-done.82 = bf16[136,960]{0,1:T(8,128)(2,1)S(1)} collective-permute-done((bf16[136,960]{0,1:T(8,128)(2,1)S(1)}, bf16[136,960]{0,1:T(8,128)(2,1)S(1)}, u32[]{:S(2)}, u32[]{:S(2)}) %collective-permute-start.82) | collective-permute-done | bytes 261152 | tf_op jit(solution)/shard_map/ppermute | solution.py:272
  564.1 7.6 %collective-permute-done.83 = bf16[136,960]{0,1:T(8,128)(2,1)S(1)} collective-permute-done((bf16[136,960]{0,1:T(8,128)(2,1)S(1)}, bf16[136,960]{0,1:T(8,128)(2,1)S(1)}, u32[]{:S(2)}, u32[]{:S(2)}) %collective-permute-start.83) | collective-permute-done | bytes 261152 | tf_op jit(solution)/shard_map/ppermute | solution.py:272
  581.5 7.5 collective-permute-done.84
  594.0 11.3 %collective-permute-done.85 = bf16[136,960]{0,1:T(8,128)(2,1)S(1)} collective-permute-done((bf16[136,960]{0,1:T(8,128)(2,1)S(1)}, bf16[136,960]{0,1:T(8,128)(2,1)S(1)}, u32[]{:S(2)}, u32[]{:S(2)}) %collective-permute-start.85) | collective-permute-done | bytes 261152 | tf_op jit(solution)/shard_map/ppermute | solution.py:272
  619.7 22.0 %collective-permute-done.90 = bf16[136,3,320]{2,1,0:T(4,128)(2,1)} collective-permute-done((bf16[136,3,320]{2,1,0:T(4,128)(2,1)}, bf16[136,3,320]{2,1,0:T(4,128)(2,1)}, u32[]{:S(2)}, u32[]{:S(2)}) %collective-permute-start.90) | collective-permute-done | bytes 261152 | tf_op jit(solution)/shard_map/ppermute | solution.py:192
  650.9 10.4 %dynamic_update_slice.227 = bf16[136,3,1280]{2,1,0:T(4,128)(2,1)} dynamic-update-slice(bf16[136,3,1280]{2,1,0:T(4,128)(2,1)} %broadcast_in_dim.80, bf16[136,3,320]{2,1,0:T(4,128)(2,1)} %copy.44, s32[]{:T(128)} %constant.131.clone.1, s32[]{:T(128)} %constant.131.clone.1, s32[]{:T(128)S(6)} %select_n.139) | dynamic-update-slice | bytes 522244 | tf_op jit(solution)/shard_map/dynamic_update_slice | solution.py:218
  664.4 25.5 %dynamic_update_slice.228 = bf16[136,3,1280]{2,1,0:T(4,128)(2,1)} dynamic-update-slice(bf16[136,3,1280]{2,1,0:T(4,128)(2,1)} %dynamic_update_slice.227, bf16[136,3,320]{2,1,0:T(4,128)(2,1)} %collective-permute-done.89, s32[]{:T(128)} %constant.131.clone.1, s32[]{:T(128)} %constant.131.clone.1, s32[]{:T(128)S(6)} %select_n.157) | dynamic-update-slice | bytes 522244 | tf_op jit(solution)/shard_map/dynamic_update_slice | solution.py:218
  690.0 10.4 %dynamic_update_slice.229 = bf16[136,3,1280]{2,1,0:T(4,128)(2,1)} dynamic-update-slice(bf16[136,3,1280]{2,1,0:T(4,128)(2,1)} %dynamic_update_slice.228, bf16[136,3,320]{2,1,0:T(4,128)(2,1)} %collective-permute-done.90, s32[]{:T(128)} %constant.131.clone.1, s32[]{:T(128)} %constant.131.clone.1, s32[]{:T(128)S(6)} %select_n.158) | dynamic-update-slice | bytes 522244 | tf_op jit(solution)/shard_map/dynamic_update_slice | solution.py:218
  700.4 24.9 %dynamic_update_slice.230 = bf16[136,3,1280]{2,1,0:T(4,128)(2,1)} dynamic-update-slice(bf16[136,3,1280]{2,1,0:T(4,128)(2,1)} %dynamic_update_slice.229, bf16[136,3,320]{2,1,0:T(4,128)(2,1)} %collective-permute-done.91, s32[]{:T(128)} %constant.131.clone.1, s32[]{:T(128)} %constant.131.clone.1, s32[]{:T(128)S(6)} %select_n.159) | dynamic-update-slice | bytes 522244 | tf_op jit(solution)/shard_map/dynamic_update_slice | solution.py:218
  (541 shorter events, 374.6 us)
Async XLA Ops:
  12.0 79.6 %collective-permute-start.14 = (bf16[512,1088]{0,1:T(8,128)(2,1)}, bf16[512,1088]{0,1:T(8,128)(2,1)}, u32[]{:S(2)}, u32[]{:S(2)}) collective-permute-start(bf16[512,1088]{0,1:T(8,128)(2,1)} %fusion.15), channel_id=1, source_target_pairs={{0,2},{1,3},{2,0},{3,1},{4,6},{5,7},{6,4},{7,5},{8,10},{9,11},{10,... | collective-permute-start | bytes 3342344 | tf_op jit(solution)/shard_map/ppermute | solution.py:192
  31.2 37.3 %collective-permute-start.6 = (bf16[136,960]{1,0:T(8,128)(2,1)S(1)}, bf16[136,960]{1,0:T(8,128)(2,1)S(1)}, u32[]{:S(2)}, u32[]{:S(2)}) collective-permute-start(bf16[136,960]{1,0:T(8,128)(2,1)S(1)} %reshape.407), channel_id=1, source_target_pairs={{0,8},{8,16},{16,24},{24,28},{28,20},{20,12},{12,4},{4,0},{1,9},{9... | collective-permute-start | bytes 783368 | tf_op jit(solution)/shard_map/ppermute | solution.py:256
  34.2 32.2 %collective-permute-start.45 = (bf16[136,272]{1,0:T(8,128)(2,1)}, bf16[136,272]{1,0:T(8,128)(2,1)S(1)}, u32[]{:S(2)}, u32[]{:S(2)}) collective-permute-start(bf16[136,272]{1,0:T(8,128)(2,1)} %get-tuple-element.105), channel_id=1, source_target_pairs={{0,1},{1,0},{2,3},{3,2},{4,5},{5,4},{6,7},{7,6},{8,9},{9,8},{10,11... | collective-permute-start | bytes 221960 | tf_op jit(solution)/shard_map/ppermute | solution.py:192
  34.4 32.3 %collective-permute-start.46 = (bf16[136,272]{1,0:T(8,128)(2,1)S(1)}, bf16[136,272]{1,0:T(8,128)(2,1)S(1)}, u32[]{:S(2)}, u32[]{:S(2)}) collective-permute-start(bf16[136,272]{1,0:T(8,128)(2,1)S(1)} %copy-done.33), channel_id=1, source_target_pairs={{0,2},{1,3},{2,0},{3,1},{4,6},{5,7},{6,4},{7,5},{8,10},{9,11},{10,... | collective-permute-start | bytes 221960 | tf_op jit(solution)/shard_map/ppermute | solution.py:192
  41.8 37.8 %collective-permute-start.7 = (bf16[136,960]{1,0:T(8,128)(2,1)S(1)}, bf16[136,960]{1,0:T(8,128)(2,1)S(1)}, u32[]{:S(2)}, u32[]{:S(2)}) collective-permute-start(bf16[136,960]{1,0:T(8,128)(2,1)S(1)} %reshape.407), channel_id=1, source_target_pairs={{0,4},{8,0},{16,8},{24,16},{28,24},{20,28},{12,20},{4,12},{1,5},{9... | collective-permute-start | bytes 783368 | tf_op jit(solution)/shard_map/ppermute | solution.py:259
  77.0 38.2 %collective-permute-start.13 = (bf16[512,1088]{0,1:T(8,128)(2,1)}, bf16[512,1088]{0,1:T(8,128)(2,1)}, u32[]{:S(2)}, u32[]{:S(2)}) collective-permute-start(bf16[512,1088]{0,1:T(8,128)(2,1)} %fusion.15), channel_id=1, source_target_pairs={{0,1},{1,0},{2,3},{3,2},{4,5},{5,4},{6,7},{7,6},{8,9},{9,8},{10,11... | collective-permute-start | bytes 3342344 | tf_op jit(solution)/shard_map/ppermute | solution.py:192
  159.4 69.4 %collective-permute-start.48 = (bf16[136,1088]{1,0:T(8,128)(2,1)S(1)}, bf16[136,1088]{1,0:T(8,128)(2,1)S(1)}, u32[]{:S(2)}, u32[]{:S(2)}) collective-permute-start(bf16[136,1088]{1,0:T(8,128)(2,1)S(1)} %dynamic_update_slice.216), channel_id=1, source_target_pairs={{0,0},{1,4},{2,8},{3,12},{4,16},{5,20},{6,24},{7,28},{8,1},{9,5},{... | collective-permute-start | bytes 887816 | tf_op jit(solution)/shard_map/ppermute | solution.py:321
  169.1 36.7 %collective-permute-start.59 = (bf16[512,1088]{0,1:T(8,128)(2,1)S(1)}, bf16[512,1088]{0,1:T(8,128)(2,1)S(1)}, u32[]{:S(2)}, u32[]{:S(2)}) collective-permute-start(bf16[512,1088]{0,1:T(8,128)(2,1)S(1)} %bitcast.168), channel_id=1, source_target_pairs={{0,1},{1,0},{2,3},{3,2},{4,5},{5,4},{6,7},{7,6},{8,9},{9,8},{10,11... | collective-permute-start | bytes 3342344 | tf_op jit(solution)/shard_map/ppermute | solution.py:192
  169.9 36.5 %collective-permute-start.60 = (bf16[512,1088]{0,1:T(8,128)(2,1)S(1)}, bf16[512,1088]{0,1:T(8,128)(2,1)S(1)}, u32[]{:S(2)}, u32[]{:S(2)}) collective-permute-start(bf16[512,1088]{0,1:T(8,128)(2,1)S(1)} %bitcast.169), channel_id=1, source_target_pairs={{0,2},{1,3},{2,0},{3,1},{4,6},{5,7},{6,4},{7,5},{8,10},{9,11},{10,... | collective-permute-start | bytes 3342344 | tf_op jit(solution)/shard_map/ppermute | solution.py:192
  205.8 50.8 %collective-permute-start.35 = (bf16[512,1088]{0,1:T(8,128)(2,1)S(1)}, bf16[512,1088]{0,1:T(8,128)(2,1)S(1)}, u32[]{:S(2)}, u32[]{:S(2)}) collective-permute-start(bf16[512,1088]{0,1:T(8,128)(2,1)S(1)} %add_convert_fusion.5), channel_id=1, source_target_pairs={{0,1},{1,0},{2,3},{3,2},{4,5},{5,4},{6,7},{7,6},{8,9},{9,8},{10,11... | collective-permute-start | bytes 3342344 | tf_op jit(solution)/shard_map/ppermute | solution.py:192
  216.0 33.7 %collective-permute-start.61 = (bf16[512,1088]{0,1:T(8,128)(2,1)S(1)}, bf16[512,1088]{0,1:T(8,128)(2,1)S(1)}, u32[]{:S(2)}, u32[]{:S(2)}) collective-permute-start(bf16[512,1088]{0,1:T(8,128)(2,1)S(1)} %collective-permute-done.60), channel_id=1, source_target_pairs={{0,1},{1,0},{2,3},{3,2},{4,5},{5,4},{6,7},{7,6},{8,9},{9,8},{10,11... | collective-permute-start | bytes 3342344 | tf_op jit(solution)/shard_map/ppermute | solution.py:192
  278.6 43.7 %collective-permute-start.114 = (bf16[136,1088]{1,0:T(8,128)(2,1)}, bf16[136,1088]{1,0:T(8,128)(2,1)}, u32[]{:S(2)}, u32[]{:S(2)}) collective-permute-start(bf16[136,1088]{1,0:T(8,128)(2,1)} %get-tuple-element.61), channel_id=1, source_target_pairs={{0,8},{8,16},{16,24},{24,28},{28,20},{20,12},{12,4},{4,0},{1,9},{9... | collective-permute-start | bytes 887816 | tf_op jit(solution)/shard_map/ppermute | solution.py:272
  279.9 46.9 %collective-permute-start.118 = (bf16[136,1088]{1,0:T(8,128)(2,1)}, bf16[136,1088]{1,0:T(8,128)(2,1)}, u32[]{:S(2)}, u32[]{:S(2)}) collective-permute-start(bf16[136,1088]{1,0:T(8,128)(2,1)} %get-tuple-element.62), channel_id=1, source_target_pairs={{0,4},{8,0},{16,8},{24,16},{28,24},{20,28},{12,20},{4,12},{1,5},{9... | collective-permute-start | bytes 887816 | tf_op jit(solution)/shard_map/ppermute | solution.py:276
  320.4 65.4 %collective-permute-start.57 = (bf16[512,1088]{0,1:T(8,128)(2,1)S(1)}, bf16[512,1088]{0,1:T(8,128)(2,1)S(1)}, u32[]{:S(2)}, u32[]{:S(2)}) collective-permute-start(bf16[512,1088]{0,1:T(8,128)(2,1)S(1)} %get-tuple-element.56), channel_id=1, source_target_pairs={{0,1},{1,0},{2,3},{3,2},{4,5},{5,4},{6,7},{7,6},{8,9},{9,8},{10,11... | collective-permute-start | bytes 3342344 | tf_op jit(solution)/shard_map/ppermute | solution.py:192
  322.3 50.0 %collective-permute-start.63 = (bf16[512,1088]{0,1:T(8,128)(2,1)}, bf16[512,1088]{0,1:T(8,128)(2,1)S(1)}, u32[]{:S(2)}, u32[]{:S(2)}) collective-permute-start(bf16[512,1088]{0,1:T(8,128)(2,1)} %get-tuple-element.54), channel_id=1, source_target_pairs={{0,1},{1,0},{2,3},{3,2},{4,5},{5,4},{6,7},{7,6},{8,9},{9,8},{10,11... | collective-permute-start | bytes 3342344 | tf_op jit(solution)/shard_map/ppermute | solution.py:192
  326.8 118.0 %collective-permute-start.62 = (bf16[512,1088]{0,1:T(8,128)(2,1)}, bf16[512,1088]{0,1:T(8,128)(2,1)}, u32[]{:S(2)}, u32[]{:S(2)}) collective-permute-start(bf16[512,1088]{0,1:T(8,128)(2,1)} %get-tuple-element.53), channel_id=1, source_target_pairs={{0,1},{1,0},{2,3},{3,2},{4,5},{5,4},{6,7},{7,6},{8,9},{9,8},{10,11... | collective-permute-start | bytes 3342344 | tf_op jit(solution)/shard_map/ppermute | solution.py:192
  375.6 69.2 %collective-permute-start.64 = (bf16[512,1088]{0,1:T(8,128)(2,1)}, bf16[512,1088]{0,1:T(8,128)(2,1)}, u32[]{:S(2)}, u32[]{:S(2)}) collective-permute-start(bf16[512,1088]{0,1:T(8,128)(2,1)} %add_convert_fusion.2), channel_id=1, source_target_pairs={{0,2},{1,3},{2,0},{3,1},{4,6},{5,7},{6,4},{7,5},{8,10},{9,11},{10,... | collective-permute-start | bytes 3342344 | tf_op jit(solution)/shard_map/ppermute | solution.py:192
  392.3 55.7 %collective-permute-start.56 = (bf16[512,1088]{0,1:T(8,128)(2,1)}, bf16[512,1088]{0,1:T(8,128)(2,1)}, u32[]{:S(2)}, u32[]{:S(2)}) collective-permute-start(bf16[512,1088]{0,1:T(8,128)(2,1)} %get-tuple-element.55), channel_id=1, source_target_pairs={{0,1},{1,0},{2,3},{3,2},{4,5},{5,4},{6,7},{7,6},{8,9},{9,8},{10,11... | collective-permute-start | bytes 3342344 | tf_op jit(solution)/shard_map/ppermute | solution.py:192
  392.3 55.7 %collective-permute-start.58 = (bf16[512,1088]{0,1:T(8,128)(2,1)}, bf16[512,1088]{0,1:T(8,128)(2,1)}, u32[]{:S(2)}, u32[]{:S(2)}) collective-permute-start(bf16[512,1088]{0,1:T(8,128)(2,1)} %add_convert_fusion.4), channel_id=1, source_target_pairs={{0,2},{1,3},{2,0},{3,1},{4,6},{5,7},{6,4},{7,5},{8,10},{9,11},{10,... | collective-permute-start | bytes 3342344 | tf_op jit(solution)/shard_map/ppermute | solution.py:192
  474.6 67.8 %collective-permute-start.92 = (bf16[136,1088]{1,0:T(8,128)(2,1)S(1)}, bf16[136,1088]{1,0:T(8,128)(2,1)S(1)}, u32[]{:S(2)}, u32[]{:S(2)}) collective-permute-start(bf16[136,1088]{1,0:T(8,128)(2,1)S(1)} %get-tuple-element.73), channel_id=1, source_target_pairs={{0,8},{8,16},{16,24},{24,28},{28,20},{20,12},{12,4},{4,0},{1,9},{9... | collective-permute-start | bytes 887816 | tf_op jit(solution)/shard_map/ppermute | solution.py:272
  484.9 69.8 %collective-permute-start.96 = (bf16[136,1088]{1,0:T(8,128)(2,1)S(1)}, bf16[136,1088]{1,0:T(8,128)(2,1)S(1)}, u32[]{:S(2)}, u32[]{:S(2)}) collective-permute-start(bf16[136,1088]{1,0:T(8,128)(2,1)S(1)} %get-tuple-element.74), channel_id=1, source_target_pairs={{0,4},{8,0},{16,8},{24,16},{28,24},{20,28},{12,20},{4,12},{1,5},{9... | collective-permute-start | bytes 887816 | tf_op jit(solution)/shard_map/ppermute | solution.py:276
  502.1 59.2 %collective-permute-start.105 = (f32[8704]{0:T(1024)S(1)}, f32[8704]{0:T(1024)S(1)}, u32[]{:S(2)}, u32[]{:S(2)}) collective-permute-start(f32[8704]{0:T(1024)S(1)} %add.852), channel_id=1, source_target_pairs={{0,8},{4,12},{8,0},{12,4},{16,24},{20,28},{24,16},{28,20},{1,9},{5... | collective-permute-start | bytes 104456 | tf_op jit(solution)/shard_map/ppermute | solution.py:285
  554.4 37.2 %collective-permute-start.75 = (bf16[512,1088]{0,1:T(8,128)(2,1)S(1)}, bf16[512,1088]{0,1:T(8,128)(2,1)S(1)}, u32[]{:S(2)}, u32[]{:S(2)}) collective-permute-start(bf16[512,1088]{0,1:T(8,128)(2,1)S(1)} %get-tuple-element.52), channel_id=1, source_target_pairs={{0,1},{1,0},{2,3},{3,2},{4,5},{5,4},{6,7},{7,6},{8,9},{9,8},{10,11... | collective-permute-start | bytes 3342344 | tf_op jit(solution)/shard_map/ppermute | solution.py:192
  564.0 54.9 %collective-permute-start.74 = (bf16[512,1088]{0,1:T(8,128)(2,1)}, bf16[512,1088]{0,1:T(8,128)(2,1)S(1)}, u32[]{:S(2)}, u32[]{:S(2)}) collective-permute-start(bf16[512,1088]{0,1:T(8,128)(2,1)} %get-tuple-element.51), channel_id=1, source_target_pairs={{0,1},{1,0},{2,3},{3,2},{4,5},{5,4},{6,7},{7,6},{8,9},{9,8},{10,11... | collective-permute-start | bytes 3342344 | tf_op jit(solution)/shard_map/ppermute | solution.py:192
  579.4 31.7 %collective-permute-start.95 = (bf16[136,1088]{1,0:T(8,128)(2,1)}, bf16[136,1088]{1,0:T(8,128)(2,1)}, u32[]{:S(2)}, u32[]{:S(2)}) collective-permute-start(bf16[136,1088]{1,0:T(8,128)(2,1)} %get-tuple-element.69), channel_id=1, source_target_pairs={{0,8},{8,16},{16,24},{24,28},{28,20},{20,12},{12,4},{4,0},{1,9},{9... | collective-permute-start | bytes 887816 | tf_op jit(solution)/shard_map/ppermute | solution.py:272
  607.3 34.4 %collective-permute-start.76 = (bf16[512,1088]{0,1:T(8,128)(2,1)}, bf16[512,1088]{0,1:T(8,128)(2,1)S(1)}, u32[]{:S(2)}, u32[]{:S(2)}) collective-permute-start(bf16[512,1088]{0,1:T(8,128)(2,1)} %add_convert_fusion.1), channel_id=1, source_target_pairs={{0,2},{1,3},{2,0},{3,1},{4,6},{5,7},{6,4},{7,5},{8,10},{9,11},{10,... | collective-permute-start | bytes 3342344 | tf_op jit(solution)/shard_map/ppermute | solution.py:192
  611.2 30.5 %collective-permute-start.90 = (bf16[136,3,320]{2,1,0:T(4,128)(2,1)}, bf16[136,3,320]{2,1,0:T(4,128)(2,1)}, u32[]{:S(2)}, u32[]{:S(2)}) collective-permute-start(bf16[136,3,320]{2,1,0:T(4,128)(2,1)} %copy.44), channel_id=1, source_target_pairs={{0,2},{1,3},{2,0},{3,1},{4,6},{5,7},{6,4},{7,5},{8,10},{9,11},{10,... | collective-permute-start | bytes 783368 | tf_op jit(solution)/shard_map/ppermute | solution.py:192
  616.7 47.7 %collective-permute-start.89 = (bf16[136,3,320]{2,1,0:T(4,128)(2,1)}, bf16[136,3,320]{2,1,0:T(4,128)(2,1)}, u32[]{:S(2)}, u32[]{:S(2)}) collective-permute-start(bf16[136,3,320]{2,1,0:T(4,128)(2,1)} %copy.44), channel_id=1, source_target_pairs={{0,1},{1,0},{2,3},{3,2},{4,5},{5,4},{6,7},{7,6},{8,9},{9,8},{10,11... | collective-permute-start | bytes 783368 | tf_op jit(solution)/shard_map/ppermute | solution.py:192
  617.2 45.4 %collective-permute-start.99 = (bf16[136,272]{1,0:T(8,128)(2,1)S(1)}, bf16[136,272]{1,0:T(8,128)(2,1)}, u32[]{:S(2)}, u32[]{:S(2)}) collective-permute-start(bf16[136,272]{1,0:T(8,128)(2,1)S(1)} %get-tuple-element.111), channel_id=1, source_target_pairs={{0,1},{1,0},{2,3},{3,2},{4,5},{5,4},{6,7},{7,6},{8,9},{9,8},{10,11... | collective-permute-start | bytes 221960 | tf_op jit(solution)/shard_map/ppermute | solution.py:192
  619.0 43.7 %collective-permute-start.101 = (bf16[136,272]{1,0:T(8,128)(2,1)}, bf16[136,272]{1,0:T(8,128)(2,1)}, u32[]{:S(2)}, u32[]{:S(2)}) collective-permute-start(bf16[136,272]{1,0:T(8,128)(2,1)} %add_convert_fusion.29), channel_id=1, source_target_pairs={{0,2},{1,3},{2,0},{3,1},{4,6},{5,7},{6,4},{7,5},{8,10},{9,11},{10,... | collective-permute-start | bytes 221960 | tf_op jit(solution)/shard_map/ppermute | solution.py:192
  641.7 58.7 %collective-permute-start.91 = (bf16[136,3,320]{2,1,0:T(4,128)(2,1)}, bf16[136,3,320]{2,1,0:T(4,128)(2,1)}, u32[]{:S(2)}, u32[]{:S(2)}) collective-permute-start(bf16[136,3,320]{2,1,0:T(4,128)(2,1)} %collective-permute-done.90), channel_id=1, source_target_pairs={{0,1},{1,0},{2,3},{3,2},{4,5},{5,4},{6,7},{7,6},{8,9},{9,8},{10,11... | collective-permute-start | bytes 783368 | tf_op jit(solution)/shard_map/ppermute | solution.py:192
  662.0 69.9 %collective-permute-start.78 = (f32[4352]{0:T(1024)S(1)}, f32[4352]{0:T(1024)S(1)}, u32[]{:S(2)}, u32[]{:S(2)}) collective-permute-start(f32[4352]{0:T(1024)S(1)} %add.823), channel_id=1, source_target_pairs={{0,2},{1,3},{2,0},{3,1},{4,6},{5,7},{6,4},{7,5},{8,10},{9,11},{10,... | collective-permute-start | bytes 52232 | tf_op jit(solution)/shard_map/ppermute | solution.py:192
  (158 other events, 2238.4 us)

commit v2 on v1

v2 whole, which is shorter than its diff:
```python
import functools

import jax
import jax.numpy as jnp
from jax import lax
from jax.experimental import pallas as pl
from jax.experimental.pallas import tpu as pltpu
from jax.sharding import PartitionSpec as P

HEADS = 17
HEAD_DIM = 64

eps = 1e-05
neg_big = -1e30
f32 = jnp.float32
bf16 = jnp.bfloat16

NN = (((1,), (0,)), ((), ()))
NT = (((1,), (1,)), ((), ()))
TN = (((0,), (0,)), ((), ()))


def mm(left, right, dims=NN):
    return lax.dot_general(left, right, dims, preferred_element_type=f32)


def layer_norm(values, norm_gain, norm_shift):
    average = jnp.mean(values, axis=-1, keepdims=True)
    centred = values - average
    variance = jnp.mean(centred * centred, axis=-1, keepdims=True)
    return centred * lax.rsqrt(variance + eps) * norm_gain + norm_shift


def after(value, *earlier):
    return lax.optimization_barrier((value, *earlier))[0]


def allowed_tile(start, i, j, block):
    key_pos = j * block + lax.broadcasted_iota(jnp.int32, (block, block), 0)
    allowed = key_pos >= start
    if i == j:
        query_pos = i * block + lax.broadcasted_iota(jnp.int32, (block, block), 1)
        allowed = allowed & (key_pos <= query_pos)
    return allowed


def attend_kernel(block, blocks, own_ref, start_ref, qkv_ref, out_ref, log_ref):
    slots = [own_ref[0] ^ i for i in range(blocks)]
    cols = [pl.ds(pl.multiple_of(slot * block, block), block) for slot in slots]
    scale = jnp.asarray(HEAD_DIM ** (-0.5), bf16)
    for i in range(blocks):
        query = qkv_ref[0, :, cols[i]] * scale
        start = start_ref[:, cols[i]]
        scores = []
        for j in range(i + 1):
            score = mm(qkv_ref[1, :, cols[j]], query, TN)
            scores.append(jnp.where(allowed_tile(start, i, j, block), score, neg_big))
        top = functools.reduce(
            jnp.maximum, [jnp.max(score, axis=0, keepdims=True) for score in scores]
        )
        total, sums = jnp.zeros_like(top), None
        for j in range(i + 1):
            power = jnp.exp(scores[j] - top)
            total = total + jnp.sum(power, axis=0, keepdims=True)
            part = mm(qkv_ref[2, :, cols[j]], power.astype(bf16))
            sums = part if sums is None else sums + part
        out_ref[slots[i]] = (sums / total).astype(bf16)
        log_ref[0, :, cols[i]] = top + jnp.log(total)


def attend_back_kernel(
    block, blocks, own_ref, start_ref, qkv_ref, out_ref, grad_ref, log_ref, *rest
):
    back_ref, query_sum = rest[-2:]
    slots = [own_ref[0] ^ i for i in range(blocks)]
    cols = [pl.ds(pl.multiple_of(slot * block, block), block) for slot in slots]
    scale = jnp.asarray(HEAD_DIM ** (-0.5), bf16)
    dots = [
        jnp.sum(out_ref[slot].astype(f32) * grad_ref[slot].astype(f32), axis=0, keepdims=True)
        for slot in slots
    ]
    for j in range(blocks):
        key = qkv_ref[1, :, cols[j]]
        value = qkv_ref[2, :, cols[j]]
        key_sum = value_sum = None
        for i in range(j, blocks):
            query = qkv_ref[0, :, cols[i]] * scale
            grad = grad_ref[slots[i]]
            score = mm(key, query, TN)
            allowed = allowed_tile(start_ref[:, cols[i]], i, j, block)
            soft = jnp.where(allowed, jnp.exp(score - log_ref[0, :, cols[i]]), 0.0)
            back = (soft * (mm(value, grad, TN) - dots[i])).astype(bf16)
            value_part = mm(grad, soft.astype(bf16), NT)
            key_part = mm(query, back, NT)
            value_sum = value_part if value_sum is None else value_sum + value_part
            key_sum = key_part if key_sum is None else key_sum + key_part
            if j == 0:
                query_sum[i] = mm(key, back)
            else:
                query_sum[i] += mm(key, back)
        back_ref[1, :, cols[j]] = key_sum.astype(bf16)
        back_ref[2, :, cols[j]] = value_sum.astype(bf16)
    for i in range(blocks):
        back_ref[0, :, cols[i]] = (query_sum[i] * HEAD_DIM ** (-0.5)).astype(bf16)


def attend(own, start, qkv, block, first, count):
    _, width, length = qkv.shape
    blocks = length // block
    pairs = count * block * block * blocks * (blocks + 1) // 2
    return pl.pallas_call(
        functools.partial(attend_kernel, block, blocks),
        grid_spec=pltpu.PrefetchScalarGridSpec(
            num_scalar_prefetch=1,
            grid=(count,),
            in_specs=[
                pl.BlockSpec((1, length), lambda h, own: (0, 0)),
                pl.BlockSpec((3, HEAD_DIM, length), lambda h, own: (0, first + h, 0)),
            ],
            out_specs=[
                pl.BlockSpec((blocks, HEAD_DIM, block), lambda h, own: (0, h, 0)),
                pl.BlockSpec((1, 1, length), lambda h, own: (h, 0, 0)),
            ],
        ),
        out_shape=[
            jax.ShapeDtypeStruct((blocks, count * HEAD_DIM, block), bf16),
            jax.ShapeDtypeStruct((count, 1, length), f32),
        ],
        compiler_params=pltpu.CompilerParams(vmem_limit_bytes=24 * 2**20),
        cost_estimate=pl.CostEstimate(
            flops=pairs * 4 * 256 * 2,
            bytes_accessed=count * HEAD_DIM * length * 8,
            transcendentals=pairs,
        ),
        name="attend",
    )(own, start, qkv)


def attend_back(own, start, qkv, out, grad, log, block, first, count, held, grad_first):
    _, width, length = qkv.shape
    blocks = length // block
    pairs = count * block * block * blocks * (blocks + 1) // 2
    tile = pl.BlockSpec((3, HEAD_DIM, length), lambda h, own: (0, first + h, 0))
    side = pl.BlockSpec((blocks, HEAD_DIM, block), lambda h, own: (0, h, 0))
    in_specs = [
        pl.BlockSpec((1, length), lambda h, own: (0, 0)),
        tile,
        side,
        pl.BlockSpec((blocks, HEAD_DIM, block), lambda h, own: (0, first - grad_first + h, 0)),
        pl.BlockSpec((1, 1, length), lambda h, own: (h, 0, 0)),
    ]
    operands = (own, start, qkv, out, grad, log)
    aliases = {}
    if held is not None:
        in_specs.append(pl.BlockSpec(memory_space=pl.ANY))
        operands = (*operands, held)
        aliases = {len(operands) - 1: 0}
    return pl.pallas_call(
        functools.partial(attend_back_kernel, block, blocks),
        grid_spec=pltpu.PrefetchScalarGridSpec(
            num_scalar_prefetch=1,
            grid=(count,),
            in_specs=in_specs,
            out_specs=tile,
            scratch_shapes=[pltpu.VMEM((blocks, HEAD_DIM, block), f32)],
        ),
        out_shape=jax.ShapeDtypeStruct(qkv.shape, bf16),
        input_output_aliases=aliases,
        compiler_params=pltpu.CompilerParams(vmem_limit_bytes=24 * 2**20),
        cost_estimate=pl.CostEstimate(
            flops=pairs * 8 * 256 * 2,
            bytes_accessed=count * HEAD_DIM * length * 18,
            transcendentals=pairs,
        ),
        name="attend_back",
    )(*operands)


def move_columns(own, sources, widths, plan, dtype):
    rows = sources[0].shape[0]

    def kernel(own_ref, *refs):
        source_refs, target_refs = refs[: len(sources)], refs[len(sources) :]
        for c, moves in enumerate(plan):

            @pl.when(own_ref[0] == c)
            def _():
                for t, (ref, width) in enumerate(zip(target_refs, widths)):
                    covered = sum(move[4] for move in moves if move[0] == t)
                    if covered < width:
                        ref[...] = jnp.zeros_like(ref)
                for t, to, s, start, count in moves:
                    piece = source_refs[s][:, start : start + count]
                    target_refs[t][:, to : to + count] = piece.astype(dtype)

    return pl.pallas_call(
        kernel,
        in_specs=[pl.BlockSpec(memory_space=pltpu.SMEM)]
        + [pl.BlockSpec(memory_space=pltpu.VMEM)] * len(sources),
        out_specs=[pl.BlockSpec(memory_space=pltpu.VMEM)] * len(widths),
        out_shape=[jax.ShapeDtypeStruct((rows, width), dtype) for width in widths],
        compiler_params=pltpu.CompilerParams(vmem_limit_bytes=32 * 2**20),
        name="move_columns",
    )(own, *sources)


def join_rows(own, blocks, dtype):
    size, width = blocks[0].shape

    def kernel(own_ref, *refs):
        for c in range(len(blocks)):

            @pl.when(own_ref[0] == c)
            def _():
                for r in range(len(blocks)):
                    refs[-1][(c ^ r) * size : ((c ^ r) + 1) * size] = refs[r][...].astype(dtype)

    return pl.pallas_call(
        kernel,
        in_specs=[pl.BlockSpec(memory_space=pltpu.SMEM)]
        + [pl.BlockSpec(memory_space=pltpu.VMEM)] * len(blocks),
        out_specs=pl.BlockSpec(memory_space=pltpu.VMEM),
        out_shape=jax.ShapeDtypeStruct((size * len(blocks), width), dtype),
        compiler_params=pltpu.CompilerParams(vmem_limit_bytes=32 * 2**20),
        name="join_rows",
    )(own, *blocks)


def solution(mesh):
    n_seq, n_ctx = mesh.shape["seq"], mesh.shape["ctx"]
    per_device = -(-HEADS // n_ctx)
    share = per_device * HEAD_DIM
    padded = share * n_ctx
    half = n_seq // 2
    cycle = list(range(0, n_seq, 2)) + list(range(1, n_seq, 2))[::-1]
    ring_right = [(cycle[p], cycle[(p + 1) % n_seq]) for p in range(n_seq)]
    ring_left = [(cycle[p], cycle[(p - 1) % n_seq]) for p in range(n_seq)]
    steps_right, steps_left = n_seq // 2, (n_seq - 1) // 2
    sizes = [1, per_device - 3, 1, 1] if per_device > 3 else [1] * per_device
    groups = [(sum(sizes[:g]), size) for g, size in enumerate(sizes)]

    def swap(value, distance):
        return lax.ppermute(value, "ctx", [(c, c ^ distance) for c in range(n_ctx)])

    def go_right(value):
        return lax.ppermute(value, "seq", ring_right)

    def go_left(value):
        return lax.ppermute(value, "seq", ring_left)

    def ctx_gather(value):
        blocks = [value]
        for r in range(1, n_ctx):
            blocks.append(swap(blocks[r - 1], 1) if r % 2 else swap(value, r))
        return blocks

    def with_neighbours(evens):
        return [block for even in evens for block in (even, swap(even, 1))]

    def ctx_exchange(blocks):
        return [blocks[0]] + [swap(blocks[r], r) for r in range(1, n_ctx)]

    def ctx_reduce(parts):
        total = None
        for r in range(n_ctx - 2, -1, -2):
            both = parts[r].astype(f32) + swap(parts[r + 1], 1).astype(f32)
            if r:
                both = swap(both.astype(bf16), r).astype(f32)
            total = both if total is None else total + both
        return total

    def in_order(blocks, own):
        size = blocks[0].shape[0]
        whole = jnp.zeros((size * n_ctx, *blocks[0].shape[1:]), blocks[0].dtype)
        for r, piece in enumerate(blocks):
            whole = lax.dynamic_update_slice_in_dim(whole, piece, (own ^ r) * size, 0)
        return whole

    def column_plans(width, column):
        take, give = [], []
        for c in range(n_ctx):
            moves = []
            for third in range(3):
                first, last = c * share, min((c + 1) * share, width)
                place = third * width + first
                while place < third * width + last:
                    shard = place // column
                    stop = min((shard + 1) * column, third * width + last)
                    to = third * share + place - third * width - first
                    moves.append((0, to, shard ^ c, place - shard * column, stop - place))
                    place = stop
            take.append(moves)
        for c in range(n_ctx):
            moves = []
            for d in range(n_ctx):
                for _, at, shard, start, count in take[d]:
                    if shard ^ d == c:
                        moves.append((0, start, c ^ d, at, count))
            give.append(moves)
        return take, give

    def body(
        tokens,
        segments,
        cotangent,
        gain_one,
        shift_one,
        w_qkv,
        bias_q,
        bias_v,
        w_out,
        bias_out,
        gain_two,
        shift_two,
        w_up,
        bias_up,
        w_down,
        bias_down,
    ):
        rows, width = tokens.shape[1:]
        depth = w_up.shape[0]
        hidden_own = w_up.shape[1]
        hidden = hidden_own * n_ctx
        own = lax.axis_index("ctx")
        own_array = jnp.reshape(own, (1,)).astype(jnp.int32)
        seq = lax.axis_index("seq")
        spot = jnp.where(seq % 2 == 0, seq // 2, n_seq - 1 - seq // 2)

        def ring_row(step):
            p = lax.rem(spot + (n_seq + step), n_seq)
            return jnp.where(p < half, 2 * p, 2 * (n_seq - 1 - p) + 1)

        def put(wholes, pieces, step):
            row = ring_row(step)
            return [
                lax.dynamic_update_slice_in_dim(whole, piece, row * piece.shape[0], 0)
                for whole, piece in zip(wholes, pieces)
            ]

        def blank(pieces):
            return [jnp.zeros((n_seq * p.shape[0], p.shape[1]), p.dtype) for p in pieces]

        def take(part, step):
            size = part.shape[0] // n_seq
            return lax.dynamic_slice_in_dim(part, ring_row(step) * size, size, 0)

        def step_right_left(step, right, left):
            return go_right(right), go_left(left) if step <= steps_left else None

        def pick(parts, step):
            pieces = [take(part, step).reshape(-1, parts[-1].shape[1]) for part in parts]
            return pieces[0] if len(pieces) == 1 else jnp.concatenate(pieces)

        def reduce_go(step, right, left):
            return go_right(right), go_left(left) if step > steps_right - steps_left else left

        def reduce_add(parts, step, right, left):
            if step > 1:
                right = (right.astype(f32) + pick(parts, step - 1).astype(f32)).astype(bf16)
            rest = step - (steps_right - steps_left)
            if rest > 1:
                left = (left.astype(f32) + pick(parts, 1 - rest).astype(f32)).astype(bf16)
            return right, left

        def reduce_step(parts, step, right, left):
            return reduce_add(parts, step, *reduce_go(step, right, left))

        def reduce_start(parts):
            return pick(parts, steps_right), pick(parts, -steps_left)

        def reduce_end(parts, right, left):
            return right.astype(f32) + left.astype(f32) + pick(parts, 0).astype(f32)

        def all_sum(value, beside):
            beside, stage = list(beside), 0
            for axis in ("ctx", "seq"):
                size, r = mesh.shape[axis], 1
                while r < size:
                    hops = [r, 2 * r, 3 * r] if 2 * r < size else [r]
                    others = [
                        lax.ppermute(value, axis, [(d, d ^ hop) for d in range(size)])
                        for hop in hops
                    ]
                    if stage < len(beside):
                        others[0], beside[stage] = lax.optimization_barrier(
                            (others[0], beside[stage])
                        )
                    value = value + others[0]
                    if len(hops) > 1:
                        value = value + (others[1] + others[2])
                    r, stage = r * (len(hops) + 1), stage + 1
            return value, beside

        inputs = tokens[0].astype(f32)
        upstream_low = cotangent[0]
        upstream = upstream_low.astype(f32)
        take_plan, give_plan = column_plans(width, w_qkv.shape[1])

        w_qkv_blocks = ctx_gather(w_qkv)
        normed_one, norm_back_one = jax.vjp(layer_norm, inputs, gain_one, shift_one)
        normed_one_low = normed_one.astype(bf16)
        normed_one_blocks = ctx_gather(normed_one_low)
        out_column = w_out.shape[1]
        aligned = -(-out_column // 128) * 128
        first_plan = [
            [(0, 0, n_ctx, 0, out_column)]
            + [(0, aligned + to, slot, at, count) for _, to, slot, at, count in moves]
            for moves in take_plan
        ]
        (w_first_rows,) = move_columns(
            own_array, [*w_qkv_blocks, w_out], [aligned + 3 * share], first_plan, bf16
        )
        wholes = put(blank([w_first_rows]), [w_first_rows], 0)
        right = left = w_first_rows
        for step in range(1, steps_right + 1):
            right, left = step_right_left(step, right, left)
            wholes = put(wholes, [right], -step)
            if left is not None:
                wholes = put(wholes, [left], step)
        w_qkv_own, w_out_columns = wholes[0][:, aligned:], wholes[0][:, :aligned]
        last = right

        upstream_evens = [upstream_low] + [
            swap(after(upstream_low, normed_one_blocks[-2]), r) for r in range(2, n_ctx, 2)
        ]
        w_out_evens = [w_out_columns] + [
            swap(after(w_out_columns, upstream_evens[-1]), r) for r in range(2, n_ctx, 2)
        ]
        normed_one_all = jnp.concatenate(normed_one_blocks)
        segment_all = jnp.concatenate(ctx_gather(segments[0]))
        start = jnp.zeros_like(segment_all)
        for number in range(1, 5):
            count = jnp.sum((segment_all < number).astype(jnp.int32))
            start = jnp.where(segment_all == number, count, start)
        start = start[None]

        piece, column = w_down.shape[0] // n_ctx, w_down.shape[1]
        w_down_pieces = w_down.reshape(n_ctx, piece, column)
        w_down_pieces = ctx_exchange(
            [lax.dynamic_index_in_dim(w_down_pieces, own ^ r, 0, False) for r in range(n_ctx)]
        )
        join_plan = [[(0, (c ^ r) * column, r, 0, column) for r in range(n_ctx)] for c in range(n_ctx)]
        (w_down_rows,) = move_columns(own_array, w_down_pieces, [width], join_plan, bf16)
        spread = [(b, (b % n_seq) * n_ctx + b // n_seq) for b in range(n_seq * n_ctx)]
        w_down_rows = lax.ppermute(after(w_down_rows, w_first_rows), ("seq", "ctx"), spread)
        w_mlp_rows = jnp.concatenate([w_up.reshape(-1, width), w_down_rows])

        def cut_mlp(block):
            upper, lower = jnp.split(block, 2)
            return upper.reshape(depth, hidden_own), lower

        bias_qkv = jnp.concatenate(
            [
                lax.dynamic_slice_in_dim(jnp.pad(bias, (0, padded - width)), own * share, share)
                for bias in (bias_q, jnp.zeros_like(bias_q), bias_v)
            ]
        )
        qkv = (mm(w_qkv_own, normed_one_all, (((0,), (1,)), ((), ()))) + bias_qkv[:, None]).astype(
            bf16
        )
        qkv = qkv.reshape(3, share, -1)
        wholes = put(blank(cut_mlp(w_mlp_rows)), cut_mlp(w_mlp_rows), 0)
        right = left = after(w_mlp_rows, last)
        outs, logs, arrived, step = [], [], [], 0
        for first, count in groups:
            if step < 1:
                step += 1
                right, left = step_right_left(step, right, left)
            elif left is not None and step < steps_right:
                qkv, right, left = lax.optimization_barrier((qkv, right, left))
                if step == 1:
                    qkv, *upstream_evens = lax.optimization_barrier((qkv, *upstream_evens))
                elif step == 2:
                    qkv, *w_out_evens = lax.optimization_barrier((qkv, *w_out_evens))
                wholes = put(wholes, cut_mlp(right), -step)
                if left is not None:
                    wholes = put(wholes, cut_mlp(left), step)
                step += 1
                right, left = step_right_left(step, right, left)
            out, log = attend(own_array, start, qkv, rows, first, count)
            outs.append(out)
            logs.append(log)
            if first + count == per_device or len(outs) == len(groups) - 1:
                sent = outs[-1:] if arrived else outs
                arrived.append(
                    ctx_exchange([jnp.concatenate([o[r] for o in sent]) for r in range(n_ctx)])
                )
        join_plan = [
            [(0, (c ^ r) * out_column, r, 0, out_column) for r in range(n_ctx)] for c in range(n_ctx)
        ]
        (w_out_all,) = move_columns(
            own_array, with_neighbours(w_out_evens), [width], join_plan, bf16
        )
        upstream_blocks = with_neighbours(upstream_evens)
        attended = in_order(
            [jnp.concatenate([part[r] for part in arrived]) for r in range(n_ctx)], own
        )[:width]
        attended, right = lax.optimization_barrier((attended, right))
        wholes = put(wholes, cut_mlp(right), -step)
        if left is not None:
            wholes = put(wholes, cut_mlp(left), step)
        middle = inputs + mm(attended, w_out_all, TN) + bias_out
        normed_two, norm_back_two = jax.vjp(layer_norm, middle, gain_two, shift_two)
        normed_two_low = normed_two.astype(bf16)
        while step < steps_right:
            step += 1
            if step == steps_right:
                right = after(right, normed_two_low)
            right, left = step_right_left(step, right, left)
            wholes = put(wholes, cut_mlp(right), -step)
            if left is not None:
                wholes = put(wholes, cut_mlp(left), step)
        w_up_own, w_down_own = wholes

        bias_up_own = lax.dynamic_slice_in_dim(bias_up, own * hidden_own, hidden_own)

        def feed(normed, grad):
            pre = mm(normed, w_up_own) + bias_up_own
            cumulative = 0.5 * (1.0 + lax.erf(pre * 0.5**0.5))
            activated = (pre * cumulative).astype(bf16)
            slope = cumulative + pre * jnp.exp(-0.5 * pre * pre) * (0.5 / jnp.pi) ** 0.5
            grad_pre = (mm(grad, w_down_own, NT) * slope).astype(bf16)
            return activated, grad_pre, mm(grad_pre, w_up_own, NT).astype(bf16)

        near = n_ctx // 2
        evens = [normed_two_low] + [swap(normed_two_low, r) for r in range(2, n_ctx, 2)]
        normed_near = with_neighbours(evens[: near // 2])
        normed_near = jnp.concatenate(normed_near)
        upstream_near = jnp.concatenate(upstream_blocks[:near])
        act_near, grad_pre_near, grad_norm_near = feed(normed_near, upstream_near)
        act_near, grad_pre_near, grad_norm_near, *evens = lax.optimization_barrier(
            (act_near, grad_pre_near, grad_norm_near, *evens)
        )
        normed_far = with_neighbours(evens[near // 2 :])
        normed_far = jnp.concatenate(normed_far)
        upstream_far = jnp.concatenate(upstream_blocks[near:])
        act_far, grad_pre_far, grad_norm_far = feed(normed_far, upstream_far)
        far_parts = jnp.split(grad_norm_far, near)
        far_sums = [
            (far_parts[r] + swap(far_parts[r + 1], 1)).astype(bf16) for r in range(0, near, 2)
        ]
        near_parts = jnp.split(grad_norm_near, near)
        near_sums = [
            near_parts[r].astype(f32) + swap(near_parts[r + 1], 1).astype(f32)
            for r in range(0, near, 2)
        ]
        act_near, act_far, grad_pre_near, grad_pre_far, *far_sums = lax.optimization_barrier(
            (act_near, act_far, grad_pre_near, grad_pre_far, *far_sums)
        )
        grad_norm_two = near_sums[0]
        for r in range(2, n_ctx, 2):
            part = near_sums[r // 2].astype(bf16) if r < near else far_sums[(r - near) // 2]
            grad_norm_two = grad_norm_two + swap(part, r).astype(f32)
        part_w_down = (mm(act_near, upstream_near, TN) + mm(act_far, upstream_far, TN)).astype(bf16)
        part_w_up = (mm(normed_near, grad_pre_near, TN) + mm(normed_far, grad_pre_far, TN)).astype(
            bf16
        )
        mlp_out_parts = [
            part
            for act in (act_near, act_far)
            for part in jnp.split(mm(act, w_down_own).astype(bf16), near)
        ]
        mlp_parts = [part_w_up, part_w_down]
        mlp_step = steps_right
        right, left = reduce_start(mlp_parts)
        right, left = reduce_go(mlp_step, right, left)
        grad_norm_two, *mlp_out_parts = lax.optimization_barrier((grad_norm_two, *mlp_out_parts))
        grad_middle_part, grad_gain_two, grad_shift_two = norm_back_two(grad_norm_two)
        grad_middle = upstream + grad_middle_part

        grad_branch = grad_middle.astype(bf16)
        grad_attended = mm(w_out_all, grad_branch, NT).astype(bf16)
        grad_attended = jnp.pad(grad_attended, ((0, padded - width), (0, 0)))
        grad_attended = grad_attended.reshape(n_ctx, share, -1)
        grad_attended = [
            lax.dynamic_index_in_dim(grad_attended, own ^ r, 0, False) for r in range(n_ctx)
        ]

        grad_attended, right, left = lax.optimization_barrier((grad_attended, right, left))
        right, left = reduce_add(mlp_parts, mlp_step, right, left)
        grad_owns = []
        for first, last in ((0, groups[0][1]), (groups[0][1], per_device)):
            if last > first:
                span = slice(first * HEAD_DIM, last * HEAD_DIM)
                grad_owns.append(
                    (first, jnp.stack(ctx_exchange([part[span] for part in grad_attended])))
                )
        mlp_sums = [
            mlp_out_parts[r].astype(f32) + swap(mlp_out_parts[r + 1], 1).astype(f32)
            for r in range(0, n_ctx, 2)
        ]
        mlp_far = [swap(mlp_sums[r // 2].astype(bf16), r) for r in range(2, n_ctx, 2)]
        grad_bias_up_own = jnp.sum(grad_pre_near.astype(f32), axis=0) + jnp.sum(
            grad_pre_far.astype(f32), axis=0
        )
        early = jnp.concatenate(
            [
                jnp.sum(upstream, axis=0),
                grad_gain_two,
                grad_shift_two,
                jnp.sum(grad_branch.astype(f32), axis=0),
                lax.dynamic_update_slice_in_dim(
                    jnp.zeros((hidden,), f32), grad_bias_up_own, own * hidden_own, 0
                ),
            ]
        )

        part_w_out = mm(attended, grad_branch).astype(bf16)
        back = None
        for g, ((first, count), out, log) in enumerate(zip(groups, outs, logs)):
            grad_first, grad_own = grad_owns[min(g, 1)]
            if g and mlp_step > 1:
                mlp_step -= 1
                right, left = reduce_step(mlp_parts, mlp_step, right, left)
                grad_own, right, left = lax.optimization_barrier((grad_own, right, left))
            if g == 1:
                grad_own, *mlp_sums = lax.optimization_barrier((grad_own, *mlp_sums))
                mlp_far = [swap(mlp_sums[r // 2].astype(bf16), r) for r in range(2, n_ctx, 2)]
            if g == 2:
                grad_own, *mlp_far = lax.optimization_barrier((grad_own, *mlp_far))
            back = attend_back(
                own_array, start, qkv, out, grad_own, log, rows, first, count, back, grad_first
            )
            if g == min(1, len(groups) - 1):
                part_plan = [
                    [(r, 0, 0, (c ^ r) * out_column, out_column) for r in range(n_ctx)]
                    for c in range(n_ctx)
                ]
                part_w_out = ctx_reduce(
                    move_columns(
                        own_array,
                        [after(part_w_out, back)],
                        [aligned] * n_ctx,
                        part_plan,
                        bf16,
                    )
                ).astype(bf16)
        while mlp_step > 1:
            mlp_step -= 1
            right, left = reduce_step(mlp_parts, mlp_step, right, left)
        grad_mlp_rows = reduce_end(mlp_parts, right, left)
        grad_w_up, grad_w_down_rows = jnp.split(grad_mlp_rows, 2)
        grad_w_up = grad_w_up.reshape(depth, hidden_own)
        back, part_w_out, early = lax.optimization_barrier((back, part_w_out, early))
        mlp_out = mlp_sums[0]
        for far in mlp_far:
            mlp_out = mlp_out + far.astype(f32)

        grad_proj = back.reshape(3 * share, -1)
        far_grad = grad_proj[:, near * rows :]
        far_parts = jnp.split(
            mm(far_grad, w_qkv_own, (((0,), (1,)), ((), ()))).astype(bf16), near
        )
        far_sums = [
            (far_parts[r] + swap(far_parts[r + 1], 1)).astype(bf16) for r in range(0, near, 2)
        ]
        grad_proj, grad_w_down_rows, *far_sums = lax.optimization_barrier(
            (grad_proj, grad_w_down_rows, *far_sums)
        )
        part_w_qkv = mm(normed_one_all, grad_proj, (((0,), (1,)), ((), ()))).astype(bf16)
        last_parts = [jnp.concatenate([part_w_out, part_w_qkv], axis=1)]
        right, left = reduce_start(last_parts)
        grad_proj, right, left = lax.optimization_barrier((grad_proj, right, left))
        near_parts = jnp.split(
            mm(grad_proj[:, : near * rows], w_qkv_own, (((0,), (1,)), ((), ()))).astype(bf16), near
        )
        near_sums = [
            near_parts[r].astype(f32) + swap(near_parts[r + 1], 1).astype(f32)
            for r in range(0, near, 2)
        ]
        grad_norm_one = near_sums[0]
        for r in range(2, n_ctx, 2):
            part = near_sums[r // 2].astype(bf16) if r < near else far_sums[(r - near) // 2]
            grad_norm_one = grad_norm_one + swap(part, r).astype(f32)

        for step in range(steps_right, 0, -1):
            right, left = reduce_step(last_parts, step, right, left)
            if step == steps_right - 1:
                output = (middle + mlp_out + bias_down).astype(bf16)
                grad_norm_one, right, left, output = lax.optimization_barrier(
                    (grad_norm_one, right, left, output)
                )
        last_rows = reduce_end(last_parts, right, left)
        grad_w_out = last_rows[:, :out_column]
        grad_w_qkv_rows = last_rows[:, aligned:].astype(bf16)
        (grad_w_qkv,) = move_columns(
            own_array, ctx_gather(grad_w_qkv_rows), [w_qkv.shape[1]], give_plan, f32
        )

        gathered = [(b, a) for a, b in spread]
        grad_w_down_rows = lax.ppermute(grad_w_down_rows.astype(bf16), ("seq", "ctx"), gathered)
        column = w_down.shape[1]
        part_plan = [[(r, 0, 0, (c ^ r) * column, column) for r in range(n_ctx)] for c in range(n_ctx)]
        grad_w_down_pieces = ctx_exchange(
            move_columns(
                own_array, [after(grad_w_down_rows, grad_norm_one)], [column] * n_ctx, part_plan, bf16
            )
        )
        grad_w_down = join_rows(own_array, grad_w_down_pieces, f32)

        grad_input_part, grad_gain_one, grad_shift_one = norm_back_one(grad_norm_one)
        grad_tokens = grad_middle + grad_input_part
        grad_bias_qkv = jnp.sum(back.astype(f32), axis=2)
        sums, (grad_tokens, grad_w_down) = all_sum(
            jnp.concatenate(
                [grad_gain_one, grad_shift_one]
                + [
                    lax.dynamic_update_slice_in_dim(
                        jnp.zeros((padded,), f32), grad_bias_qkv[g], own * share, 0
                    )[:width]
                    for g in (0, 2)
                ]
                + [early]
            ),
            [grad_tokens, grad_w_down],
        )
        (
            grad_gain_one,
            grad_shift_one,
            grad_bias_q,
            grad_bias_v,
            grad_bias_down,
            grad_gain_two,
            grad_shift_two,
            grad_bias_out,
        ) = (sums[g * width : (g + 1) * width] for g in range(8))
        grad_bias_up = sums[8 * width :]
        return (
            output[None],
            grad_tokens[None],
            grad_gain_one,
            grad_shift_one,
            grad_w_qkv,
            grad_bias_q,
            grad_bias_v,
            grad_w_out,
            grad_bias_out,
            grad_gain_two,
            grad_shift_two,
            grad_w_up,
            grad_bias_up,
            grad_w_down,
            grad_bias_down,
        )

    block = P("seq", "ctx", None)
    split = P("seq", "ctx")
    return jax.shard_map(
        body,
        mesh=mesh,
        in_specs=(
            block,
            split,
            block,
            P(),
            P(),
            split,
            P(),
            P(),
            split,
            P(),
            P(),
            P(),
            split,
            P(),
            split,
            P(),
        ),
        out_specs=(
            block,
            block,
            P(),
            P(),
            split,
            P(),
            P(),
            split,
            P(),
            P(),
            P(),
            split,
            P(),
            split,
            P(),
        ),
        check_vma=False,
    )
```

time: 760 us -> 461 us (0.61)
  local copies, waits for them, and re-layouts: 146 us -> 40.6 us
  waiting for transfers between devices: 246 us -> 161 us
  starting transfers between devices: 136 us -> 79.1 us
  other arithmetic: 57.7 us -> 37.4 us
  between operations: 20.4 us -> 2.77 us
  matrix products: 82 us -> 70 us
    dynamic_update_slice x53 -> x17, local copies, waits for them, and re-layouts: 110 us -> 0.93 us  [put(): lax.dynamic_update_slice_in_dim(whole, piece, row * piece.shape[0], 0)]
    ppermute x63 -> x36, waiting for transfers between devices: 161 us -> 98.4 us  [the longest x16 56.6 us: go_right(): return lax.ppermute(value, 'seq', ring_right)]
    ppermute x61 -> x51, starting transfers between devices: 59.2 us -> 27 us  [swap(): return lax.ppermute(value, 'ctx', [(c, c ^ distance) for c in range(n_ctx)])]
    ppermute x63 -> x36, starting transfers between devices: 75.8 us -> 50.1 us  [the longest x16 29.8 us: go_right(): return lax.ppermute(value, 'seq', ring_right)]
    ppermute x61 -> x51, waiting for transfers between devices: 85.5 us -> 62.8 us  [swap(): return lax.ppermute(value, 'ctx', [(c, c ^ distance) for c in range(n_ctx)])]
    unnamed x134 -> x181, local copies, waits for them, and re-layouts: 4.71 us -> 22.7 us
    convert_element_type x23 -> x14, other arithmetic: 26.6 us -> 10.8 us  [the longest x1 3.4 us: body(): output = (middle + mlp_out + bias_down).astype(bf16)]
    dot_general x12 -> x19, matrix products: 82 us -> 70 us  [mm(): return lax.dot_general(left, right, dims, preferred_element_type=f32)]
  transfers between devices with their start and end apart: 125 -> 88, of which waited for: 45 -> 38; matrix products, arithmetic and copies ran while one was open for 35% -> 22% of each run, Pallas kernels for 5% -> 14%
where the time goes in v2:
time: 461 us; the launch traced here: 455 us
  waiting for transfers between devices  161 us (35%)
  starting transfers between devices  79.1 us (17%)
  matrix products  70 us (15%)
  Pallas kernels  63.8 us (14%)
  local copies, waits for them, and re-layouts  40.6 us (9%)
  other arithmetic  37.4 us (8%)
    dot_general x19, matrix products, mm(): return lax.dot_general(left, right, dims, preferred_element_type=f32)  70 us
    ppermute x51, waiting for transfers between devices, swap(): return lax.ppermute(value, 'ctx', [(c, c ^ distance) for c in range(n_ctx)])  62.8 us
    ppermute x16, waiting for transfers between devices, go_right(): return lax.ppermute(value, 'seq', ring_right)  56.6 us
    pallas_call x4, Pallas kernels, attend_back(): pl.pallas_call(functools.partial(attend_back_kernel, block, blocks), grid...  37.3 us
    ppermute x12, waiting for transfers between devices, go_left(): return lax.ppermute(value, 'seq', ring_left)  35.5 us
    ppermute x16, starting transfers between devices, go_right(): return lax.ppermute(value, 'seq', ring_right)  29.8 us
    ppermute x51, starting transfers between devices, swap(): return lax.ppermute(value, 'ctx', [(c, c ^ distance) for c in range(n_ctx)])  27 us
    unnamed x181, local copies, waits for them, and re-layouts  22.7 us
  transfers between devices with their start and end apart: 88, of which 38 were waited for; matrix products, arithmetic and copies ran while one was open for 22% of the time, Pallas kernels for 14%

profile of v2, /device:TPU:0, one launch (start us, length us, event | category | flops | bytes accessed | tf_op | source)
XLA Modules:
  0.0 454.8 jit_solution(6387896203496650727)
XLA Ops:
  23.7 4.5 collective-permute-start.6
  29.7 8.5 %collective-permute-done.6 = bf16[136,1344]{1,0:T(8,128)(2,1)S(1)} collective-permute-done((bf16[136,1344]{1,0:T(8,128)(2,1)S(1)}, bf16[136,1344]{1,0:T(8,128)(2,1)S(1)}, u32[]{:S(2)}, u32[]{:S(2)}) %collective-permute-start.6) | collective-permute-done | bytes 365600 | tf_op jit(solution)/shard_map/ppermute | solution.py:246
  38.3 8.6 %collective-permute-start.8 = (bf16[136,1344]{1,0:T(8,128)(2,1)S(1)}, bf16[136,1344]{1,0:T(8,128)(2,1)S(1)}, u32[]{:S(2)}, u32[]{:S(2)}) collective-permute-start(bf16[136,1344]{1,0:T(8,128)(2,1)S(1)} %collective-permute-done.6), channel_id=1, source_target_pairs={{0,8},{8,16},{16,24},{24,28},{28,20},{20,12},{12,4},{4,0},{1,9},{9... | collective-permute-start | bytes 1096712 | tf_op jit(solution)/shard_map/ppermute | solution.py:246
  46.9 8.3 %collective-permute-done.7 = bf16[136,1344]{1,0:T(8,128)(2,1)S(1)} collective-permute-done((bf16[136,1344]{1,0:T(8,128)(2,1)S(1)}, bf16[136,1344]{1,0:T(8,128)(2,1)S(1)}, u32[]{:S(2)}, u32[]{:S(2)}) %collective-permute-start.7) | collective-permute-done | bytes 365600 | tf_op jit(solution)/shard_map/ppermute | solution.py:249
  57.5 8.6 %collective-permute-done.9 = bf16[136,1344]{1,0:T(8,128)(2,1)S(1)} collective-permute-done((bf16[136,1344]{1,0:T(8,128)(2,1)S(1)}, bf16[136,1344]{1,0:T(8,128)(2,1)S(1)}, u32[]{:S(2)}, u32[]{:S(2)}) %collective-permute-start.9) | collective-permute-done | bytes 365600 | tf_op jit(solution)/shard_map/ppermute | solution.py:249
  68.3 7.9 %collective-permute-done.11 = bf16[136,1344]{1,0:T(8,128)(2,1)S(1)} collective-permute-done((bf16[136,1344]{1,0:T(8,128)(2,1)S(1)}, bf16[136,1344]{1,0:T(8,128)(2,1)S(1)}, u32[]{:S(2)}, u32[]{:S(2)}) %collective-permute-start.11) | collective-permute-done | bytes 365600 | tf_op jit(solution)/shard_map/ppermute | solution.py:249
  82.3 5.4 %add_convert_fusion = bf16[960,2048]{1,0:T(8,128)(2,1)S(1)} fusion(f32[960]{0:T(1024)S(1)} %pad_maximum_fusion.14, bf16[1088,1344]{1,0:T(8,128)(2,1)S(1)} %constant_dynamic-update-slice_fusion.2, bf16[512,1088]{0,1:T(8,128)(2,1)S(1)} %collective-permute-done.15, bf16[512,1088]{0,1:T(8,128)(2,1)S(1)} %collective-permute-done.14, ...), kind=kOutput, calls=%fused_computation.11 | convolution fusion | flops 4299948032 | bytes 10620928 | tf_op jit(solution)/shard_map/dot_general | solution.py:24
  87.7 4.4 attend.5
  98.8 8.8 %attend.6 = (bf16[4,128,512]{2,1,0:T(8,128)(2,1)S(1)}, f32[2,1,2048]{2,1,0:T(1,128)S(1)}) custom-call(s32[1]{0:T(128)} %bitcast.own_ref, s32[1,2048]{1,0:T(1,128)S(1)} %compare_select_fusion.3.start_ref, bf16[3,320,2048]{2,1,0:T(8,128)(2,1)S(1)} %bitcast.143), custom_call_target="tpu_custom_call" | custom-call | flops 10737418240 | bytes 2097152 | tf_op jit(solution)/shard_map/attend/pallas_call | solution.py:111
  107.8 5.0 %collective-permute-done.23 = bf16[272,1088]{1,0:T(8,128)(2,1)S(1)} collective-permute-done((bf16[272,1088]{1,0:T(8,128)(2,1)S(1)}, bf16[272,1088]{1,0:T(8,128)(2,1)S(1)}, u32[]{:S(2)}, u32[]{:S(2)}) %collective-permute-start.23) | collective-permute-done | bytes 591904 | tf_op jit(solution)/shard_map/ppermute | solution.py:246
  121.0 7.6 %collective-permute-done.26 = bf16[272,1088]{1,0:T(8,128)(2,1)S(1)} collective-permute-done((bf16[272,1088]{1,0:T(8,128)(2,1)S(1)}, bf16[272,1088]{1,0:T(8,128)(2,1)S(1)}, u32[]{:S(2)}, u32[]{:S(2)}) %collective-permute-start.26) | collective-permute-done | bytes 591904 | tf_op jit(solution)/shard_map/ppermute | solution.py:246
  128.8 4.3 attend.4
  137.8 6.0 %collective-permute-done.33 = bf16[64,512]{1,0:T(8,128)(2,1)S(1)} collective-permute-done((bf16[64,512]{1,0:T(8,128)(2,1)S(1)}, bf16[64,512]{1,0:T(8,128)(2,1)S(1)}, u32[]{:S(2)}, u32[]{:S(2)}) %collective-permute-start.33) | collective-permute-done | bytes 65568 | tf_op jit(solution)/shard_map/ppermute | solution.py:243
  155.3 5.2 %multiply_convert_fusion.1 = (bf16[1024,1088]{0,1:T(8,128)(2,1)}, f32[1024,1088]{0,1:T(8,128)S(1)}) fusion(f32[1088]{0:T(1024)S(1)} %dynamic_slice.117, bf16[1088,1088]{1,0:T(8,128)(2,1)S(1)} %get-tuple-element.286, bf16[512,1088]{0,1:T(8,128)(2,1)S(1)} %collective-permute-done.37, bf16[512,1088]{0,1:T(8,128)(2,1)S(1)} %add_convert_fusion.2), kind=kOutput, calls=%fused_computation.34 | convolution fusion | flops 2435448832 | bytes 11284736 | tf_op jit(solution)/shard_map/dot_general | solution.py:24
  160.6 4.5 fusion.10
  169.4 10.3 %collective-permute-done.39 = bf16[512,1088]{0,1:T(8,128)(2,1)S(1)} collective-permute-done((bf16[512,1088]{0,1:T(8,128)(2,1)S(1)}, bf16[512,1088]{0,1:T(8,128)(2,1)S(1)}, u32[]{:S(2)}, u32[]{:S(2)}) %collective-permute-start.39) | collective-permute-done | bytes 1114144 | tf_op jit(solution)/shard_map/ppermute | solution.py:243
  182.6 5.2 %multiply_convert_fusion = (bf16[1024,1088]{0,1:T(8,128)(2,1)}, f32[1024,1088]{0,1:T(8,128)S(1)}) fusion(f32[1088]{0:T(1024)S(1)} %dynamic_slice.117, bf16[1024,1088]{0,1:T(8,128)(2,1)S(1)} %constant_dynamic-update-slice_fusion.12, bf16[1088,1088]{1,0:T(8,128)(2,1)S(1)} %get-tuple-element.286), kind=kOutput, calls=%fused_computation.32 | convolution fusion | flops 2430992384 | bytes 11284736 | tf_op jit(solution)/shard_map/dot_general | solution.py:24
  201.6 4.9 %convolution_convert_fusion.5 = bf16[1024,1088]{0,1:T(8,128)(2,1)S(1)} fusion(bf16[1024,1088]{0,1:T(8,128)(2,1)} %get-tuple-element.136, bf16[1088,1088]{1,0:T(8,128)(2,1)S(1)} %copy-done.34), kind=kOutput, calls=%fused_computation.42 | convolution fusion | flops 2425421824 | bytes 6823936 | tf_op jit(solution)/shard_map/dot_general | solution.py:24
  231.1 5.1 %collective-permute-done.44 = bf16[512,1088]{0,1:T(8,128)(2,1)S(1)} collective-permute-done((bf16[512,1088]{0,1:T(8,128)(2,1)S(1)}, bf16[512,1088]{0,1:T(8,128)(2,1)S(1)}, u32[]{:S(2)}, u32[]{:S(2)}) %collective-permute-start.44) | collective-permute-done | bytes 1114144 | tf_op jit(solution)/shard_map/ppermute | solution.py:243
  250.4 11.6 %collective-permute-done.60 = bf16[64,512]{1,0:T(8,128)(2,1)S(1)} collective-permute-done((bf16[64,512]{1,0:T(8,128)(2,1)S(1)}, bf16[64,512]{1,0:T(8,128)(2,1)S(1)}, u32[]{:S(2)}, u32[]{:S(2)}) %collective-permute-start.60) | collective-permute-done | bytes 65568 | tf_op jit(solution)/shard_map/ppermute | solution.py:243
  264.4 7.4 %attend_back.4.rest_0_ = bf16[3,320,2048]{2,1,0:T(8,128)(2,1)S(1)} custom-call(s32[1]{0:T(128)} %bitcast.own_ref, s32[1,2048]{1,0:T(1,128)S(1)} %compare_select_fusion.3.start_ref, bf16[3,320,2048]{2,1,0:T(8,128)(2,1)S(1)} %bitcast.146, bf16[4,64,512]{2,1,0:T(8,128)(2,1)S(1)} %get-tuple-element.121.out_ref, ...), custom_call_target="tpu_custom_call" | custom-call | flops 10737418240 | bytes 2359296 | tf_op jit(solution)/shard_map/attend_back/pallas_call | solution.py:158
  272.6 6.0 %collective-permute-done.50 = bf16[272,1088]{1,0:T(8,128)(2,1)S(1)} collective-permute-done((bf16[272,1088]{1,0:T(8,128)(2,1)S(1)}, bf16[272,1088]{1,0:T(8,128)(2,1)S(1)}, u32[]{:S(2)}, u32[]{:S(2)}) %collective-permute-start.50) | collective-permute-done | bytes 591904 | tf_op jit(solution)/shard_map/ppermute | solution.py:246
  285.4 15.0 %attend_back.5.rest_0_ = bf16[3,320,2048]{2,1,0:T(8,128)(2,1)S(1)} custom-call(s32[1]{0:T(128)} %bitcast.own_ref, s32[1,2048]{1,0:T(1,128)S(1)} %compare_select_fusion.3.start_ref, bf16[3,320,2048]{2,1,0:T(8,128)(2,1)S(1)} %bitcast.147, bf16[4,128,512]{2,1,0:T(8,128)(2,1)S(1)} %get-tuple-element.122.out_ref, ...), custom_call_target="tpu_custom_call", output_to_operand_aliasing={{}: (6, {})} | custom-call | flops 21474836480 | bytes 4718592 | tf_op jit(solution)/shard_map/attend_back/pallas_call | solution.py:158
  308.8 13.9 %collective-permute-done.54 = bf16[272,1088]{1,0:T(8,128)(2,1)} collective-permute-done((bf16[272,1088]{1,0:T(8,128)(2,1)}, bf16[272,1088]{1,0:T(8,128)(2,1)}, u32[]{:S(2)}, u32[]{:S(2)}) %collective-permute-start.54) | collective-permute-done | bytes 591904 | tf_op jit(solution)/shard_map/ppermute | solution.py:246
  332.1 7.4 %attend_back.6.rest_0_ = bf16[3,320,2048]{2,1,0:T(8,128)(2,1)S(1)} custom-call(s32[1]{0:T(128)} %bitcast.own_ref, s32[1,2048]{1,0:T(1,128)S(1)} %compare_select_fusion.3.start_ref, bf16[3,320,2048]{2,1,0:T(8,128)(2,1)S(1)} %bitcast.148, bf16[4,64,512]{2,1,0:T(8,128)(2,1)S(1)} %copy-done.6, ...), custom_call_target="tpu_custom_call", output_to_operand_aliasing={{}: (6, {})} | custom-call | flops 10737418240 | bytes 2359296 | tf_op jit(solution)/shard_map/attend_back/pallas_call | solution.py:158
  339.5 7.6 %attend_back.7 = bf16[3,320,2048]{2,1,0:T(8,128)(2,1)S(1)} custom-call(s32[1]{0:T(128)} %bitcast.own_ref, s32[1,2048]{1,0:T(1,128)S(1)} %compare_select_fusion.3.start_ref, bf16[3,320,2048]{2,1,0:T(8,128)(2,1)S(1)} %bitcast.149, bf16[4,64,512]{2,1,0:T(8,128)(2,1)S(1)} %copy-done.8, ...), custom_call_target="tpu_custom_call", output_to_operand_aliasing={{}: (6, {})} | custom-call | flops 10737418240 | bytes 2359296 | tf_op jit(solution)/shard_map/attend_back/pallas_call | solution.py:158
  359.3 6.6 %convolution_convert_fusion.7 = bf16[1088,960]{0,1:T(8,128)(2,1)} fusion(bf16[960,2048]{1,0:T(8,128)(2,1)S(1)} %bitcast.140, bf16[512,1088]{0,1:T(8,128)(2,1)S(1)} %copy-done.82, bf16[512,1088]{0,1:T(8,128)(2,1)S(1)} %copy-done.78, bf16[512,1088]{0,1:T(8,128)(2,1)S(1)} %copy-done.80, bf16[512,1088]{0,1:T(8,128)(2,1)S(1)} %copy-done.50), kind=kOutput, calls=%fused_computation.44 | convolution fusion | flops 4297060352 | bytes 10477568 | tf_op jit(solution)/shard_map/dot_general | solution.py:24
  394.4 5.1 %collective-permute-done.68 = bf16[136,1344]{1,0:T(8,128)(2,1)} collective-permute-done((bf16[136,1344]{1,0:T(8,128)(2,1)}, bf16[136,1344]{1,0:T(8,128)(2,1)}, u32[]{:S(2)}, u32[]{:S(2)}) %collective-permute-start.68) | collective-permute-done | bytes 365600 | tf_op jit(solution)/shard_map/ppermute | solution.py:246
  401.3 5.0 %collective-permute-done.66 = bf16[512,1088]{0,1:T(8,128)(2,1)} collective-permute-done((bf16[512,1088]{0,1:T(8,128)(2,1)}, bf16[512,1088]{0,1:T(8,128)(2,1)}, u32[]{:S(2)}, u32[]{:S(2)}) %collective-permute-start.66) | collective-permute-done | bytes 1114144 | tf_op jit(solution)/shard_map/ppermute | solution.py:243
  413.1 5.2 %add_add_fusion.2 = f32[512,1088]{0,1:T(8,128)} fusion(f32[512,1088]{0,1:T(8,128)} %copy-done.23, f32[512]{0:T(512)S(1)} %negate_multiply_fusion, f32[512]{0:T(512)S(1)} %negate_multiply_fusion.1, f32[512]{0:T(512)S(1)} %multiply_multiply_fusion.2, f32[512]{0:T(512)S(1)} %copy-done.66, bf16[1,512,1088]{1,2,0:T(8,128)(2,1)} %param.16, f32[512]{0:T(512)S(1)} %copy-done.68, ...), kind=kLoop, calls=%fused_computation.75 | loop fusion | flops 6684672 | bytes 8927488 | tf_op jit(solution)/shard_map/add | solution.py:702
  434.1 6.3 %collective-permute-done.74 = f32[13056]{0:T(1024)S(1)} collective-permute-done((f32[13056]{0:T(1024)S(1)}, f32[13056]{0:T(1024)S(1)}, u32[]{:S(2)}, u32[]{:S(2)}) %collective-permute-start.74) | collective-permute-done | bytes 52256 | tf_op jit(solution)/shard_map/ppermute | solution.py:381
  443.3 6.3 %collective-permute-done.86.refs_2_ = bf16[136,960]{1,0:T(8,128)(2,1)S(1)} collective-permute-done((bf16[136,960]{1,0:T(8,128)(2,1)S(1)}, bf16[136,960]{1,0:T(8,128)(2,1)S(1)}, u32[]{:S(2)}, u32[]{:S(2)}) %collective-permute-start.86) | collective-permute-done | bytes 261152 | tf_op jit(solution)/shard_map/ppermute | solution.py:243
  (489 shorter events, 225.6 us)
Async XLA Ops:
  3.7 16.5 %collective-permute-start.3 = (bf16[136,816]{1,0:T(8,128)(2,1)}, bf16[136,816]{1,0:T(8,128)(2,1)S(1)}, u32[]{:S(2)}, u32[]{:S(2)}) collective-permute-start(bf16[136,816]{1,0:T(8,128)(2,1)} %refs_0_.1), channel_id=1, source_target_pairs={{0,1},{1,0},{2,3},{3,2},{4,5},{5,4},{6,7},{7,6},{8,9},{9,8},{10,11... | collective-permute-start | bytes 665864 | tf_op jit(solution)/shard_map/ppermute | solution.py:243
  15.9 39.4 %collective-permute-start.14 = (bf16[512,1088]{0,1:T(8,128)(2,1)S(1)}, bf16[512,1088]{0,1:T(8,128)(2,1)S(1)}, u32[]{:S(2)}, u32[]{:S(2)}) collective-permute-start(bf16[512,1088]{0,1:T(8,128)(2,1)S(1)} %fusion.21), channel_id=1, source_target_pairs={{0,2},{1,3},{2,0},{3,1},{4,6},{5,7},{6,4},{7,5},{8,10},{9,11},{10,... | collective-permute-start | bytes 3342344 | tf_op jit(solution)/shard_map/ppermute | solution.py:243
  19.5 62.7 %collective-permute-start.13 = (bf16[512,1088]{0,1:T(8,128)(2,1)S(1)}, bf16[512,1088]{0,1:T(8,128)(2,1)S(1)}, u32[]{:S(2)}, u32[]{:S(2)}) collective-permute-start(bf16[512,1088]{0,1:T(8,128)(2,1)S(1)} %fusion.21), channel_id=1, source_target_pairs={{0,1},{1,0},{2,3},{3,2},{4,5},{5,4},{6,7},{7,6},{8,9},{9,8},{10,11... | collective-permute-start | bytes 3342344 | tf_op jit(solution)/shard_map/ppermute | solution.py:243
  28.2 26.9 %collective-permute-start.7 = (bf16[136,1344]{1,0:T(8,128)(2,1)S(1)}, bf16[136,1344]{1,0:T(8,128)(2,1)S(1)}, u32[]{:S(2)}, u32[]{:S(2)}) collective-permute-start(bf16[136,1344]{1,0:T(8,128)(2,1)S(1)} %move_columns.6), channel_id=1, source_target_pairs={{0,4},{8,0},{16,8},{24,16},{28,24},{20,28},{12,20},{4,12},{1,5},{9... | collective-permute-start | bytes 1096712 | tf_op jit(solution)/shard_map/ppermute | solution.py:249
  38.3 17.3 %collective-permute-start.8 = (bf16[136,1344]{1,0:T(8,128)(2,1)S(1)}, bf16[136,1344]{1,0:T(8,128)(2,1)S(1)}, u32[]{:S(2)}, u32[]{:S(2)}) collective-permute-start(bf16[136,1344]{1,0:T(8,128)(2,1)S(1)} %collective-permute-done.6), channel_id=1, source_target_pairs={{0,8},{8,16},{16,24},{24,28},{28,20},{20,12},{12,4},{4,0},{1,9},{9... | collective-permute-start | bytes 1096712 | tf_op jit(solution)/shard_map/ppermute | solution.py:246
  55.3 26.6 %collective-permute-start.22 = (bf16[512,1088]{0,1:T(8,128)(2,1)S(1)}, bf16[512,1088]{0,1:T(8,128)(2,1)S(1)}, u32[]{:S(2)}, u32[]{:S(2)}) collective-permute-start(bf16[512,1088]{0,1:T(8,128)(2,1)S(1)} %bitcast.150), channel_id=1, source_target_pairs={{0,2},{1,3},{2,0},{3,1},{4,6},{5,7},{6,4},{7,5},{8,10},{9,11},{10,... | collective-permute-start | bytes 3342344 | tf_op jit(solution)/shard_map/ppermute | solution.py:243
  55.4 26.9 %collective-permute-start.15 = (bf16[512,1088]{0,1:T(8,128)(2,1)S(1)}, bf16[512,1088]{0,1:T(8,128)(2,1)S(1)}, u32[]{:S(2)}, u32[]{:S(2)}) collective-permute-start(bf16[512,1088]{0,1:T(8,128)(2,1)S(1)} %collective-permute-done.14), channel_id=1, source_target_pairs={{0,1},{1,0},{2,3},{3,2},{4,5},{5,4},{6,7},{7,6},{8,9},{9,8},{10,11... | collective-permute-start | bytes 3342344 | tf_op jit(solution)/shard_map/ppermute | solution.py:243
  79.8 16.2 %collective-permute-start.21 = (bf16[272,1088]{1,0:T(8,128)(2,1)S(1)}, bf16[272,1088]{1,0:T(8,128)(2,1)S(1)}, u32[]{:S(2)}, u32[]{:S(2)}) collective-permute-start(bf16[272,1088]{1,0:T(8,128)(2,1)S(1)} %pad_maximum_fusion.7), channel_id=1, source_target_pairs={{0,4},{8,0},{16,8},{24,16},{28,24},{20,28},{12,20},{4,12},{1,5},{9... | collective-permute-start | bytes 1775624 | tf_op jit(solution)/shard_map/ppermute | solution.py:249
  81.9 31.3 %collective-permute-start.25 = (bf16[1088,384]{1,0:T(8,128)(2,1)S(1)}, bf16[1088,384]{1,0:T(8,128)(2,1)S(1)}, u32[]{:S(2)}, u32[]{:S(2)}) collective-permute-start(bf16[1088,384]{1,0:T(8,128)(2,1)S(1)} %slice.178.refs_0_), channel_id=1, source_target_pairs={{0,2},{1,3},{2,0},{3,1},{4,6},{5,7},{6,4},{7,5},{8,10},{9,11},{10,... | collective-permute-start | bytes 2506760 | tf_op jit(solution)/shard_map/ppermute | solution.py:243
  96.3 24.6 %collective-permute-start.38 = (bf16[512,1088]{0,1:T(8,128)(2,1)S(1)}, bf16[512,1088]{0,1:T(8,128)(2,1)S(1)}, u32[]{:S(2)}, u32[]{:S(2)}) collective-permute-start(bf16[512,1088]{0,1:T(8,128)(2,1)S(1)} %bitcast.152), channel_id=1, source_target_pairs={{0,1},{1,0},{2,3},{3,2},{4,5},{5,4},{6,7},{7,6},{8,9},{9,8},{10,11... | collective-permute-start | bytes 3342344 | tf_op jit(solution)/shard_map/ppermute | solution.py:243
  96.3 16.5 %collective-permute-start.23 = (bf16[272,1088]{1,0:T(8,128)(2,1)S(1)}, bf16[272,1088]{1,0:T(8,128)(2,1)S(1)}, u32[]{:S(2)}, u32[]{:S(2)}) collective-permute-start(bf16[272,1088]{1,0:T(8,128)(2,1)S(1)} %collective-permute-done.20), channel_id=1, source_target_pairs={{0,8},{8,16},{16,24},{24,28},{28,20},{20,12},{12,4},{4,0},{1,9},{9... | collective-permute-start | bytes 1775624 | tf_op jit(solution)/shard_map/ppermute | solution.py:246
  96.7 16.6 %collective-permute-start.24 = (bf16[272,1088]{1,0:T(8,128)(2,1)S(1)}, bf16[272,1088]{1,0:T(8,128)(2,1)S(1)}, u32[]{:S(2)}, u32[]{:S(2)}) collective-permute-start(bf16[272,1088]{1,0:T(8,128)(2,1)S(1)} %collective-permute-done.21), channel_id=1, source_target_pairs={{0,4},{8,0},{16,8},{24,16},{28,24},{20,28},{12,20},{4,12},{1,5},{9... | collective-permute-start | bytes 1775624 | tf_op jit(solution)/shard_map/ppermute | solution.py:249
  115.3 32.4 %collective-permute-start.28 = (bf16[1088,384]{1,0:T(8,128)(2,1)S(1)}, bf16[1088,384]{1,0:T(8,128)(2,1)S(1)}, u32[]{:S(2)}, u32[]{:S(2)}) collective-permute-start(bf16[1088,384]{1,0:T(8,128)(2,1)S(1)} %slice.178.refs_0_), channel_id=1, source_target_pairs={{0,1},{1,0},{2,3},{3,2},{4,5},{5,4},{6,7},{7,6},{8,9},{9,8},{10,11... | collective-permute-start | bytes 2506760 | tf_op jit(solution)/shard_map/ppermute | solution.py:243
  115.3 32.4 %collective-permute-start.29 = (bf16[1088,384]{1,0:T(8,128)(2,1)S(1)}, bf16[1088,384]{1,0:T(8,128)(2,1)S(1)}, u32[]{:S(2)}, u32[]{:S(2)}) collective-permute-start(bf16[1088,384]{1,0:T(8,128)(2,1)S(1)} %collective-permute-done.25.refs_2_), channel_id=1, source_target_pairs={{0,1},{1,0},{2,3},{3,2},{4,5},{5,4},{6,7},{7,6},{8,9},{9,8},{10,11... | collective-permute-start | bytes 2506760 | tf_op jit(solution)/shard_map/ppermute | solution.py:243
  145.1 34.7 %collective-permute-start.42 = (bf16[512,1088]{0,1:T(8,128)(2,1)S(1)}, bf16[512,1088]{0,1:T(8,128)(2,1)S(1)}, u32[]{:S(2)}, u32[]{:S(2)}) collective-permute-start(bf16[512,1088]{0,1:T(8,128)(2,1)S(1)} %collective-permute-done.22), channel_id=1, source_target_pairs={{0,1},{1,0},{2,3},{3,2},{4,5},{5,4},{6,7},{7,6},{8,9},{9,8},{10,11... | collective-permute-start | bytes 3342344 | tf_op jit(solution)/shard_map/ppermute | solution.py:243
  153.1 26.5 %collective-permute-start.39 = (bf16[512,1088]{0,1:T(8,128)(2,1)S(1)}, bf16[512,1088]{0,1:T(8,128)(2,1)S(1)}, u32[]{:S(2)}, u32[]{:S(2)}) collective-permute-start(bf16[512,1088]{0,1:T(8,128)(2,1)S(1)} %add_convert_fusion.2), channel_id=1, source_target_pairs={{0,2},{1,3},{2,0},{3,1},{4,6},{5,7},{6,4},{7,5},{8,10},{9,11},{10,... | collective-permute-start | bytes 3342344 | tf_op jit(solution)/shard_map/ppermute | solution.py:243
  198.7 32.4 %collective-permute-start.40 = (bf16[512,1088]{0,1:T(8,128)(2,1)S(1)}, bf16[512,1088]{0,1:T(8,128)(2,1)S(1)}, u32[]{:S(2)}, u32[]{:S(2)}) collective-permute-start(bf16[512,1088]{0,1:T(8,128)(2,1)S(1)} %split.99), channel_id=1, source_target_pairs={{0,1},{1,0},{2,3},{3,2},{4,5},{5,4},{6,7},{7,6},{8,9},{9,8},{10,11... | collective-permute-start | bytes 3342344 | tf_op jit(solution)/shard_map/ppermute | solution.py:243
  209.6 26.7 %collective-permute-start.44 = (bf16[512,1088]{0,1:T(8,128)(2,1)S(1)}, bf16[512,1088]{0,1:T(8,128)(2,1)S(1)}, u32[]{:S(2)}, u32[]{:S(2)}) collective-permute-start(bf16[512,1088]{0,1:T(8,128)(2,1)S(1)} %slice_add_fusion.1), channel_id=1, source_target_pairs={{0,2},{1,3},{2,0},{3,1},{4,6},{5,7},{6,4},{7,5},{8,10},{9,11},{10,... | collective-permute-start | bytes 3342344 | tf_op jit(solution)/shard_map/ppermute | solution.py:243
  227.9 16.3 %collective-permute-start.45 = (bf16[272,1088]{1,0:T(8,128)(2,1)S(1)}, bf16[272,1088]{1,0:T(8,128)(2,1)S(1)}, u32[]{:S(2)}, u32[]{:S(2)}) collective-permute-start(bf16[272,1088]{1,0:T(8,128)(2,1)S(1)} %pad_maximum_fusion.8), channel_id=1, source_target_pairs={{0,8},{8,16},{16,24},{24,28},{28,20},{20,12},{12,4},{4,0},{1,9},{9... | collective-permute-start | bytes 1775624 | tf_op jit(solution)/shard_map/ppermute | solution.py:246
  246.5 25.4 %collective-permute-start.49 = (bf16[256,512]{1,0:T(8,128)(2,1)S(1)}, bf16[256,512]{1,0:T(8,128)(2,1)S(1)}, u32[]{:S(2)}, u32[]{:S(2)}) collective-permute-start(bf16[256,512]{1,0:T(8,128)(2,1)S(1)} %slice.155), channel_id=1, source_target_pairs={{0,3},{1,2},{2,1},{3,0},{4,7},{5,6},{6,5},{7,4},{8,11},{9,10},{10,... | collective-permute-start | bytes 786440 | tf_op jit(solution)/shard_map/ppermute | solution.py:243
  246.6 25.4 %collective-permute-start.48 = (bf16[256,512]{1,0:T(8,128)(2,1)S(1)}, bf16[256,512]{1,0:T(8,128)(2,1)S(1)}, u32[]{:S(2)}, u32[]{:S(2)}) collective-permute-start(bf16[256,512]{1,0:T(8,128)(2,1)S(1)} %slice.154), channel_id=1, source_target_pairs={{0,2},{1,3},{2,0},{3,1},{4,6},{5,7},{6,4},{7,5},{8,10},{9,11},{10,... | collective-permute-start | bytes 786440 | tf_op jit(solution)/shard_map/ppermute | solution.py:243
  262.0 16.5 %collective-permute-start.50 = (bf16[272,1088]{1,0:T(8,128)(2,1)S(1)}, bf16[272,1088]{1,0:T(8,128)(2,1)S(1)}, u32[]{:S(2)}, u32[]{:S(2)}) collective-permute-start(bf16[272,1088]{1,0:T(8,128)(2,1)S(1)} %add_convert_fusion.9), channel_id=1, source_target_pairs={{0,8},{8,16},{16,24},{24,28},{28,20},{20,12},{12,4},{4,0},{1,9},{9... | collective-permute-start | bytes 1775624 | tf_op jit(solution)/shard_map/ppermute | solution.py:246
  280.1 24.7 %collective-permute-start.52 = (bf16[272,1088]{1,0:T(8,128)(2,1)S(1)}, bf16[272,1088]{1,0:T(8,128)(2,1)S(1)}, u32[]{:S(2)}, u32[]{:S(2)}) collective-permute-start(bf16[272,1088]{1,0:T(8,128)(2,1)S(1)} %add_convert_fusion.8), channel_id=1, source_target_pairs={{0,8},{8,16},{16,24},{24,28},{28,20},{20,12},{12,4},{4,0},{1,9},{9... | collective-permute-start | bytes 1775624 | tf_op jit(solution)/shard_map/ppermute | solution.py:246
  281.2 24.8 %collective-permute-start.53 = (bf16[272,1088]{1,0:T(8,128)(2,1)S(1)}, bf16[272,1088]{1,0:T(8,128)(2,1)S(1)}, u32[]{:S(2)}, u32[]{:S(2)}) collective-permute-start(bf16[272,1088]{1,0:T(8,128)(2,1)S(1)} %add_convert_fusion.6), channel_id=1, source_target_pairs={{0,4},{8,0},{16,8},{24,16},{28,24},{20,28},{12,20},{4,12},{1,5},{9... | collective-permute-start | bytes 1775624 | tf_op jit(solution)/shard_map/ppermute | solution.py:249
  302.3 25.5 %collective-permute-start.57 = (bf16[512,1088]{0,1:T(8,128)(2,1)}, bf16[512,1088]{0,1:T(8,128)(2,1)}, u32[]{:S(2)}, u32[]{:S(2)}) collective-permute-start(bf16[512,1088]{0,1:T(8,128)(2,1)} %convert_add_fusion.2), channel_id=1, source_target_pairs={{0,2},{1,3},{2,0},{3,1},{4,6},{5,7},{6,4},{7,5},{8,10},{9,11},{10,... | collective-permute-start | bytes 3342344 | tf_op jit(solution)/shard_map/ppermute | solution.py:243
  304.8 17.9 %collective-permute-start.61 = (bf16[1088,384]{1,0:T(8,128)(2,1)}, bf16[1088,384]{1,0:T(8,128)(2,1)}, u32[]{:S(2)}, u32[]{:S(2)}) collective-permute-start(bf16[1088,384]{1,0:T(8,128)(2,1)} %get-tuple-element.166), channel_id=1, source_target_pairs={{0,1},{1,0},{2,3},{3,2},{4,5},{5,4},{6,7},{7,6},{8,9},{9,8},{10,11... | collective-permute-start | bytes 2506760 | tf_op jit(solution)/shard_map/ppermute | solution.py:243
  305.9 16.8 %collective-permute-start.54 = (bf16[272,1088]{1,0:T(8,128)(2,1)}, bf16[272,1088]{1,0:T(8,128)(2,1)}, u32[]{:S(2)}, u32[]{:S(2)}) collective-permute-start(bf16[272,1088]{1,0:T(8,128)(2,1)} %add_convert_fusion.5), channel_id=1, source_target_pairs={{0,8},{8,16},{16,24},{24,28},{28,20},{20,12},{12,4},{4,0},{1,9},{9... | collective-permute-start | bytes 1775624 | tf_op jit(solution)/shard_map/ppermute | solution.py:246
  308.6 38.5 %collective-permute-start.63 = (bf16[1088,384]{1,0:T(8,128)(2,1)}, bf16[1088,384]{1,0:T(8,128)(2,1)S(1)}, u32[]{:S(2)}, u32[]{:S(2)}) collective-permute-start(bf16[1088,384]{1,0:T(8,128)(2,1)} %copy-done.11), channel_id=1, source_target_pairs={{0,1},{1,0},{2,3},{3,2},{4,5},{5,4},{6,7},{7,6},{8,9},{9,8},{10,11... | collective-permute-start | bytes 2506760 | tf_op jit(solution)/shard_map/ppermute | solution.py:243
  324.1 23.0 %collective-permute-start.62 = (bf16[1088,384]{1,0:T(8,128)(2,1)S(1)}, bf16[1088,384]{1,0:T(8,128)(2,1)S(1)}, u32[]{:S(2)}, u32[]{:S(2)}) collective-permute-start(bf16[1088,384]{1,0:T(8,128)(2,1)S(1)} %add_convert_fusion.4), channel_id=1, source_target_pairs={{0,2},{1,3},{2,0},{3,1},{4,6},{5,7},{6,4},{7,5},{8,10},{9,11},{10,... | collective-permute-start | bytes 2506760 | tf_op jit(solution)/shard_map/ppermute | solution.py:243
  374.8 31.5 %collective-permute-start.66 = (bf16[512,1088]{0,1:T(8,128)(2,1)}, bf16[512,1088]{0,1:T(8,128)(2,1)}, u32[]{:S(2)}, u32[]{:S(2)}) collective-permute-start(bf16[512,1088]{0,1:T(8,128)(2,1)} %slice_add_fusion), channel_id=1, source_target_pairs={{0,2},{1,3},{2,0},{3,1},{4,6},{5,7},{6,4},{7,5},{8,10},{9,11},{10,... | collective-permute-start | bytes 3342344 | tf_op jit(solution)/shard_map/ppermute | solution.py:243
  383.9 22.4 %collective-permute-start.65 = (bf16[512,1088]{0,1:T(8,128)(2,1)}, bf16[512,1088]{0,1:T(8,128)(2,1)}, u32[]{:S(2)}, u32[]{:S(2)}) collective-permute-start(bf16[512,1088]{0,1:T(8,128)(2,1)} %split.122), channel_id=1, source_target_pairs={{0,1},{1,0},{2,3},{3,2},{4,5},{5,4},{6,7},{7,6},{8,9},{9,8},{10,11... | collective-permute-start | bytes 3342344 | tf_op jit(solution)/shard_map/ppermute | solution.py:243
  392.5 25.8 %collective-permute-start.75 = (bf16[136,1088]{1,0:T(8,128)(2,1)}, bf16[136,1088]{1,0:T(8,128)(2,1)S(1)}, u32[]{:S(2)}, u32[]{:S(2)}) collective-permute-start(bf16[136,1088]{1,0:T(8,128)(2,1)} %split.118), channel_id=1, source_target_pairs={{0,0},{4,1},{8,2},{12,3},{16,4},{20,5},{24,6},{28,7},{1,8},{5,9},{... | collective-permute-start | bytes 887816 | tf_op jit(solution)/shard_map/ppermute | solution.py:691
  (144 other events, 1260.5 us)

commit v3 on v2

--- a/solution.py
+++ b/solution.py
@@ -582,9 +582,10 @@
         for first, last in ((0, groups[0][1]), (groups[0][1], per_device)):
             if last > first:
                 span = slice(first * HEAD_DIM, last * HEAD_DIM)
-                grad_owns.append(
-                    (first, jnp.stack(ctx_exchange([part[span] for part in grad_attended])))
-                )
+                sent = [part[span] for part in grad_attended]
+                if grad_owns:
+                    sent = after(sent, grad_owns[0][1])
+                grad_owns.append((first, jnp.stack(ctx_exchange(sent))))
         mlp_sums = [
             mlp_out_parts[r].astype(f32) + swap(mlp_out_parts[r + 1], 1).astype(f32)
             for r in range(0, n_ctx, 2)

time: 461 us -> 451 us (0.978)
  waiting for transfers between devices: 161 us -> 152 us
where the time goes in v3:
time: 451 us; the launch traced here: 445 us
  waiting for transfers between devices  152 us (34%)
  starting transfers between devices  79.8 us (18%)
  matrix products  70 us (16%)
  Pallas kernels  63.8 us (14%)
  local copies, waits for them, and re-layouts  39.5 us (9%)
  other arithmetic  37.4 us (8%)
    dot_general x19, matrix products, mm(): return lax.dot_general(left, right, dims, preferred_element_type=f32)  70 us
    ppermute x51, waiting for transfers between devices, swap(): return lax.ppermute(value, 'ctx', [(c, c ^ distance) for c in range(n_ctx)])  58.8 us
    ppermute x16, waiting for transfers between devices, go_right(): return lax.ppermute(value, 'seq', ring_right)  52.7 us
    pallas_call x4, Pallas kernels, attend_back(): pl.pallas_call(functools.partial(attend_back_kernel, block, blocks), grid...  37.3 us
    ppermute x12, waiting for transfers between devices, go_left(): return lax.ppermute(value, 'seq', ring_left)  34.5 us
    ppermute x16, starting transfers between devices, go_right(): return lax.ppermute(value, 'seq', ring_right)  28.3 us
    ppermute x51, starting transfers between devices, swap(): return lax.ppermute(value, 'ctx', [(c, c ^ distance) for c in range(n_ctx)])  27.8 us
    pallas_call x4, Pallas kernels, attend(): pl.pallas_call(functools.partial(attend_kernel, block, blocks), grid_spec...  21.8 us
  transfers between devices with their start and end apart: 88, of which 38 were waited for; matrix products, arithmetic and copies ran while one was open for 22% of the time, Pallas kernels for 14%

profile of v3, /device:TPU:0, one launch (start us, length us, event | category | flops | bytes accessed | tf_op | source)
XLA Modules:
  0.0 445.2 jit_solution(6225285376876301746)
XLA Ops:
  23.7 4.5 %collective-permute-start.6 = (bf16[136,1344]{1,0:T(8,128)(2,1)S(1)}, bf16[136,1344]{1,0:T(8,128)(2,1)S(1)}, u32[]{:S(2)}, u32[]{:S(2)}) collective-permute-start(bf16[136,1344]{1,0:T(8,128)(2,1)S(1)} %move_columns.6), channel_id=1, source_target_pairs={{0,8},{8,16},{16,24},{24,28},{28,20},{20,12},{12,4},{4,0},{1,9},{9... | collective-permute-start | bytes 1096712 | tf_op jit(solution)/shard_map/ppermute | solution.py:246
  29.7 8.5 %collective-permute-done.6 = bf16[136,1344]{1,0:T(8,128)(2,1)S(1)} collective-permute-done((bf16[136,1344]{1,0:T(8,128)(2,1)S(1)}, bf16[136,1344]{1,0:T(8,128)(2,1)S(1)}, u32[]{:S(2)}, u32[]{:S(2)}) %collective-permute-start.6) | collective-permute-done | bytes 365600 | tf_op jit(solution)/shard_map/ppermute | solution.py:246
  38.3 8.6 %collective-permute-start.8 = (bf16[136,1344]{1,0:T(8,128)(2,1)S(1)}, bf16[136,1344]{1,0:T(8,128)(2,1)S(1)}, u32[]{:S(2)}, u32[]{:S(2)}) collective-permute-start(bf16[136,1344]{1,0:T(8,128)(2,1)S(1)} %collective-permute-done.6), channel_id=1, source_target_pairs={{0,8},{8,16},{16,24},{24,28},{28,20},{20,12},{12,4},{4,0},{1,9},{9... | collective-permute-start | bytes 1096712 | tf_op jit(solution)/shard_map/ppermute | solution.py:246
  46.9 8.3 %collective-permute-done.7 = bf16[136,1344]{1,0:T(8,128)(2,1)S(1)} collective-permute-done((bf16[136,1344]{1,0:T(8,128)(2,1)S(1)}, bf16[136,1344]{1,0:T(8,128)(2,1)S(1)}, u32[]{:S(2)}, u32[]{:S(2)}) %collective-permute-start.7) | collective-permute-done | bytes 365600 | tf_op jit(solution)/shard_map/ppermute | solution.py:249
  57.5 8.6 %collective-permute-done.9 = bf16[136,1344]{1,0:T(8,128)(2,1)S(1)} collective-permute-done((bf16[136,1344]{1,0:T(8,128)(2,1)S(1)}, bf16[136,1344]{1,0:T(8,128)(2,1)S(1)}, u32[]{:S(2)}, u32[]{:S(2)}) %collective-permute-start.9) | collective-permute-done | bytes 365600 | tf_op jit(solution)/shard_map/ppermute | solution.py:249
  68.3 7.9 %collective-permute-done.11 = bf16[136,1344]{1,0:T(8,128)(2,1)S(1)} collective-permute-done((bf16[136,1344]{1,0:T(8,128)(2,1)S(1)}, bf16[136,1344]{1,0:T(8,128)(2,1)S(1)}, u32[]{:S(2)}, u32[]{:S(2)}) %collective-permute-start.11) | collective-permute-done | bytes 365600 | tf_op jit(solution)/shard_map/ppermute | solution.py:249
  82.3 5.4 %add_convert_fusion = bf16[960,2048]{1,0:T(8,128)(2,1)S(1)} fusion(f32[960]{0:T(1024)S(1)} %pad_maximum_fusion.14, bf16[1088,1344]{1,0:T(8,128)(2,1)S(1)} %constant_dynamic-update-slice_fusion.2, bf16[512,1088]{0,1:T(8,128)(2,1)S(1)} %collective-permute-done.15, bf16[512,1088]{0,1:T(8,128)(2,1)S(1)} %collective-permute-done.14, ...), kind=kOutput, calls=%fused_computation.11 | convolution fusion | flops 4299948032 | bytes 10620928 | tf_op jit(solution)/shard_map/dot_general | solution.py:24
  87.7 4.4 attend.5
  98.8 8.8 %attend.6 = (bf16[4,128,512]{2,1,0:T(8,128)(2,1)S(1)}, f32[2,1,2048]{2,1,0:T(1,128)S(1)}) custom-call(s32[1]{0:T(128)} %bitcast.own_ref, s32[1,2048]{1,0:T(1,128)S(1)} %compare_select_fusion.3.start_ref, bf16[3,320,2048]{2,1,0:T(8,128)(2,1)S(1)} %bitcast.142), custom_call_target="tpu_custom_call" | custom-call | flops 10737418240 | bytes 2097152 | tf_op jit(solution)/shard_map/attend/pallas_call | solution.py:111
  107.8 5.0 %collective-permute-done.23 = bf16[272,1088]{1,0:T(8,128)(2,1)S(1)} collective-permute-done((bf16[272,1088]{1,0:T(8,128)(2,1)S(1)}, bf16[272,1088]{1,0:T(8,128)(2,1)S(1)}, u32[]{:S(2)}, u32[]{:S(2)}) %collective-permute-start.23) | collective-permute-done | bytes 591904 | tf_op jit(solution)/shard_map/ppermute | solution.py:246
  121.0 7.6 %collective-permute-done.26 = bf16[272,1088]{1,0:T(8,128)(2,1)S(1)} collective-permute-done((bf16[272,1088]{1,0:T(8,128)(2,1)S(1)}, bf16[272,1088]{1,0:T(8,128)(2,1)S(1)}, u32[]{:S(2)}, u32[]{:S(2)}) %collective-permute-start.26) | collective-permute-done | bytes 591904 | tf_op jit(solution)/shard_map/ppermute | solution.py:246
  128.8 4.3 attend.4
  137.8 6.0 %collective-permute-done.33 = bf16[64,512]{1,0:T(8,128)(2,1)S(1)} collective-permute-done((bf16[64,512]{1,0:T(8,128)(2,1)S(1)}, bf16[64,512]{1,0:T(8,128)(2,1)S(1)}, u32[]{:S(2)}, u32[]{:S(2)}) %collective-permute-start.33) | collective-permute-done | bytes 65568 | tf_op jit(solution)/shard_map/ppermute | solution.py:243
  155.3 5.2 %multiply_convert_fusion.1 = (bf16[1024,1088]{0,1:T(8,128)(2,1)}, f32[1024,1088]{0,1:T(8,128)S(1)}) fusion(f32[1088]{0:T(1024)S(1)} %dynamic_slice.117, bf16[1088,1088]{1,0:T(8,128)(2,1)S(1)} %get-tuple-element.294, bf16[512,1088]{0,1:T(8,128)(2,1)S(1)} %collective-permute-done.37, bf16[512,1088]{0,1:T(8,128)(2,1)S(1)} %add_convert_fusion.2), kind=kOutput, calls=%fused_computation.34 | convolution fusion | flops 2435448832 | bytes 11284736 | tf_op jit(solution)/shard_map/dot_general | solution.py:24
  160.6 4.5 %fusion.10 = bf16[1024,1088]{0,1:T(8,128)(2,1)S(1)} fusion(f32[1024,1088]{0,1:T(8,128)S(1)} %get-tuple-element.340, bf16[1088,1088]{1,0:T(8,128)(2,1)S(1)} %get-tuple-element.293, bf16[1024,1088]{0,1:T(8,128)(2,1)S(1)} %constant_dynamic-update-slice_fusion.10), kind=kOutput, calls=%fused_computation.36 | convolution fusion | flops 2435448832 | bytes 11280384 | tf_op jit(solution)/shard_map/dot_general | solution.py:24
  169.4 10.3 %collective-permute-done.39 = bf16[512,1088]{0,1:T(8,128)(2,1)S(1)} collective-permute-done((bf16[512,1088]{0,1:T(8,128)(2,1)S(1)}, bf16[512,1088]{0,1:T(8,128)(2,1)S(1)}, u32[]{:S(2)}, u32[]{:S(2)}) %collective-permute-start.39) | collective-permute-done | bytes 1114144 | tf_op jit(solution)/shard_map/ppermute | solution.py:243
  182.6 5.2 %multiply_convert_fusion = (bf16[1024,1088]{0,1:T(8,128)(2,1)}, f32[1024,1088]{0,1:T(8,128)S(1)}) fusion(f32[1088]{0:T(1024)S(1)} %dynamic_slice.117, bf16[1024,1088]{0,1:T(8,128)(2,1)S(1)} %constant_dynamic-update-slice_fusion.12, bf16[1088,1088]{1,0:T(8,128)(2,1)S(1)} %get-tuple-element.294), kind=kOutput, calls=%fused_computation.32 | convolution fusion | flops 2430992384 | bytes 11284736 | tf_op jit(solution)/shard_map/dot_general | solution.py:24
  201.6 4.9 %convolution_convert_fusion.5 = bf16[1024,1088]{0,1:T(8,128)(2,1)S(1)} fusion(bf16[1024,1088]{0,1:T(8,128)(2,1)} %get-tuple-element.140, bf16[1088,1088]{1,0:T(8,128)(2,1)S(1)} %copy-done.34), kind=kOutput, calls=%fused_computation.42 | convolution fusion | flops 2425421824 | bytes 6823936 | tf_op jit(solution)/shard_map/dot_general | solution.py:24
  231.1 5.1 %collective-permute-done.44 = bf16[512,1088]{0,1:T(8,128)(2,1)S(1)} collective-permute-done((bf16[512,1088]{0,1:T(8,128)(2,1)S(1)}, bf16[512,1088]{0,1:T(8,128)(2,1)S(1)}, u32[]{:S(2)}, u32[]{:S(2)}) %collective-permute-start.44) | collective-permute-done | bytes 1114144 | tf_op jit(solution)/shard_map/ppermute | solution.py:243
  255.2 7.4 %attend_back.4.rest_0_ = bf16[3,320,2048]{2,1,0:T(8,128)(2,1)S(1)} custom-call(s32[1]{0:T(128)} %bitcast.own_ref, s32[1,2048]{1,0:T(1,128)S(1)} %compare_select_fusion.3.start_ref, bf16[3,320,2048]{2,1,0:T(8,128)(2,1)S(1)} %bitcast.145, bf16[4,64,512]{2,1,0:T(8,128)(2,1)S(1)} %get-tuple-element.125.out_ref, ...), custom_call_target="tpu_custom_call" | custom-call | flops 10737418240 | bytes 2359296 | tf_op jit(solution)/shard_map/attend_back/pallas_call | solution.py:158
  263.1 4.5 %collective-permute-done.51 = bf16[256,512]{1,0:T(8,128)(2,1)S(1)} collective-permute-done((bf16[256,512]{1,0:T(8,128)(2,1)S(1)}, bf16[256,512]{1,0:T(8,128)(2,1)S(1)}, u32[]{:S(2)}, u32[]{:S(2)}) %collective-permute-start.51) | collective-permute-done | bytes 262176 | tf_op jit(solution)/shard_map/ppermute | solution.py:243
  273.3 15.0 %attend_back.5.rest_0_ = bf16[3,320,2048]{2,1,0:T(8,128)(2,1)S(1)} custom-call(s32[1]{0:T(128)} %bitcast.own_ref, s32[1,2048]{1,0:T(1,128)S(1)} %compare_select_fusion.3.start_ref, bf16[3,320,2048]{2,1,0:T(8,128)(2,1)S(1)} %bitcast.146, bf16[4,128,512]{2,1,0:T(8,128)(2,1)S(1)} %get-tuple-element.126.out_ref, ...), custom_call_target="tpu_custom_call", output_to_operand_aliasing={{}: (6, {})} | custom-call | flops 21474836480 | bytes 4718592 | tf_op jit(solution)/shard_map/attend_back/pallas_call | solution.py:158
  297.3 14.2 %collective-permute-done.57 = bf16[272,1088]{1,0:T(8,128)(2,1)} collective-permute-done((bf16[272,1088]{1,0:T(8,128)(2,1)}, bf16[272,1088]{1,0:T(8,128)(2,1)}, u32[]{:S(2)}, u32[]{:S(2)}) %collective-permute-start.57) | collective-permute-done | bytes 591904 | tf_op jit(solution)/shard_map/ppermute | solution.py:246
  313.5 4.5 %collective-permute-done.60 = bf16[512,1088]{0,1:T(8,128)(2,1)} collective-permute-done((bf16[512,1088]{0,1:T(8,128)(2,1)}, bf16[512,1088]{0,1:T(8,128)(2,1)}, u32[]{:S(2)}, u32[]{:S(2)}) %collective-permute-start.60) | collective-permute-done | bytes 1114144 | tf_op jit(solution)/shard_map/ppermute | solution.py:243
  322.2 7.4 %attend_back.6.rest_0_ = bf16[3,320,2048]{2,1,0:T(8,128)(2,1)S(1)} custom-call(s32[1]{0:T(128)} %bitcast.own_ref, s32[1,2048]{1,0:T(1,128)S(1)} %compare_select_fusion.3.start_ref, bf16[3,320,2048]{2,1,0:T(8,128)(2,1)S(1)} %bitcast.147, bf16[4,64,512]{2,1,0:T(8,128)(2,1)S(1)} %copy-done.6, ...), custom_call_target="tpu_custom_call", output_to_operand_aliasing={{}: (6, {})} | custom-call | flops 10737418240 | bytes 2359296 | tf_op jit(solution)/shard_map/attend_back/pallas_call | solution.py:158
  329.7 7.6 %attend_back.7 = bf16[3,320,2048]{2,1,0:T(8,128)(2,1)S(1)} custom-call(s32[1]{0:T(128)} %bitcast.own_ref, s32[1,2048]{1,0:T(1,128)S(1)} %compare_select_fusion.3.start_ref, bf16[3,320,2048]{2,1,0:T(8,128)(2,1)S(1)} %bitcast.148, bf16[4,64,512]{2,1,0:T(8,128)(2,1)S(1)} %copy-done.8, ...), custom_call_target="tpu_custom_call", output_to_operand_aliasing={{}: (6, {})} | custom-call | flops 10737418240 | bytes 2359296 | tf_op jit(solution)/shard_map/attend_back/pallas_call | solution.py:158
  349.5 6.6 %convolution_convert_fusion.7 = bf16[1088,960]{0,1:T(8,128)(2,1)} fusion(bf16[960,2048]{1,0:T(8,128)(2,1)S(1)} %bitcast.139, bf16[512,1088]{0,1:T(8,128)(2,1)S(1)} %copy-done.82, bf16[512,1088]{0,1:T(8,128)(2,1)S(1)} %copy-done.78, bf16[512,1088]{0,1:T(8,128)(2,1)S(1)} %copy-done.80, bf16[512,1088]{0,1:T(8,128)(2,1)S(1)} %copy-done.50), kind=kOutput, calls=%fused_computation.44 | convolution fusion | flops 4297060352 | bytes 10477568 | tf_op jit(solution)/shard_map/dot_general | solution.py:24
  384.6 4.8 %collective-permute-done.68 = bf16[136,1344]{1,0:T(8,128)(2,1)} collective-permute-done((bf16[136,1344]{1,0:T(8,128)(2,1)}, bf16[136,1344]{1,0:T(8,128)(2,1)}, u32[]{:S(2)}, u32[]{:S(2)}) %collective-permute-start.68) | collective-permute-done | bytes 365600 | tf_op jit(solution)/shard_map/ppermute | solution.py:246
  391.3 5.5 %collective-permute-done.66 = bf16[512,1088]{0,1:T(8,128)(2,1)} collective-permute-done((bf16[512,1088]{0,1:T(8,128)(2,1)}, bf16[512,1088]{0,1:T(8,128)(2,1)}, u32[]{:S(2)}, u32[]{:S(2)}) %collective-permute-start.66) | collective-permute-done | bytes 1114144 | tf_op jit(solution)/shard_map/ppermute | solution.py:243
  403.6 5.2 %add_add_fusion.2 = f32[512,1088]{0,1:T(8,128)} fusion(f32[512,1088]{0,1:T(8,128)} %copy-done.23, f32[512]{0:T(512)S(1)} %negate_multiply_fusion, f32[512]{0:T(512)S(1)} %negate_multiply_fusion.1, f32[512]{0:T(512)S(1)} %multiply_multiply_fusion.2, f32[512]{0:T(512)S(1)} %copy-done.66, bf16[1,512,1088]{1,2,0:T(8,128)(2,1)} %param.16, f32[512]{0:T(512)S(1)} %copy-done.68, ...), kind=kLoop, calls=%fused_computation.75 | loop fusion | flops 6684672 | bytes 8927488 | tf_op jit(solution)/shard_map/add | solution.py:703
  424.5 5.8 %collective-permute-done.74 = f32[13056]{0:T(1024)S(1)} collective-permute-done((f32[13056]{0:T(1024)S(1)}, f32[13056]{0:T(1024)S(1)}, u32[]{:S(2)}, u32[]{:S(2)}) %collective-permute-start.74) | collective-permute-done | bytes 52256 | tf_op jit(solution)/shard_map/ppermute | solution.py:381
  433.7 6.3 %collective-permute-done.86.refs_2_ = bf16[136,960]{1,0:T(8,128)(2,1)S(1)} collective-permute-done((bf16[136,960]{1,0:T(8,128)(2,1)S(1)}, bf16[136,960]{1,0:T(8,128)(2,1)S(1)}, u32[]{:S(2)}, u32[]{:S(2)}) %collective-permute-start.86) | collective-permute-done | bytes 261152 | tf_op jit(solution)/shard_map/ppermute | solution.py:243
  (489 shorter events, 224.6 us)
Async XLA Ops:
  3.7 16.5 %collective-permute-start.3 = (bf16[136,816]{1,0:T(8,128)(2,1)}, bf16[136,816]{1,0:T(8,128)(2,1)S(1)}, u32[]{:S(2)}, u32[]{:S(2)}) collective-permute-start(bf16[136,816]{1,0:T(8,128)(2,1)} %refs_0_.1), channel_id=1, source_target_pairs={{0,1},{1,0},{2,3},{3,2},{4,5},{5,4},{6,7},{7,6},{8,9},{9,8},{10,11... | collective-permute-start | bytes 665864 | tf_op jit(solution)/shard_map/ppermute | solution.py:243
  15.9 39.4 %collective-permute-start.14 = (bf16[512,1088]{0,1:T(8,128)(2,1)S(1)}, bf16[512,1088]{0,1:T(8,128)(2,1)S(1)}, u32[]{:S(2)}, u32[]{:S(2)}) collective-permute-start(bf16[512,1088]{0,1:T(8,128)(2,1)S(1)} %fusion.21), channel_id=1, source_target_pairs={{0,2},{1,3},{2,0},{3,1},{4,6},{5,7},{6,4},{7,5},{8,10},{9,11},{10,... | collective-permute-start | bytes 3342344 | tf_op jit(solution)/shard_map/ppermute | solution.py:243
  19.5 62.7 %collective-permute-start.13 = (bf16[512,1088]{0,1:T(8,128)(2,1)S(1)}, bf16[512,1088]{0,1:T(8,128)(2,1)S(1)}, u32[]{:S(2)}, u32[]{:S(2)}) collective-permute-start(bf16[512,1088]{0,1:T(8,128)(2,1)S(1)} %fusion.21), channel_id=1, source_target_pairs={{0,1},{1,0},{2,3},{3,2},{4,5},{5,4},{6,7},{7,6},{8,9},{9,8},{10,11... | collective-permute-start | bytes 3342344 | tf_op jit(solution)/shard_map/ppermute | solution.py:243
  28.2 26.9 %collective-permute-start.7 = (bf16[136,1344]{1,0:T(8,128)(2,1)S(1)}, bf16[136,1344]{1,0:T(8,128)(2,1)S(1)}, u32[]{:S(2)}, u32[]{:S(2)}) collective-permute-start(bf16[136,1344]{1,0:T(8,128)(2,1)S(1)} %move_columns.6), channel_id=1, source_target_pairs={{0,4},{8,0},{16,8},{24,16},{28,24},{20,28},{12,20},{4,12},{1,5},{9... | collective-permute-start | bytes 1096712 | tf_op jit(solution)/shard_map/ppermute | solution.py:249
  38.3 17.3 %collective-permute-start.8 = (bf16[136,1344]{1,0:T(8,128)(2,1)S(1)}, bf16[136,1344]{1,0:T(8,128)(2,1)S(1)}, u32[]{:S(2)}, u32[]{:S(2)}) collective-permute-start(bf16[136,1344]{1,0:T(8,128)(2,1)S(1)} %collective-permute-done.6), channel_id=1, source_target_pairs={{0,8},{8,16},{16,24},{24,28},{28,20},{20,12},{12,4},{4,0},{1,9},{9... | collective-permute-start | bytes 1096712 | tf_op jit(solution)/shard_map/ppermute | solution.py:246
  55.3 26.6 %collective-permute-start.22 = (bf16[512,1088]{0,1:T(8,128)(2,1)S(1)}, bf16[512,1088]{0,1:T(8,128)(2,1)S(1)}, u32[]{:S(2)}, u32[]{:S(2)}) collective-permute-start(bf16[512,1088]{0,1:T(8,128)(2,1)S(1)} %bitcast.149), channel_id=1, source_target_pairs={{0,2},{1,3},{2,0},{3,1},{4,6},{5,7},{6,4},{7,5},{8,10},{9,11},{10,... | collective-permute-start | bytes 3342344 | tf_op jit(solution)/shard_map/ppermute | solution.py:243
  55.4 26.9 %collective-permute-start.15 = (bf16[512,1088]{0,1:T(8,128)(2,1)S(1)}, bf16[512,1088]{0,1:T(8,128)(2,1)S(1)}, u32[]{:S(2)}, u32[]{:S(2)}) collective-permute-start(bf16[512,1088]{0,1:T(8,128)(2,1)S(1)} %collective-permute-done.14), channel_id=1, source_target_pairs={{0,1},{1,0},{2,3},{3,2},{4,5},{5,4},{6,7},{7,6},{8,9},{9,8},{10,11... | collective-permute-start | bytes 3342344 | tf_op jit(solution)/shard_map/ppermute | solution.py:243
  78.2 16.1 %collective-permute-start.20 = (bf16[272,1088]{1,0:T(8,128)(2,1)S(1)}, bf16[272,1088]{1,0:T(8,128)(2,1)S(1)}, u32[]{:S(2)}, u32[]{:S(2)}) collective-permute-start(bf16[272,1088]{1,0:T(8,128)(2,1)S(1)} %pad_maximum_fusion.7), channel_id=1, source_target_pairs={{0,8},{8,16},{16,24},{24,28},{28,20},{20,12},{12,4},{4,0},{1,9},{9... | collective-permute-start | bytes 1775624 | tf_op jit(solution)/shard_map/ppermute | solution.py:246
  79.8 16.2 %collective-permute-start.21 = (bf16[272,1088]{1,0:T(8,128)(2,1)S(1)}, bf16[272,1088]{1,0:T(8,128)(2,1)S(1)}, u32[]{:S(2)}, u32[]{:S(2)}) collective-permute-start(bf16[272,1088]{1,0:T(8,128)(2,1)S(1)} %pad_maximum_fusion.7), channel_id=1, source_target_pairs={{0,4},{8,0},{16,8},{24,16},{28,24},{20,28},{12,20},{4,12},{1,5},{9... | collective-permute-start | bytes 1775624 | tf_op jit(solution)/shard_map/ppermute | solution.py:249
  81.9 31.3 %collective-permute-start.25 = (bf16[1088,384]{1,0:T(8,128)(2,1)S(1)}, bf16[1088,384]{1,0:T(8,128)(2,1)S(1)}, u32[]{:S(2)}, u32[]{:S(2)}) collective-permute-start(bf16[1088,384]{1,0:T(8,128)(2,1)S(1)} %slice.178.refs_0_), channel_id=1, source_target_pairs={{0,2},{1,3},{2,0},{3,1},{4,6},{5,7},{6,4},{7,5},{8,10},{9,11},{10,... | collective-permute-start | bytes 2506760 | tf_op jit(solution)/shard_map/ppermute | solution.py:243
  96.3 24.6 %collective-permute-start.38 = (bf16[512,1088]{0,1:T(8,128)(2,1)S(1)}, bf16[512,1088]{0,1:T(8,128)(2,1)S(1)}, u32[]{:S(2)}, u32[]{:S(2)}) collective-permute-start(bf16[512,1088]{0,1:T(8,128)(2,1)S(1)} %bitcast.151), channel_id=1, source_target_pairs={{0,1},{1,0},{2,3},{3,2},{4,5},{5,4},{6,7},{7,6},{8,9},{9,8},{10,11... | collective-permute-start | bytes 3342344 | tf_op jit(solution)/shard_map/ppermute | solution.py:243
  96.3 16.5 %collective-permute-start.23 = (bf16[272,1088]{1,0:T(8,128)(2,1)S(1)}, bf16[272,1088]{1,0:T(8,128)(2,1)S(1)}, u32[]{:S(2)}, u32[]{:S(2)}) collective-permute-start(bf16[272,1088]{1,0:T(8,128)(2,1)S(1)} %collective-permute-done.20), channel_id=1, source_target_pairs={{0,8},{8,16},{16,24},{24,28},{28,20},{20,12},{12,4},{4,0},{1,9},{9... | collective-permute-start | bytes 1775624 | tf_op jit(solution)/shard_map/ppermute | solution.py:246
  96.7 16.6 %collective-permute-start.24 = (bf16[272,1088]{1,0:T(8,128)(2,1)S(1)}, bf16[272,1088]{1,0:T(8,128)(2,1)S(1)}, u32[]{:S(2)}, u32[]{:S(2)}) collective-permute-start(bf16[272,1088]{1,0:T(8,128)(2,1)S(1)} %collective-permute-done.21), channel_id=1, source_target_pairs={{0,4},{8,0},{16,8},{24,16},{28,24},{20,28},{12,20},{4,12},{1,5},{9... | collective-permute-start | bytes 1775624 | tf_op jit(solution)/shard_map/ppermute | solution.py:249
  115.3 32.4 %collective-permute-start.28 = (bf16[1088,384]{1,0:T(8,128)(2,1)S(1)}, bf16[1088,384]{1,0:T(8,128)(2,1)S(1)}, u32[]{:S(2)}, u32[]{:S(2)}) collective-permute-start(bf16[1088,384]{1,0:T(8,128)(2,1)S(1)} %slice.178.refs_0_), channel_id=1, source_target_pairs={{0,1},{1,0},{2,3},{3,2},{4,5},{5,4},{6,7},{7,6},{8,9},{9,8},{10,11... | collective-permute-start | bytes 2506760 | tf_op jit(solution)/shard_map/ppermute | solution.py:243
  115.3 32.4 %collective-permute-start.29 = (bf16[1088,384]{1,0:T(8,128)(2,1)S(1)}, bf16[1088,384]{1,0:T(8,128)(2,1)S(1)}, u32[]{:S(2)}, u32[]{:S(2)}) collective-permute-start(bf16[1088,384]{1,0:T(8,128)(2,1)S(1)} %collective-permute-done.25.refs_2_), channel_id=1, source_target_pairs={{0,1},{1,0},{2,3},{3,2},{4,5},{5,4},{6,7},{7,6},{8,9},{9,8},{10,11... | collective-permute-start | bytes 2506760 | tf_op jit(solution)/shard_map/ppermute | solution.py:243
  145.1 34.7 %collective-permute-start.42 = (bf16[512,1088]{0,1:T(8,128)(2,1)S(1)}, bf16[512,1088]{0,1:T(8,128)(2,1)S(1)}, u32[]{:S(2)}, u32[]{:S(2)}) collective-permute-start(bf16[512,1088]{0,1:T(8,128)(2,1)S(1)} %collective-permute-done.22), channel_id=1, source_target_pairs={{0,1},{1,0},{2,3},{3,2},{4,5},{5,4},{6,7},{7,6},{8,9},{9,8},{10,11... | collective-permute-start | bytes 3342344 | tf_op jit(solution)/shard_map/ppermute | solution.py:243
  153.1 26.5 %collective-permute-start.39 = (bf16[512,1088]{0,1:T(8,128)(2,1)S(1)}, bf16[512,1088]{0,1:T(8,128)(2,1)S(1)}, u32[]{:S(2)}, u32[]{:S(2)}) collective-permute-start(bf16[512,1088]{0,1:T(8,128)(2,1)S(1)} %add_convert_fusion.2), channel_id=1, source_target_pairs={{0,2},{1,3},{2,0},{3,1},{4,6},{5,7},{6,4},{7,5},{8,10},{9,11},{10,... | collective-permute-start | bytes 3342344 | tf_op jit(solution)/shard_map/ppermute | solution.py:243
  198.7 32.4 %collective-permute-start.40 = (bf16[512,1088]{0,1:T(8,128)(2,1)S(1)}, bf16[512,1088]{0,1:T(8,128)(2,1)S(1)}, u32[]{:S(2)}, u32[]{:S(2)}) collective-permute-start(bf16[512,1088]{0,1:T(8,128)(2,1)S(1)} %split.99), channel_id=1, source_target_pairs={{0,1},{1,0},{2,3},{3,2},{4,5},{5,4},{6,7},{7,6},{8,9},{9,8},{10,11... | collective-permute-start | bytes 3342344 | tf_op jit(solution)/shard_map/ppermute | solution.py:243
  209.6 26.7 %collective-permute-start.44 = (bf16[512,1088]{0,1:T(8,128)(2,1)S(1)}, bf16[512,1088]{0,1:T(8,128)(2,1)S(1)}, u32[]{:S(2)}, u32[]{:S(2)}) collective-permute-start(bf16[512,1088]{0,1:T(8,128)(2,1)S(1)} %slice_add_fusion.1), channel_id=1, source_target_pairs={{0,2},{1,3},{2,0},{3,1},{4,6},{5,7},{6,4},{7,5},{8,10},{9,11},{10,... | collective-permute-start | bytes 3342344 | tf_op jit(solution)/shard_map/ppermute | solution.py:243
  230.2 16.1 %collective-permute-start.46 = (bf16[272,1088]{1,0:T(8,128)(2,1)S(1)}, bf16[272,1088]{1,0:T(8,128)(2,1)S(1)}, u32[]{:S(2)}, u32[]{:S(2)}) collective-permute-start(bf16[272,1088]{1,0:T(8,128)(2,1)S(1)} %pad_maximum_fusion.9), channel_id=1, source_target_pairs={{0,4},{8,0},{16,8},{24,16},{28,24},{20,28},{12,20},{4,12},{1,5},{9... | collective-permute-start | bytes 1775624 | tf_op jit(solution)/shard_map/ppermute | solution.py:249
  250.3 17.4 %collective-permute-start.53 = (bf16[272,1088]{1,0:T(8,128)(2,1)S(1)}, bf16[272,1088]{1,0:T(8,128)(2,1)S(1)}, u32[]{:S(2)}, u32[]{:S(2)}) collective-permute-start(bf16[272,1088]{1,0:T(8,128)(2,1)S(1)} %add_convert_fusion.9), channel_id=1, source_target_pairs={{0,8},{8,16},{16,24},{24,28},{28,20},{20,12},{12,4},{4,0},{1,9},{9... | collective-permute-start | bytes 1775624 | tf_op jit(solution)/shard_map/ppermute | solution.py:246
  251.1 16.8 %collective-permute-start.54 = (bf16[272,1088]{1,0:T(8,128)(2,1)S(1)}, bf16[272,1088]{1,0:T(8,128)(2,1)S(1)}, u32[]{:S(2)}, u32[]{:S(2)}) collective-permute-start(bf16[272,1088]{1,0:T(8,128)(2,1)S(1)} %add_convert_fusion.7), channel_id=1, source_target_pairs={{0,4},{8,0},{16,8},{24,16},{28,24},{20,28},{12,20},{4,12},{1,5},{9... | collective-permute-start | bytes 1775624 | tf_op jit(solution)/shard_map/ppermute | solution.py:249
  268.1 25.5 %collective-permute-start.55 = (bf16[272,1088]{1,0:T(8,128)(2,1)S(1)}, bf16[272,1088]{1,0:T(8,128)(2,1)S(1)}, u32[]{:S(2)}, u32[]{:S(2)}) collective-permute-start(bf16[272,1088]{1,0:T(8,128)(2,1)S(1)} %add_convert_fusion.8), channel_id=1, source_target_pairs={{0,8},{8,16},{16,24},{24,28},{28,20},{20,12},{12,4},{4,0},{1,9},{9... | collective-permute-start | bytes 1775624 | tf_op jit(solution)/shard_map/ppermute | solution.py:246
  269.5 25.2 %collective-permute-start.56 = (bf16[272,1088]{1,0:T(8,128)(2,1)S(1)}, bf16[272,1088]{1,0:T(8,128)(2,1)S(1)}, u32[]{:S(2)}, u32[]{:S(2)}) collective-permute-start(bf16[272,1088]{1,0:T(8,128)(2,1)S(1)} %add_convert_fusion.6), channel_id=1, source_target_pairs={{0,4},{8,0},{16,8},{24,16},{28,24},{20,28},{12,20},{4,12},{1,5},{9... | collective-permute-start | bytes 1775624 | tf_op jit(solution)/shard_map/ppermute | solution.py:249
  290.2 27.8 %collective-permute-start.60 = (bf16[512,1088]{0,1:T(8,128)(2,1)}, bf16[512,1088]{0,1:T(8,128)(2,1)}, u32[]{:S(2)}, u32[]{:S(2)}) collective-permute-start(bf16[512,1088]{0,1:T(8,128)(2,1)} %convert_add_fusion.2), channel_id=1, source_target_pairs={{0,2},{1,3},{2,0},{3,1},{4,6},{5,7},{6,4},{7,5},{8,10},{9,11},{10,... | collective-permute-start | bytes 3342344 | tf_op jit(solution)/shard_map/ppermute | solution.py:243
  293.6 17.9 %collective-permute-start.61 = (bf16[1088,384]{1,0:T(8,128)(2,1)}, bf16[1088,384]{1,0:T(8,128)(2,1)}, u32[]{:S(2)}, u32[]{:S(2)}) collective-permute-start(bf16[1088,384]{1,0:T(8,128)(2,1)} %get-tuple-element.174), channel_id=1, source_target_pairs={{0,1},{1,0},{2,3},{3,2},{4,5},{5,4},{6,7},{7,6},{8,9},{9,8},{10,11... | collective-permute-start | bytes 2506760 | tf_op jit(solution)/shard_map/ppermute | solution.py:243
  294.7 16.8 %collective-permute-start.57 = (bf16[272,1088]{1,0:T(8,128)(2,1)}, bf16[272,1088]{1,0:T(8,128)(2,1)}, u32[]{:S(2)}, u32[]{:S(2)}) collective-permute-start(bf16[272,1088]{1,0:T(8,128)(2,1)} %add_convert_fusion.5), channel_id=1, source_target_pairs={{0,8},{8,16},{16,24},{24,28},{28,20},{20,12},{12,4},{4,0},{1,9},{9... | collective-permute-start | bytes 1775624 | tf_op jit(solution)/shard_map/ppermute | solution.py:246
  297.1 40.2 %collective-permute-start.63 = (bf16[1088,384]{1,0:T(8,128)(2,1)}, bf16[1088,384]{1,0:T(8,128)(2,1)S(1)}, u32[]{:S(2)}, u32[]{:S(2)}) collective-permute-start(bf16[1088,384]{1,0:T(8,128)(2,1)} %copy-done.11), channel_id=1, source_target_pairs={{0,1},{1,0},{2,3},{3,2},{4,5},{5,4},{6,7},{7,6},{8,9},{9,8},{10,11... | collective-permute-start | bytes 2506760 | tf_op jit(solution)/shard_map/ppermute | solution.py:243
  312.8 24.5 %collective-permute-start.62 = (bf16[1088,384]{1,0:T(8,128)(2,1)S(1)}, bf16[1088,384]{1,0:T(8,128)(2,1)S(1)}, u32[]{:S(2)}, u32[]{:S(2)}) collective-permute-start(bf16[1088,384]{1,0:T(8,128)(2,1)S(1)} %add_convert_fusion.4), channel_id=1, source_target_pairs={{0,2},{1,3},{2,0},{3,1},{4,6},{5,7},{6,4},{7,5},{8,10},{9,11},{10,... | collective-permute-start | bytes 2506760 | tf_op jit(solution)/shard_map/ppermute | solution.py:243
  364.9 31.9 %collective-permute-start.66 = (bf16[512,1088]{0,1:T(8,128)(2,1)}, bf16[512,1088]{0,1:T(8,128)(2,1)}, u32[]{:S(2)}, u32[]{:S(2)}) collective-permute-start(bf16[512,1088]{0,1:T(8,128)(2,1)} %slice_add_fusion), channel_id=1, source_target_pairs={{0,2},{1,3},{2,0},{3,1},{4,6},{5,7},{6,4},{7,5},{8,10},{9,11},{10,... | collective-permute-start | bytes 3342344 | tf_op jit(solution)/shard_map/ppermute | solution.py:243
  374.0 22.8 %collective-permute-start.65 = (bf16[512,1088]{0,1:T(8,128)(2,1)}, bf16[512,1088]{0,1:T(8,128)(2,1)}, u32[]{:S(2)}, u32[]{:S(2)}) collective-permute-start(bf16[512,1088]{0,1:T(8,128)(2,1)} %split.122), channel_id=1, source_target_pairs={{0,1},{1,0},{2,3},{3,2},{4,5},{5,4},{6,7},{7,6},{8,9},{9,8},{10,11... | collective-permute-start | bytes 3342344 | tf_op jit(solution)/shard_map/ppermute | solution.py:243
  382.7 26.1 %collective-permute-start.75 = (bf16[136,1088]{1,0:T(8,128)(2,1)}, bf16[136,1088]{1,0:T(8,128)(2,1)S(1)}, u32[]{:S(2)}, u32[]{:S(2)}) collective-permute-start(bf16[136,1088]{1,0:T(8,128)(2,1)} %split.118), channel_id=1, source_target_pairs={{0,0},{4,1},{8,2},{12,3},{16,4},{20,5},{24,6},{28,7},{1,8},{5,9},{... | collective-permute-start | bytes 887816 | tf_op jit(solution)/shard_map/ppermute | solution.py:692
  (144 other events, 1207.3 us)
